TPU v7x, 32 devices: a whole 2x2x4 slice. The times are simulated.
32 devices in a mesh: dp: 2 (over core), blk: 16 (over z, y, x).
Axes of the slice: x: 2, y: 2, z: 4, core: 2. Of those that a mesh axis runs over, the one named last changes fastest.
Arguments:
- tokens: float32 [2, 2048, 768], P('dp', 'blk'), may hold values from -6 to 6
- cotangent: float32 [2, 2048, 768], P('dp', 'blk'), may hold values from -6 to 6
- mixer_weight: float32 [768, 3200], P(None, 'blk'), may hold values from -0.21875 to 0.21875
- widen_weight: float32 [2, 768, 1536], P(None, None, 'blk'), may hold values from -0.21875 to 0.21875
- narrow_weight: float32 [2, 1536, 768], P(None, None, 'blk'), may hold values from -0.15625 to 0.15625
- vectors: float32 [12288], replicated, may hold values from -8 to 8
- averager: float32 [4, 768, 16], replicated, may hold values from -181.01934 to 181.01934
- bias_index: int32 [4095], replicated, may hold values from 0 to 127, as said below
- mixer_rows: float32 [768], replicated, may hold values from 2.625168e-08 to 1.0500672e-07
- mixer_cols: float32 [3200], P('blk'), may hold values from 2.625168e-08 to 1.0500672e-07
- widen_rows: float32 [2, 768], replicated, may hold values from 2.625168e-08 to 1.0500672e-07
- widen_cols: float32 [2, 1536], P(None, 'blk'), may hold values from 2.625168e-08 to 1.0500672e-07
- narrow_rows: float32 [2, 1536], replicated, may hold values from 2.625168e-08 to 1.0500672e-07
- narrow_cols: float32 [2, 768], P(None, 'blk'), may hold values from 2.625168e-08 to 1.0500672e-07
- vector_moment: float32 [12288], replicated, may hold values from 1.0500672e-07 to 4.1450022e-07
- averager_moment: float32 [4, 768, 16], replicated, may hold values from 2.625168e-08 to 1.0500672e-07
Outputs:
- block_out: float32 [2, 2048, 768], P('dp', 'blk')
- tokens_grad: float32 [2, 2048, 768], P('dp', 'blk')
- mixer_grad: float32 [768, 3200], P(None, 'blk')
- widen_grad: float32 [2, 768, 1536], P(None, None, 'blk')
- narrow_grad: float32 [2, 1536, 768], P(None, None, 'blk')
- vector_grad: float32 [12288], replicated
- averager_grad: float32 [4, 768, 16], replicated
- mixer_new: float32 [768, 3200], P(None, 'blk')
- widen_new: float32 [2, 768, 1536], P(None, None, 'blk')
- narrow_new: float32 [2, 1536, 768], P(None, None, 'blk')
- vector_new: float32 [12288], replicated
- averager_new: float32 [4, 768, 16], replicated
- rows_mixer: float32 [768], replicated
- cols_mixer: float32 [3200], P('blk')
- rows_widen: float32 [2, 768], replicated
- cols_widen: float32 [2, 1536], P(None, 'blk')
- rows_narrow: float32 [2, 1536], replicated
- cols_narrow: float32 [2, 768], P(None, 'blk')
- moment_vector: float32 [12288], replicated
- moment_averager: float32 [4, 768, 16], replicated
- clip_norm: float32 [], replicated
Inputs may be any that keep to these rules, and one draw needn't show every extreme that they name: `bias_index`: entry 2047 + k is the table row for a key k positions after its query; k = 0 takes row 0.
All inputs are finite; a program needn't handle non-finite values.
Results may differ from a plain program's by a relative error of at most 0.015.
Values may be sent and summed in bfloat16 or wider, within the bound.
A program may use at most 192 MiB of HBM per device.

v0:
```python
import jax
import jax.numpy as jnp
from jax import lax
from jax.sharding import PartitionSpec as P

D = 768
ZD = 128
VD = 1536
FF = 1536
NH = 16
NB = 128
STEP = 10
MX = 3200


EPS_NORM = 1e-05
EPS_ONE = 1e-30
EPS_TWO = 0.001
CLIP_NORM = 1.0
CLIP_UPDATE = 1.0
RATE = 0.5


def carried_in(part, axis, combine, identity, reverse):
    count = lax.axis_size(axis)
    place = lax.axis_index(axis)
    ahead = count - 1 - place if reverse else place
    gathered = jax.tree.map(lambda a: lax.all_gather(a, axis), part)
    state = jax.tree.map(lambda a, e: jnp.zeros_like(a) + jnp.asarray(e, a.dtype), part, identity)

    def one(turn, state):
        source = count - 1 - turn if reverse else turn
        return combine(
            state, jax.tree.map(lambda a: lax.dynamic_index_in_dim(a, source, 0, False), gathered)
        )

    return lax.fori_loop(0, ahead, one, state)


def pieces(vectors):
    widths = (MX, VD, D, FF, D, D, D, D, D, D, 2 * ZD, 2 * ZD, NB)
    collected = []
    offset = 0
    for width in widths:
        collected.append(vectors[offset : offset + width])
        offset = offset + width
    return collected


def product(left_side, right_side, pattern):
    return jnp.einsum(pattern, left_side, right_side, preferred_element_type=jnp.float32)


def silu_grad(values):
    logistic = jax.nn.sigmoid(values)
    return logistic * (1.0 + values * (1.0 - logistic))


def layer_norm(values, norm_gain, norm_shift):
    centered = values - jnp.mean(values, axis=-1, keepdims=True)
    inverse = lax.rsqrt(jnp.mean(centered * centered, axis=-1, keepdims=True) + EPS_NORM)
    normed = centered * inverse
    return (normed * norm_gain + norm_shift, normed, inverse)


def norm_back(incoming, normed, inverse, norm_gain):
    scaled = incoming * norm_gain
    result = inverse * (
        scaled
        - jnp.mean(scaled, axis=-1, keepdims=True)
        - normed * jnp.mean(scaled * normed, axis=-1, keepdims=True)
    )
    return (result, jnp.sum(incoming * normed, axis=0), jnp.sum(incoming, axis=0))


def running(drive, decays, backward):
    result = drive
    factor = decays
    stride = 1
    total_rows = drive.shape[0]
    while stride < total_rows:
        padding = jnp.zeros((stride,) + drive.shape[1:], jnp.float32)
        if backward:
            shifted = jnp.concatenate([result[stride:], padding], axis=0)
        else:
            shifted = jnp.concatenate([padding, result[:-stride]], axis=0)
        result = result + factor * shifted
        factor = factor * factor
        stride = stride * 2
    return result


def compose(earlier, latter):
    return (earlier[0] * latter[0], latter[0] * earlier[1] + latter[1])


def toeplitz(profile, row_count, column_count):
    width_all = row_count + column_count
    tiled = jnp.tile(profile, row_count)[: row_count * (width_all - 1)]
    return tiled.reshape(row_count, width_all - 1)[:, row_count - 1 :]


def diagonal_sums(matrix):
    row_count, column_count = matrix.shape
    width_all = row_count + column_count
    padded = jnp.pad(matrix, ((0, 0), (row_count - 1, 0)))
    flattened = jnp.pad(padded.reshape(-1), (0, row_count))
    return jnp.sum(flattened.reshape(row_count, width_all), axis=0, dtype=jnp.float32)


def plain_update(weight, gradient, moment, decay_rate):
    moment_new = decay_rate * moment + (1.0 - decay_rate) * (gradient * gradient + EPS_ONE)
    update = gradient * lax.rsqrt(moment_new)
    rms_update = jnp.sqrt(jnp.mean(update * update))
    update = update / jnp.maximum(1.0, rms_update / CLIP_UPDATE)
    rms_weight = jnp.sqrt(jnp.mean(weight * weight))
    return (weight - RATE * jnp.maximum(EPS_TWO, rms_weight) * update, moment_new)


def on_device(
    tokens,
    cotangent,
    mixer_weight,
    widen_weight,
    narrow_weight,
    vectors,
    averager,
    bias_index,
    mixer_rows,
    mixer_cols,
    widen_rows,
    widen_cols,
    narrow_rows,
    narrow_cols,
    vector_moment,
    averager_moment,
):
    blocks = lax.axis_size("blk")
    position = lax.axis_index("blk")
    length = tokens.shape[1]
    full_length = length * blocks
    shards = (
        mixer_weight.astype(jnp.bfloat16),
        widen_weight.astype(jnp.bfloat16),
        narrow_weight.astype(jnp.bfloat16),
    )
    mixer_low, widen_low, narrow_low = (
        lax.all_gather(shards[0], "blk", axis=1, tiled=True),
        lax.all_gather(shards[1], "blk", axis=2, tiled=True),
        lax.all_gather(shards[2], "blk", axis=2, tiled=True),
    )
    (
        bias_mixer,
        bias_value,
        bias_hidden,
        bias_expand,
        bias_project,
        gain_one,
        shift_one,
        gain_two,
        shift_two,
        omega_scale,
        qk_gain,
        qk_shift,
        bias_table,
    ) = pieces(vectors)
    damping = jax.nn.sigmoid(averager[0])
    mixing = jax.nn.sigmoid(averager[1])
    decays = 1.0 - damping * mixing
    log_decay = jnp.log(decays)
    inflow = damping * averager[2]
    outflow = averager[3] * NH ** (-0.5)
    inputs = tokens[0]
    drive = inflow[None] * inputs[:, :, None]
    local_states = running(drive, decays, False)
    whole_decay = jnp.exp(log_decay * length)
    identity = (jnp.ones_like(decays), jnp.zeros_like(decays))
    entering = carried_in((whole_decay, local_states[-1]), "blk", compose, identity, False)[1]
    steps_ahead = (jnp.arange(length, dtype=jnp.int32) + 1).astype(jnp.float32)
    states = local_states + jnp.exp(log_decay[None] * steps_ahead[:, None, None]) * entering[None]
    pre_act = jnp.sum(states * outflow[None], axis=2) + omega_scale * inputs
    prime_low = jax.nn.silu(pre_act).astype(jnp.bfloat16)
    mixed_out = jnp.dot(prime_low, mixer_low, preferred_element_type=jnp.float32) + bias_mixer
    update_gate = jax.nn.sigmoid(mixed_out[:, :D])
    shared_pre = mixed_out[:, D : D + ZD]
    reset_pre = mixed_out[:, D + ZD : D + ZD + VD]
    hidden_x = mixed_out[:, D + ZD + VD :]
    shared = jax.nn.silu(shared_pre)
    reset_gate = jax.nn.silu(reset_pre)
    scaling = ZD ** (-0.5)
    queries = ((shared * qk_gain[:ZD] + qk_shift[:ZD]) * scaling).astype(jnp.bfloat16)
    key_rows = (shared * qk_gain[ZD:] + qk_shift[ZD:]).astype(jnp.bfloat16)
    inputs_low = inputs.astype(jnp.bfloat16)
    value_pre = jnp.dot(inputs_low, widen_low[0], preferred_element_type=jnp.float32) + bias_value
    value_rows = jax.nn.silu(value_pre).astype(jnp.bfloat16)
    key_all, value_all = (
        lax.all_gather(key_rows, "blk", axis=0, tiled=True),
        lax.all_gather(value_rows, "blk", axis=0, tiled=True),
    )
    buckets = jnp.arange(NB, dtype=jnp.int32)
    selector = (bias_index[:, None] == buckets[None, :]).astype(jnp.float32)
    bias_row = jnp.concatenate(
        [
            jnp.dot(selector, bias_table, precision=lax.Precision.HIGHEST),
            jnp.zeros((1,), jnp.float32),
        ]
    )
    begin = (blocks - 1 - position) * length
    profile = lax.dynamic_slice_in_dim(bias_row, begin, length + full_length)
    scores = product(queries, key_all, "qc,kc->qk") + toeplitz(profile, length, full_length)
    row_peak = jnp.max(scores, axis=1, keepdims=True)
    log_total = row_peak + jnp.log(jnp.sum(jnp.exp(scores - row_peak), axis=1, keepdims=True))
    softened = jnp.exp(scores - log_total)
    softened_low = softened.astype(jnp.bfloat16)
    attended = jnp.dot(softened_low, value_all, preferred_element_type=jnp.float32)
    gated_low = (reset_gate * attended).astype(jnp.bfloat16)
    hidden_pre = (
        hidden_x
        + jnp.dot(gated_low, narrow_low[0], preferred_element_type=jnp.float32)
        + bias_hidden
    )
    hidden_act = jax.nn.silu(hidden_pre)
    residual_one = inputs + update_gate * (hidden_act - inputs)
    layer_one, normed_one, inverse_one = layer_norm(residual_one, gain_one, shift_one)
    layer_low = layer_one.astype(jnp.bfloat16)
    expand_pre = jnp.dot(layer_low, widen_low[1], preferred_element_type=jnp.float32) + bias_expand
    expand_low = jax.nn.silu(expand_pre).astype(jnp.bfloat16)
    project_two = (
        jnp.dot(expand_low, narrow_low[1], preferred_element_type=jnp.float32) + bias_project
    )
    block_out, normed_two, inverse_two = layer_norm(layer_one + project_two, gain_two, shift_two)
    grad_second, gain_two_grad, shift_two_grad = norm_back(
        cotangent[0], normed_two, inverse_two, gain_two
    )
    project_low = grad_second.astype(jnp.bfloat16)
    grad_down = product(expand_low, project_low, "tf,td->fd")
    expand_grad_low = (
        product(project_low, narrow_low[1], "td,fd->tf") * silu_grad(expand_pre)
    ).astype(jnp.bfloat16)
    grad_up = product(layer_low, expand_grad_low, "td,tf->df")
    grad_layer = grad_second + product(expand_grad_low, widen_low[1], "tf,df->td")
    grad_first, gain_one_grad, shift_one_grad = norm_back(
        grad_layer, normed_one, inverse_one, gain_one
    )
    grad_update = grad_first * (hidden_act - inputs)
    hidden_grad_low = (grad_first * update_gate * silu_grad(hidden_pre)).astype(jnp.bfloat16)
    grad_hidden_weight = product(gated_low, hidden_grad_low, "tv,td->vd")
    grad_gated = product(hidden_grad_low, narrow_low[0], "td,vd->tv")
    grad_reset = grad_gated * attended
    attend_grad_low = (grad_gated * reset_gate).astype(jnp.bfloat16)
    grad_softened = product(attend_grad_low, value_all, "tv,kv->tk")
    row_inner = jnp.sum(softened * grad_softened, axis=1, keepdims=True)
    score_grad_low = (softened * (grad_softened - row_inner)).astype(jnp.bfloat16)
    grad_queries = product(score_grad_low, key_all, "tk,kc->tc")
    profile_grad = diagonal_sums(score_grad_low)
    partial_keys = product(score_grad_low, queries, "tk,tc->kc")
    partial_values = product(softened_low, attend_grad_low, "tk,tv->kv")
    grad_keys, grad_values = (
        lax.psum_scatter(partial_keys, "blk", scatter_dimension=0, tiled=True),
        lax.psum_scatter(partial_values, "blk", scatter_dimension=0, tiled=True),
    )
    grad_shared = grad_queries * scaling * qk_gain[:ZD] + grad_keys * qk_gain[ZD:]
    qk_gain_grad = jnp.concatenate(
        [jnp.sum(grad_queries * scaling * shared, axis=0), jnp.sum(grad_keys * shared, axis=0)]
    )
    qk_shift_grad = jnp.concatenate(
        [jnp.sum(grad_queries * scaling, axis=0), jnp.sum(grad_keys, axis=0)]
    )
    value_grad_low = (grad_values * silu_grad(value_pre)).astype(jnp.bfloat16)
    grad_value_weight = product(inputs_low, value_grad_low, "td,tv->dv")
    mixed_grad_low = jnp.concatenate(
        [
            grad_update * update_gate * (1.0 - update_gate),
            grad_shared * silu_grad(shared_pre),
            grad_reset * silu_grad(reset_pre),
            hidden_grad_low.astype(jnp.float32),
        ],
        axis=1,
    ).astype(jnp.bfloat16)
    grad_mixer_weight = product(prime_low, mixed_grad_low, "td,tm->dm")
    grad_pre = product(mixed_grad_low, mixer_low, "tm,dm->td") * silu_grad(pre_act)
    local_adjoint = running(outflow[None] * grad_pre[:, :, None], decays, True)
    leaving = carried_in((whole_decay, decays * local_adjoint[0]), "blk", compose, identity, True)[
        1
    ]
    steps_behind = (length - 1 - jnp.arange(length, dtype=jnp.int32)).astype(jnp.float32)
    adjoint = local_adjoint + jnp.exp(log_decay[None] * steps_behind[:, None, None]) * leaving[None]
    previous = jnp.concatenate([entering[None], states[:-1]], axis=0)
    grad_decay = jnp.sum(adjoint * previous, axis=0)
    grad_inflow = jnp.sum(adjoint * inputs[:, :, None], axis=0)
    grad_outflow = jnp.sum(grad_pre[:, :, None] * states, axis=0)
    tokens_grad = (
        grad_first * (1.0 - update_gate)
        + product(value_grad_low, widen_low[0], "tv,dv->td")
        + grad_pre * omega_scale
        + jnp.sum(adjoint * inflow[None], axis=2)
    )
    grad_damping = -mixing * grad_decay + averager[2] * grad_inflow
    average_grad = jnp.stack(
        [
            grad_damping * damping * (1.0 - damping),
            -damping * grad_decay * mixing * (1.0 - mixing),
            damping * grad_inflow,
            grad_outflow * NH ** (-0.5),
        ]
    )
    row_grad = lax.dynamic_update_slice(
        jnp.zeros((2 * full_length,), jnp.float32), profile_grad, (begin,)
    )
    table_grad = jnp.dot(row_grad[:-1], selector, precision=lax.Precision.HIGHEST)
    vector_local = jnp.concatenate(
        [
            jnp.sum(mixed_grad_low, axis=0, dtype=jnp.float32),
            jnp.sum(value_grad_low, axis=0, dtype=jnp.float32),
            jnp.sum(hidden_grad_low, axis=0, dtype=jnp.float32),
            jnp.sum(expand_grad_low, axis=0, dtype=jnp.float32),
            jnp.sum(project_low, axis=0, dtype=jnp.float32),
            gain_one_grad,
            shift_one_grad,
            gain_two_grad,
            shift_two_grad,
            jnp.sum(grad_pre * inputs, axis=0),
            qk_gain_grad,
            qk_shift_grad,
            table_grad,
        ]
    )
    full_grads = (
        grad_mixer_weight,
        jnp.stack([grad_value_weight, grad_up]),
        jnp.stack([grad_hidden_weight, grad_down]),
    )
    column_grads = (
        lax.psum_scatter(
            full_grads[0].astype(jnp.bfloat16), "blk", scatter_dimension=1, tiled=True
        ).astype(jnp.float32),
        lax.psum_scatter(
            full_grads[1].astype(jnp.bfloat16), "blk", scatter_dimension=2, tiled=True
        ).astype(jnp.float32),
        lax.psum_scatter(
            full_grads[2].astype(jnp.bfloat16), "blk", scatter_dimension=2, tiled=True
        ).astype(jnp.float32),
    )
    mixer_part, widen_part, narrow_part = (
        lax.psum(column_grads[0].astype(jnp.bfloat16), "dp").astype(jnp.float32),
        lax.psum(column_grads[1].astype(jnp.bfloat16), "dp").astype(jnp.float32),
        lax.psum(column_grads[2].astype(jnp.bfloat16), "dp").astype(jnp.float32),
    )
    vector_sum, average_sum = lax.psum((vector_local, average_grad), ("dp", "blk"))
    stacks = (mixer_part[None], widen_part, narrow_part)
    masters = (mixer_weight[None], widen_weight, narrow_weight)
    rows_old = (mixer_rows[None], widen_rows, narrow_rows)
    columns_old = (mixer_cols[None], widen_cols, narrow_cols)
    column_total = (MX, VD, D)
    local_square = jnp.sum(vector_sum * vector_sum) + jnp.sum(average_sum * average_sum)
    grad_squares = tuple((jnp.sum(matrix * matrix, axis=(1, 2)) for matrix in stacks))
    weight_squares = tuple((jnp.sum(matrix * matrix, axis=(1, 2)) for matrix in masters))
    decay_rate = 1.0 - STEP ** (-0.8)
    summed = lax.psum(grad_squares + weight_squares, "blk")
    clip_norm = jnp.sqrt(
        jnp.sum(summed[0]) + jnp.sum(summed[1]) + jnp.sum(summed[2]) + local_square
    )
    factor = jnp.minimum(1.0, CLIP_NORM / clip_norm)
    clipped = tuple((matrix * factor for matrix in stacks))
    squares = tuple((matrix * matrix + EPS_ONE for matrix in clipped))
    row_sums = lax.psum(tuple((jnp.sum(square_part, axis=2) for square_part in squares)), "blk")
    column_means = tuple((jnp.mean(square_part, axis=1) for square_part in squares))
    weight_total = summed[3:6]
    rows_new = tuple(
        (
            decay_rate * rows_old[member]
            + (1.0 - decay_rate) * row_sums[member] / column_total[member]
            for member in range(3)
        )
    )
    columns_new = tuple(
        (
            decay_rate * columns_old[member] + (1.0 - decay_rate) * column_means[member]
            for member in range(3)
        )
    )
    updates = tuple(
        (
            clipped[member]
            * lax.rsqrt(
                rows_new[member][:, :, None]
                * columns_new[member][:, None, :]
                / jnp.mean(rows_new[member], axis=1)[:, None, None]
            )
            for member in range(3)
        )
    )
    update_squares = lax.psum(
        tuple((jnp.sum(update * update, axis=(1, 2)) for update in updates)), "blk"
    )
    new_list = []
    for member in range(3):
        entries = rows_old[member].shape[1] * column_total[member]
        rms_update = jnp.sqrt(update_squares[member] / entries)
        bounded = updates[member] / jnp.maximum(1.0, rms_update / CLIP_UPDATE)[:, None, None]
        rms_weight = jnp.sqrt(weight_total[member] / entries)
        new_list.append(
            masters[member] - RATE * jnp.maximum(EPS_TWO, rms_weight)[:, None, None] * bounded
        )
    vector_grad = vector_sum * factor
    averager_grad = average_sum * factor
    vector_new, moment_vector = plain_update(vectors, vector_grad, vector_moment, decay_rate)
    averager_new, moment_averager = plain_update(
        averager, averager_grad, averager_moment, decay_rate
    )
    return (
        block_out[None],
        tokens_grad[None],
        clipped[0][0],
        clipped[1],
        clipped[2],
        vector_grad,
        averager_grad,
        new_list[0][0],
        new_list[1],
        new_list[2],
        vector_new,
        averager_new,
        rows_new[0][0],
        columns_new[0][0],
        rows_new[1],
        columns_new[1],
        rows_new[2],
        columns_new[2],
        moment_vector,
        moment_averager,
        clip_norm,
    )


def solution(mesh):
    in_specs = (
        P("dp", "blk", None),
        P("dp", "blk", None),
        P(None, "blk"),
        P(None, None, "blk"),
        P(None, None, "blk"),
        P(),
        P(),
        P(),
        P(),
        P("blk"),
        P(),
        P(None, "blk"),
        P(),
        P(None, "blk"),
        P(),
        P(),
    )
    out_specs = (
        P("dp", "blk", None),
        P("dp", "blk", None),
        P(None, "blk"),
        P(None, None, "blk"),
        P(None, None, "blk"),
        P(),
        P(),
        P(None, "blk"),
        P(None, None, "blk"),
        P(None, None, "blk"),
        P(),
        P(),
        P(),
        P("blk"),
        P(),
        P(None, "blk"),
        P(),
        P(None, "blk"),
        P(),
        P(),
        P(),
    )
    return jax.shard_map(
        on_device, mesh=mesh, in_specs=in_specs, out_specs=out_specs, check_vma=False
    )
```

profile of v0, /device:TPU:0, one launch (start us, length us, event | category | flops | bytes accessed | tf_op | source)
XLA Modules:
  0.0 1533.0 jit_solution(9323523332051825680)
XLA Ops:
  7.3 2.7 multiply_reduce_fusion.10
  10.0 2.7 multiply_reduce_fusion.6
  13.6 81.0 %all-gather.7.cloned.1.call-done = bf16[2,768,1536]{1,2,0:T(8,128)(2,1)} async-done(((bf16[2,768,96]{1,2,0:T(8,128)(2,1)}), bf16[2,768,1536]{1,2,0:T(8,128)(2,1)}) %all-gather.7.cloned.1.call-update) | async-done | bytes 4718608 | tf_op jit(solution)/shard_map/all_gather | solution.py:149
  94.5 3.7 multiply_convert_fusion.6
  103.7 2.1 multiply_add_fusion.14
  106.3 2.2 multiply_add_fusion.13
  116.0 2.6 copy-done
  118.7 1.5 fusion.7
  120.4 1.8 reshape.211
  122.3 50.9 %all_gather.29 = f32[16,768,16]{1,2,0:T(8,128)S(1)} all-gather(f32[1,768,16]{1,2,0:T(8,128)S(1)} %slice.208), channel_id=1, replica_groups=mesh['dp'=2,'blk'=16] {'blk'}, dimensions={0}, use_global_device_ids=true | all-gather | bytes 835584 | tf_op jit(solution)/shard_map/all_gather | solution.py:28
  173.1 43.8 %all_gather.28 = f32[16,768,16]{1,2,0:T(8,128)S(1)} all-gather(f32[1,768,16]{1,2,0:T(8,128)S(1)} %copy-done.63), channel_id=1, replica_groups=mesh['dp'=2,'blk'=16] {'blk'}, dimensions={0}, use_global_device_ids=true | all-gather | bytes 835584 | tf_op jit(solution)/shard_map/all_gather | solution.py:28
  217.0 6.6 multiply_reduce_fusion.3
  223.8 4.4 convolution_add_fusion
  228.3 45.4 %all_gather.31 = bf16[2048,128]{1,0:T(8,128)(2,1)S(1)} all-gather(bf16[128,128]{1,0:T(8,128)(2,1)S(1)} %add_convert_fusion), channel_id=1, replica_groups=mesh['dp'=2,'blk'=16] {'blk'}, dimensions={0}, use_global_device_ids=true | all-gather | bytes 557056 | tf_op jit(solution)/shard_map/all_gather | solution.py:197
  274.4 23.7 %all-gather.9.cloned.1.call-done = bf16[2048,1536]{1,0:T(8,128)(2,1)} async-done(((bf16[128,1536]{1,0:T(8,128)(2,1)}), bf16[2048,1536]{1,0:T(8,128)(2,1)}) %all-gather.9.cloned.1.call-update) | async-done | bytes 6291472 | tf_op jit(solution)/shard_map/all_gather | solution.py:198
  298.1 5.0 multiply_convert_fusion.5
  303.2 78.4 %all-gather.11.cloned.1.call-done = bf16[2,1536,768]{1,2,0:T(8,128)(2,1)} async-done(((bf16[2,1536,48]{1,2,0:T(8,128)(2,1)}), bf16[2,1536,768]{1,2,0:T(8,128)(2,1)}) %all-gather.11.cloned.1.call-update) | async-done | bytes 4718608 | tf_op jit(solution)/shard_map/all_gather | solution.py:150
  381.5 3.0 fusion.75
  384.8 2.6 convolution_add_fusion.1
  389.4 1.5 convert_reduce_fusion.3
  393.5 1.7 convert_reduce_fusion.4
  395.2 1.5 multiply_convert_fusion.3
  396.9 2.2 multiply_reduce_fusion.4
  400.9 7.5 fusion.64
  408.5 5.9 slice.228
  414.4 2.2 fusion.3
  416.7 2.2 fusion.4
  418.9 58.4 %reduce-scatter.7.cloned.1.call-done = f32[128,128]{1,0:T(8,128)} async-done(((f32[2048,128]{1,0:T(8,128)}), f32[128,128]{1,0:T(8,128)}) %reduce-scatter.7.cloned.1.call-update) | async-done | bytes 65552 | tf_op jit(solution)/shard_map/reduce_scatter | solution.py:259
  477.2 1.7 multiply_reduce_fusion.21
  479.0 3.9 multiply_reduce_fusion.11
  486.1 2.8 multiply_reduce_fusion
  489.7 1.4 multiply_add_fusion.6
  491.9 1.4 multiply_add_fusion.5
  501.8 2.6 copy-done.1
  504.4 49.0 %all_gather.35 = f32[16,768,16]{1,2,0:T(8,128)S(1)} all-gather(f32[1,768,16]{1,2,0:T(8,128)S(1)} %slice_multiply_fusion), channel_id=1, replica_groups=mesh['dp'=2,'blk'=16] {'blk'}, dimensions={0}, use_global_device_ids=true | all-gather | bytes 835584 | tf_op jit(solution)/shard_map/all_gather | solution.py:28
  553.5 12.7 while.27
  566.2 7.9 fusion
  575.0 4.3 pad_maximum_fusion.1
  579.3 12.8 copy.64
  592.3 3.6 convolution_convert_fusion
  596.0 1.9 fusion.2
  597.9 94.8 %reduce-scatter.5.cloned.1.call-done = f32[128,1536]{1,0:T(8,128)} async-done(((f32[2048,1536]{1,0:T(8,128)}), f32[128,1536]{1,0:T(8,128)}) %reduce-scatter.5.cloned.1.call-update) | async-done | bytes 786448 | tf_op jit(solution)/shard_map/reduce_scatter | solution.py:260
  692.8 2.3 convert_reduce_fusion.2
  696.6 2.5 pad_maximum_fusion
  699.9 1.6 multiply_reduce_fusion.19
  710.6 110.4 %all-reduce.25.cloned.1.call-done = f32[4,768,16]{1,2,0:T(8,128)} async-done(((f32[4,768,16]{1,2,0:T(8,128)}), f32[4,768,16]{1,2,0:T(8,128)}) %all-reduce.25.cloned.1.call-update) | async-done | bytes 196624 | tf_op jit(solution)/shard_map/psum | solution.py:349
  821.0 1.7 multiply_reduce_fusion.20
  822.6 184.7 %all-reduce.27.cloned.1.call-done = bf16[2,1536,768]{1,0,2:T(2,128)(2,1)} async-done(((bf16[2,1536,768]{1,0,2:T(2,128)(2,1)}), bf16[2,1536,768]{1,0,2:T(2,128)(2,1)}) %all-reduce.27.cloned.1.call-update) | async-done | bytes 4718608
  1007.4 1.9 constant_dynamic-slice_fusion
  1015.5 135.6 %reduce-scatter.9.cloned.1.call-done = bf16[768,200]{0,1:T(8,128)(2,1)} async-done(((bf16[768,3200]{0,1:T(8,128)(2,1)}), bf16[768,200]{0,1:T(8,128)(2,1)}) %reduce-scatter.9.cloned.1.call-update) | async-done | bytes 307216 | tf_op jit(solution)/shard_map/reduce_scatter | solution.py:334
  1151.1 142.6 %reduce-scatter.11.cloned.1.call-done = bf16[2,768,96]{1,2,0:T(8,128)(2,1)} async-done(((bf16[2,768,1536]{1,2,0:T(8,128)(2,1)}), bf16[2,768,96]{1,2,0:T(8,128)(2,1)}) %reduce-scatter.11.cloned.1.call-update) | async-done | bytes 294928 | tf_op jit(solution)/shard_map/reduce_scatter | solution.py:337
  1295.6 40.3 %psum.125 = f32[12288]{0:T(1024)S(1)} all-reduce(f32[12288]{0:T(1024)S(1)} %constant_dynamic-update-slice_fusion), channel_id=1, replica_groups=mesh['dp'=2,'blk'=16] {'dp','blk'}, use_global_device_ids=true, to_apply=%region_48.49 | all-reduce | flops 12288 | bytes 98304 | tf_op jit(solution)/shard_map/psum | solution.py:349
  1336.5 3.7 fusion.19
  1340.2 1.7 fusion.27
  1343.1 1.7 fusion.29
  1346.1 40.9 %all-reduce.19 = (f32[]{:T(128)}, f32[2]{0:T(128)S(1)}, f32[2]{0:T(128)S(1)}) all-reduce(f32[]{:T(128)} %fusion.27, f32[2]{0:T(128)S(1)} %fusion.28, f32[2]{0:T(128)S(1)} %fusion.29), channel_id=1, replica_groups=mesh['dp'=2,'blk'=16] {'blk'}, use_global_device_ids=true, to_apply=%region_22.23 | all-reduce | flops 5 | bytes 40 | tf_op jit(solution)/shard_map/psum | solution.py:359
  1390.2 1.6 fusion.40
  1393.0 1.4 fusion.30
  1394.5 1.5 multiply_reduce_fusion.18
  1398.6 71.8 %all-reduce.18 = (f32[1,768]{1,0:T(1,128)S(1)}, f32[2,768]{1,0:T(2,128)S(1)}, f32[2,1536]{1,0:T(2,128)S(1)}) all-reduce(f32[1,768]{1,0:T(1,128)S(1)} %reduce_sum.566, f32[2,768]{1,0:T(2,128)S(1)} %get-tuple-element.268, f32[2,1536]{1,0:T(2,128)S(1)} %get-tuple-element.273), channel_id=1, replica_groups=mesh['dp'=2,'blk'=16] {'blk'}, use_global_device_ids=true, to_apply=%region_58.59 | all-reduce | flops 5376 | bytes 43008 | tf_op jit(solution)/shard_map/psum | solution.py:366
  1473.2 3.2 multiply_reduce_fusion.7
  1478.2 37.2 %all-reduce.17 = (f32[1]{0:T(128)}, f32[1]{0:T(128)}, f32[2]{0:T(128)S(1)}, f32[2]{0:T(128)S(1)}, f32[2]{0:T(128)S(1)}, /*index=5*/f32[2]{0:T(128)S(1)}) all-reduce(f32[1]{0:T(128)} %bitcast.38, f32[1]{0:T(128)} %bitcast.36, f32[2]{0:T(128)S(1)} %multiply_reduce_fusion.9, ...), channel_id=1, replica_groups=mesh['dp'=2,'blk'=16] {'blk'}, use_global_device_ids=true, to_apply=%region_62.63 | all-reduce | flops 10 | bytes 80 | tf_op jit(solution)/shard_map/psum | solution.py:393
  1518.4 2.0 copy.68
  1520.4 2.2 multiply_subtract_fusion.1
  (383 shorter events, 79.2 us)
Async XLA Ops:
  7.2 92.7 %copy-start.2 = (f32[1,128,768]{2,1,0:T(8,128)S(1)}, f32[1,128,768]{2,1,0:T(8,128)}, u32[]{:S(2)}) copy-start(f32[1,128,768]{2,1,0:T(8,128)} %param.20) | copy-start | bytes 1179652
  7.2 91.1 %copy-start.22 = (f32[2,1536,48]{1,2,0:T(8,128)S(1)}, f32[2,1536,48]{1,2,0:T(8,128)}, u32[]{:S(2)}) copy-start(f32[2,1536,48]{1,2,0:T(8,128)} %param.24) | copy-start | bytes 1769476
  7.2 92.6 %copy-start.18 = (f32[4,768,16]{1,2,0:T(8,128)S(1)}, f32[4,768,16]{1,2,0:T(8,128)}, u32[]{:S(2)}) copy-start(f32[4,768,16]{1,2,0:T(8,128)} %param.26) | copy-start | bytes 589828
  7.2 87.3 %all-gather.7.cloned.1.call-start = ((), (), s32[]{:S(2)}) async-start(), calls=%async_computation.5 | async-start | bytes 5013504 | tf_op jit(solution)/shard_map/all_gather | solution.py:149
  10.0 213.8 %all-gather.5.cloned.1.call-start = ((), (), s32[]{:S(2)}) async-start(), calls=%async_computation.4 | async-start | bytes 5222400 | tf_op jit(solution)/shard_map/all_gather | solution.py:148
  12.7 285.4 %all-gather.9.cloned.1.call-start = ((), (), s32[]{:S(2)}) async-start(), calls=%async_computation.6 | async-start | bytes 6684672 | tf_op jit(solution)/shard_map/all_gather | solution.py:198
  98.3 283.3 %all-gather.11.cloned.1.call-start = ((), (), s32[]{:S(2)}) async-start(), calls=%async_computation.7 | async-start | bytes 5013504 | tf_op jit(solution)/shard_map/all_gather | solution.py:150
  99.8 377.5 %reduce-scatter.7.cloned.1.call-start = ((), (), s32[]{:S(2)}) async-start(), calls=%async_computation.9 | async-start | bytes 1114112 | tf_op jit(solution)/shard_map/reduce_scatter | solution.py:259
  99.9 117.1 %copy-start.43 = (f32[768,16]{0,1:T(8,128)}, f32[768,16]{0,1:T(8,128)S(1)}, u32[]{:S(2)}) copy-start(f32[768,16]{0,1:T(8,128)S(1)} %get-tuple-element.337) | copy-start | bytes 147460
  103.7 9.5 copy-start.47
  103.7 11.1 copy-start.45
  118.6 54.5 %copy-start.63 = (f32[1,768,16]{1,2,0:T(8,128)S(1)}, f32[1,768,16]{1,2,0:T(8,128)}, u32[]{:S(2)}) copy-start(f32[1,768,16]{1,2,0:T(8,128)} %get-tuple-element.372) | copy-start | bytes 147460
  122.2 265.2 %copy-start.77 = (f32[768]{0:T(1024)}, f32[768]{0:T(1024)S(1)}, u32[]{:S(2)}) copy-start(f32[768]{0:T(1024)S(1)} %get-tuple-element.366) | copy-start | bytes 9220
  122.2 271.2 %copy-start.73 = (f32[768]{0:T(1024)}, f32[768]{0:T(1024)S(1)}, u32[]{:S(2)}) copy-start(f32[768]{0:T(1024)S(1)} %get-tuple-element.367) | copy-start | bytes 9220
  122.3 356.7 %copy-start.76 = (f32[768]{0:T(1024)}, f32[768]{0:T(1024)S(1)}, u32[]{:S(2)}) copy-start(f32[768]{0:T(1024)S(1)} %get-tuple-element.369) | copy-start | bytes 9220
  223.6 50.1 %copy-start.8 = (f32[128,2175]{1,0:T(8,128)S(1)}, f32[128,2175]{1,0:T(8,128)}, u32[]{:S(2)}) copy-start(f32[128,2175]{1,0:T(8,128)} %reshape.211) | copy-start | bytes 3340804
  228.2 45.9 %copy-start.16 = (f32[128,3200]{1,0:T(8,128)}, f32[128,3200]{1,0:T(8,128)S(1)}, u32[]{:S(2)}) copy-start(f32[128,3200]{1,0:T(8,128)S(1)} %convolution_add_fusion) | copy-start | bytes 4915204
  273.7 29.5 %copy-start.24 = (bf16[2048,128]{1,0:T(8,128)(2,1)}, bf16[2048,128]{1,0:T(8,128)(2,1)S(1)}, u32[]{:S(2)}) copy-start(bf16[2048,128]{1,0:T(8,128)(2,1)S(1)} %all_gather.31) | copy-start | bytes 1572868
  303.2 78.4 %copy-start.60 = (bf16[128,1536]{1,0:T(8,128)(2,1)}, bf16[128,1536]{1,0:T(8,128)(2,1)S(1)}, u32[]{:S(2)}) copy-start(bf16[128,1536]{1,0:T(8,128)(2,1)S(1)} %get-tuple-element.383) | copy-start | bytes 1179652
  395.2 83.7 %copy-start.13 = (bf16[128,768]{1,0:T(8,128)(2,1)}, bf16[128,768]{1,0:T(8,128)(2,1)S(1)}, u32[]{:S(2)}) copy-start(bf16[128,768]{1,0:T(8,128)(2,1)S(1)} %get-tuple-element.330) | copy-start | bytes 589828
  399.5 77.8 %copy-start.6 = (bf16[128,2048]{1,0:T(8,128)(2,1)}, bf16[128,2048]{1,0:T(8,128)(2,1)S(1)}, u32[]{:S(2)}) copy-start(bf16[128,2048]{1,0:T(8,128)(2,1)S(1)} %multiply_convert_fusion) | copy-start | bytes 1572868
  400.9 291.9 %reduce-scatter.5.cloned.1.call-start = ((), (), s32[]{:S(2)}) async-start(), calls=%async_computation.8 | async-start | bytes 13369344 | tf_op jit(solution)/shard_map/reduce_scatter | solution.py:260
  408.4 412.6 %all-reduce.25.cloned.1.call-start = ((), (), s32[]{:S(2)}) async-start(), calls=%async_computation.12 | async-start | bytes 393216 | tf_op jit(solution)/shard_map/psum | solution.py:349
  414.4 62.8 %copy-start.25 = (bf16[2048,128]{1,0:T(8,128)(2,1)S(1)}, bf16[2048,128]{1,0:T(8,128)(2,1)}, u32[]{:S(2)}) copy-start(bf16[2048,128]{1,0:T(8,128)(2,1)} %copy-done.24) | copy-start | bytes 1572868
  414.4 64.5 %copy-start.29 = (bf16[128,768]{1,0:T(8,128)(2,1)S(1)}, bf16[128,768]{1,0:T(8,128)(2,1)}, u32[]{:S(2)}) copy-start(bf16[128,768]{1,0:T(8,128)(2,1)} %get-tuple-element.339) | copy-start | bytes 589828
  414.4 64.5 %copy-start.32 = (f32[128,768]{1,0:T(8,128)S(1)}, f32[128,768]{1,0:T(8,128)}, u32[]{:S(2)}) copy-start(f32[128,768]{1,0:T(8,128)} %copy-done.31) | copy-start | bytes 1179652
  414.4 64.6 %copy-start.34 = (bf16[128,1536]{1,0:T(8,128)(2,1)S(1)}, bf16[128,1536]{1,0:T(8,128)(2,1)}, u32[]{:S(2)}) copy-start(bf16[128,1536]{1,0:T(8,128)(2,1)} %get-tuple-element.341) | copy-start | bytes 1179652
  500.7 65.5 %copy-start.44 = (f32[768,16]{0,1:T(8,128)S(1)}, f32[768,16]{0,1:T(8,128)}, u32[]{:S(2)}) copy-start(f32[768,16]{0,1:T(8,128)} %copy-done.43) | copy-start | bytes 147460
  574.9 432.5 %all-reduce.27.cloned.1.call-start = ((), (), s32[]{:S(2)}) async-start(), calls=%async_computation.13 | async-start | bytes 9437184
  579.3 13.0 copy-start.14
  579.3 13.0 copy-start.28
  579.3 13.0 copy-start.30
  579.3 13.0 copy-start.35
  579.3 13.0 copy-start.68
  592.2 558.9 %reduce-scatter.9.cloned.1.call-start = ((), (), s32[]{:S(2)}) async-start(), calls=%async_computation.10 | async-start | bytes 5222400 | tf_op jit(solution)/shard_map/reduce_scatter | solution.py:334
  595.9 697.7 %reduce-scatter.11.cloned.1.call-start = ((), (), s32[]{:S(2)}) async-start(), calls=%async_computation.11 | async-start | bytes 5013504 | tf_op jit(solution)/shard_map/reduce_scatter | solution.py:337
  696.6 10.1 copy-start.7
  699.2 10.1 copy-start.15
  699.2 641.0 %all-reduce.29.cloned.1.call-start = ((), (), s32[]{:S(2)}) async-start(), calls=%async_computation.14 | async-start | bytes 1794048 | tf_op jit(solution)/shard_map/psum | solution.py:345
  699.9 10.6 copy-start.71
  699.9 314.2 %copy-start.79 = (f32[768]{0:T(1024)S(1)}, f32[768]{0:T(1024)}, u32[]{:S(2)}) copy-start(f32[768]{0:T(1024)} %reduce_sum.549) | copy-start | bytes 9220
  709.3 685.2 %copy-start.64 = (f32[4,768,16]{1,2,0:T(8,128)S(1)}, f32[4,768,16]{1,2,0:T(8,128)}, u32[]{:S(2)}) copy-start(f32[4,768,16]{1,2,0:T(8,128)} %param.35) | copy-start | bytes 589828
  710.5 686.1 %copy-start.72 = (f32[12288]{0:T(1024)S(1)}, f32[12288]{0:T(1024)}, u32[]{:S(2)}) copy-start(f32[12288]{0:T(1024)} %param.34) | copy-start | bytes 147460
  710.5 759.9 %copy-start.84 = (f32[2,768]{1,0:T(2,128)S(1)}, f32[2,768]{1,0:T(2,128)}, u32[]{:S(2)}) copy-start(f32[2,768]{1,0:T(2,128)} %param.30) | copy-start | bytes 18436
  821.0 573.5 %copy-start.38 = (f32[4,768,16]{1,2,0:T(8,128)S(1)}, f32[4,768,16]{1,2,0:T(8,128)}, u32[]{:S(2)}) copy-start(f32[4,768,16]{1,2,0:T(8,128)} %all-reduce.25.cloned.1.call-done) | copy-start | bytes 589828
  822.6 648.4 %copy-start.81 = (f32[2,1536]{1,0:T(2,128)S(1)}, f32[2,1536]{1,0:T(2,128)}, u32[]{:S(2)}) copy-start(f32[2,1536]{1,0:T(2,128)} %param.32) | copy-start | bytes 36868
  822.6 649.1 %copy-start.91 = (f32[2,48]{1,0:T(2,128)S(1)}, f32[2,48]{1,0:T(2,128)}, u32[]{:S(2)}) copy-start(f32[2,48]{1,0:T(2,128)} %param.33) | copy-start | bytes 1156
  822.6 649.2 %copy-start.92 = (f32[2,96]{1,0:T(2,128)S(1)}, f32[2,96]{1,0:T(2,128)}, u32[]{:S(2)}) copy-start(f32[2,96]{1,0:T(2,128)} %param.31) | copy-start | bytes 2308
  822.6 649.3 %copy-start.80 = (f32[768]{0:T(1024)S(1)}, f32[768]{0:T(1024)}, u32[]{:S(2)}) copy-start(f32[768]{0:T(1024)} %broadcast_multiply_fusion.4) | copy-start | bytes 9220
  822.6 650.5 %copy-start.93 = (f32[200]{0:T(256)S(1)}, f32[200]{0:T(256)}, u32[]{:S(2)}) copy-start(f32[200]{0:T(256)} %param.29) | copy-start | bytes 2404
  1336.5 141.7 %copy-start.88 = (f32[2]{0:T(128)S(1)}, f32[2]{0:T(128)}, u32[]{:S(2)}) copy-start(f32[2]{0:T(128)} %get-tuple-element.347) | copy-start | bytes 28
  1336.5 179.0 %copy-start.23 = (f32[2,1536,48]{1,2,0:T(8,128)S(1)}, f32[2,1536,48]{1,2,0:T(8,128)}, u32[]{:S(2)}) copy-start(f32[2,1536,48]{1,2,0:T(8,128)} %param.24) | copy-start | bytes 1769476
  1343.1 179.5 %copy-start.21 = (f32[768,200]{0,1:T(8,128)S(1)}, f32[768,200]{0,1:T(8,128)}, u32[]{:S(2)}) copy-start(f32[768,200]{0,1:T(8,128)} %param.22) | copy-start | bytes 1843204
  1393.0 130.7 %copy-start.5 = (f32[2,768,96]{1,2,0:T(8,128)}, f32[2,768,96]{1,2,0:T(8,128)S(1)}, u32[]{:S(2)}) copy-start(f32[2,768,96]{1,2,0:T(8,128)S(1)} %get-tuple-element.325) | copy-start | bytes 1769476
  1393.0 130.7 %copy-start.20 = (f32[4,768,16]{1,2,0:T(8,128)S(1)}, f32[4,768,16]{1,2,0:T(8,128)}, u32[]{:S(2)}) copy-start(f32[4,768,16]{1,2,0:T(8,128)} %param.26) | copy-start | bytes 589828
  1394.5 130.0 %copy-start.4 = (f32[768,200]{0,1:T(8,128)}, f32[768,200]{0,1:T(8,128)S(1)}, u32[]{:S(2)}) copy-start(f32[768,200]{0,1:T(8,128)S(1)} %get-tuple-element.326) | copy-start | bytes 1843204
  1395.9 129.1 %copy-start.39 = (f32[4,768,16]{1,2,0:T(8,128)}, f32[4,768,16]{1,2,0:T(8,128)S(1)}, u32[]{:S(2)}) copy-start(f32[4,768,16]{1,2,0:T(8,128)S(1)} %get-tuple-element.314) | copy-start | bytes 589828
  1397.9 126.5 %copy-start.65 = (f32[12288]{0:T(1024)S(1)}, f32[12288]{0:T(1024)}, u32[]{:S(2)}) copy-start(f32[12288]{0:T(1024)} %get-tuple-element.317) | copy-start | bytes 147460
  1470.5 54.5 %copy-start.69 = (f32[2,768]{1,0:T(2,128)}, f32[2,768]{1,0:T(2,128)S(1)}, u32[]{:S(2)}) copy-start(f32[2,768]{1,0:T(2,128)S(1)} %get-tuple-element.324) | copy-start | bytes 18436
  1471.2 53.9 %copy-start.70 = (f32[2,1536]{1,0:T(2,128)}, f32[2,1536]{1,0:T(2,128)S(1)}, u32[]{:S(2)}) copy-start(f32[2,1536]{1,0:T(2,128)S(1)} %get-tuple-element.322) | copy-start | bytes 36868
  1471.8 53.3 %copy-start.87 = (f32[2,48]{1,0:T(2,128)}, f32[2,48]{1,0:T(2,128)S(1)}, u32[]{:S(2)}) copy-start(f32[2,48]{1,0:T(2,128)S(1)} %multiply_add_fusion.27) | copy-start | bytes 1156
  1471.9 53.2 %copy-start.83 = (f32[2,96]{1,0:T(2,128)}, f32[2,96]{1,0:T(2,128)S(1)}, u32[]{:S(2)}) copy-start(f32[2,96]{1,0:T(2,128)S(1)} %multiply_add_fusion.28) | copy-start | bytes 2308
  1472.5 52.6 %copy-start.75 = (f32[768]{0:T(1024)}, f32[768]{0:T(1024)S(1)}, u32[]{:S(2)}) copy-start(f32[768]{0:T(1024)S(1)} %get-tuple-element.276) | copy-start | bytes 9220
  1473.2 51.9 %copy-start.82 = (f32[200]{0:T(256)}, f32[200]{0:T(256)S(1)}, u32[]{:S(2)}) copy-start(f32[200]{0:T(256)S(1)} %multiply_add_fusion.29) | copy-start | bytes 2404
  (57 other events, 238.8 us)
Sparse Core Ops, SparseCore 0:
  11.3 83.1 all-gather.6
  97.9 97.2 all-gather.4
  198.5 99.5 all-gather.8
  301.3 80.2 all-gather.10
  401.0 76.2 reduce-scatter.6
  483.7 209.0 reduce-scatter.4
  698.3 122.6 all-reduce.24
  826.7 180.6 all-reduce.26
  1013.4 137.5 reduce-scatter.8
  1156.9 136.6 reduce-scatter.10
  1296.8 18.5 all-reduce.28
where the time goes:
time: 1540 us; the launch traced here: 1530 us
  waiting for transfers between devices  910 us (59%)
  blocking collectives  379 us (25%)
  other arithmetic  106 us (7%)
  matrix products  57.7 us (4%)
  local copies, waits for them, and re-layouts  54.2 us (4%)
  between operations  25.6 us (2%)
    unnamed x12, waiting for transfers between devices  185 us
    all_gather x3, blocking collectives, carried_in(): gathered = jax.tree.map(lambda a: lax.all_gather(a, axis), part)  144 us
    reduce_scatter x1, waiting for transfers between devices, on_device(): lax.psum_scatter(full_grads[1].astype(jnp.bfloat16), 'blk', scatter_dimen...  143 us
    reduce_scatter x1, waiting for transfers between devices, on_device(): lax.psum_scatter(full_grads[0].astype(jnp.bfloat16), 'blk', scatter_dimen...  136 us
    psum x1, waiting for transfers between devices, on_device(): lax.psum((vector_local, average_grad), ('dp', 'blk'))  110 us
    reduce_scatter x1, waiting for transfers between devices, on_device(): lax.psum_scatter(partial_values, 'blk', scatter_dimension=0, tiled=True)  94.8 us
    all_gather x1, waiting for transfers between devices, on_device(): lax.all_gather(shards[1], 'blk', axis=2, tiled=True)  81 us
    all_gather x1, waiting for transfers between devices, on_device(): lax.all_gather(shards[2], 'blk', axis=2, tiled=True)  78.4 us
  transfers between devices with their start and end apart: 11, of which 9 were waited for; matrix products, arithmetic and copies ran while one was open for 10% of the time, Pallas kernels for 0%

commit v1 on v0

--- a/solution.py
+++ b/solution.py
@@ -1,6 +1,9 @@
+import functools
 import jax
 import jax.numpy as jnp
 from jax import lax
+from jax.experimental import pallas as pl
+from jax.experimental.pallas import tpu as pltpu
 from jax.sharding import PartitionSpec as P
 
 D = 768
@@ -11,14 +14,1032 @@
 NB = 128
 STEP = 10
 MX = 3200
-
-
 EPS_NORM = 1e-05
 EPS_ONE = 1e-30
 EPS_TWO = 0.001
 CLIP_NORM = 1.0
 CLIP_UPDATE = 1.0
 RATE = 0.5
+
+OFF_MX = 0
+OFF_V = MX
+OFF_H = OFF_V + VD
+OFF_UP = OFF_H + D
+OFF_DOWN = OFF_UP + FF
+OFF_G1 = OFF_DOWN + D
+OFF_S1 = OFF_G1 + D
+OFF_G2 = OFF_S1 + D
+OFF_S2 = OFF_G2 + D
+OFF_OM = OFF_S2 + D
+OFF_QG = OFF_OM + D
+OFF_QS = OFF_QG + 2 * ZD
+OFF_TB = OFF_QS + 2 * ZD
+NVEC = OFF_TB + NB
+
+MESH = pl.DeviceIdType.MESH
+BF = jnp.bfloat16
+F32 = jnp.float32
+NN = (((1,), (0,)), ((), ()))
+NT = (((1,), (1,)), ((), ()))
+TN = (((0,), (0,)), ((), ()))
+
+
+def dot(a, b, dims=NN):
+    return lax.dot_general(a, b, dims, preferred_element_type=F32)
+
+
+def sigmoid(v):
+    return jax.nn.sigmoid(v)
+
+
+def silu(v):
+    return v * sigmoid(v)
+
+
+def silu_grad(v):
+    s = sigmoid(v)
+    return s * (1.0 + v * (1.0 - s))
+
+
+class Place:
+    def __init__(self, lines):
+        self.lines = lines
+        self.dp = lax.axis_index("dp")
+        blk = lax.axis_index("blk")
+        self.blk = blk
+        self.c = self.dp % 2
+        self.g = blk // 4
+        self.p = blk % 4
+        self.b = self.p // 2
+        self.a = self.p % 2
+        self.na = 1 - self.a
+        self.nb = 1 - self.b
+
+    def sib(self):
+        return (self.dp + 1 - 2 * self.c, self.blk)
+
+    def at(self, g, b, a):
+        return (self.dp, g * 4 + b * 2 + a)
+
+    def line(self, k):
+        return (self.g + k) % self.lines
+
+    def plane(self, k):
+        return (self.p + k) % 4
+
+    def pick(self, first, second):
+        return first + self.c * (second - first)
+
+
+def vec(ref, off, width):
+    parts = []
+    while width > 0:
+        row, lane = off // D, off % D
+        take = min(width, D - lane)
+        parts.append(ref[row : row + 1, lane : lane + take])
+        off, width = off + take, width - take
+    return parts[0] if len(parts) == 1 else jnp.concatenate(parts, axis=1)
+
+
+def greet(me, others):
+    bar = pltpu.get_barrier_semaphore()
+    for dev in others:
+        pl.semaphore_signal(bar, inc=1, device_id=dev, device_id_type=MESH)
+    pl.semaphore_wait(bar, len(others))
+
+
+def close_peers(me):
+    out = [me.sib()]
+    for k in range(1, me.lines):
+        out.append(me.at(me.line(k), me.b, me.a))
+    for k in range(1, 4):
+        q = me.plane(k)
+        out.append(me.at(me.g, q // 2, q % 2))
+    return out
+
+
+def rcopy(src, dst, ssem, rsem, dev):
+    return pltpu.make_async_remote_copy(
+        src_ref=src, dst_ref=dst, send_sem=ssem, recv_sem=rsem, device_id=dev, device_id_type=MESH
+    )
+
+
+class Gather:
+    def __init__(self, me, W, ssem, rsem):
+        self.me, self.W, self.ssem, self.rsem = me, W, ssem, rsem
+        self.half = W.shape[-1] // 2
+        self.G = me.lines
+        self.started = []
+
+    def cols(self, c):
+        return pl.ds(pl.multiple_of(c * self.half, 128), self.half)
+
+    def one(self, g, b, a, c):
+        return self.W.at[g, b, a, :, self.cols(c)]
+
+    def many(self, b, a, c):
+        return self.W.at[:, b, a, :, self.cols(c)]
+
+    def go(self, src, slot, dev):
+        cp = rcopy(src, src, self.ssem.at[slot], self.rsem.at[slot], dev)
+        cp.start()
+        self.started.append(cp)
+
+    def await_in(self, ref, slot):
+        rcopy(ref, ref, self.ssem.at[slot], self.rsem.at[slot], self.me.sib()).wait_recv()
+
+    def z(self):
+        me = self.me
+        for k in range(1, self.G):
+            self.go(self.one(me.g, me.b, me.a, me.c), k, me.at(me.line(k), me.b, me.a))
+
+    def first(self):
+        me, G = self.me, self.G
+        for k in range(1, G):
+            self.await_in(self.one((me.g + G - k) % G, me.b, me.a, me.c), k)
+        own = self.many(me.b, me.a, me.c)
+        self.go(own, G, me.at(me.g, me.b, me.na))
+        self.go(own, G + 1, me.at(me.g, me.nb, me.a))
+        self.go(own, G + 3, me.sib())
+
+    def second(self):
+        me, G = self.me, self.G
+        x = self.many(me.b, me.na, me.c)
+        y = self.many(me.nb, me.a, me.c)
+        self.await_in(x, G)
+        self.await_in(y, G + 1)
+        fwd = self.many(me.pick(me.b, me.nb), me.pick(me.na, me.a), me.c)
+        self.go(fwd, G + 2, me.at(me.g, me.pick(me.nb, me.b), me.pick(me.a, me.na)))
+        self.go(x, G + 4, me.sib())
+        self.go(y, G + 5, me.sib())
+
+    def third(self):
+        me, G = self.me, self.G
+        d = self.many(me.nb, me.na, me.c)
+        self.await_in(d, G + 2)
+        self.go(d, G + 6, me.sib())
+
+    def done(self):
+        me, G = self.me, self.G
+        o = 1 - me.c
+        self.await_in(self.many(me.b, me.a, o), G + 3)
+        self.await_in(self.many(me.b, me.na, o), G + 4)
+        self.await_in(self.many(me.nb, me.a, o), G + 5)
+        self.await_in(self.many(me.nb, me.na, o), G + 6)
+
+    def drain(self):
+        for cp in self.started:
+            cp.wait_send()
+
+
+def gather_slots(G):
+    return G + 7
+
+
+def decays_of(avg_ref):
+    damp = sigmoid(avg_ref[0])
+    mix = sigmoid(avg_ref[1])
+    dec = 1.0 - damp * mix
+    return damp, mix, dec, damp * avg_ref[2], avg_ref[3] * NH ** (-0.5)
+
+
+def power(v, n):
+    while n > 1:
+        v = v * v
+        n = n // 2
+    return v
+
+
+def ma_pass(x_ref, h, dec, inf, outf, pre_ref, keep=None):
+    def step(i, h):
+        if keep is not None:
+            keep[i] = h
+        xs = x_ref[pl.ds(i * 8, 8), :]
+        rows = []
+        for r in range(8):
+            h = dec * h + inf * xs[r : r + 1]
+            if pre_ref is not None:
+                rows.append(jnp.sum(outf * h, axis=0, keepdims=True))
+        if pre_ref is not None:
+            pre_ref[pl.ds(i * 8, 8), :] = jnp.concatenate(rows, axis=0)
+        return h
+
+    return lax.fori_loop(0, x_ref.shape[0] // 8, step, h)
+
+
+def toeplitz_block(bias_ref, m):
+    w = jnp.concatenate([bias_ref[pl.ds(m, 1), :], bias_ref[pl.ds(m + 1, 1), :]], axis=1)
+    return pltpu.roll(jnp.broadcast_to(w, (128, 256)), 1, 1, stride=1, stride_axis=0)[:, 128:]
+
+
+def as_rows(col):
+    return jnp.broadcast_to(col, (128, 128)).T[0:8]
+
+
+def as_col(rows):
+    return jnp.broadcast_to(rows[0:1], (128, 128)).T[:, 0:1]
+
+
+def fwd_kernel(
+    G, rows,
+    x_ref, wid_ref, mix_ref, nar_ref, avg_ref, vec_ref, bias_ref,
+    w0_o, mx_o, n0_o, w1_o, n1_o, mixed_o, pre_o, ent_o, att_o, lse_o, s_o, q_o, k_o, v_o, vp_o, xb_o,
+    w0, mx, n0, w1, n1, mxc, fin, ftot, ob, oin, lout, lin, xb, qb, kb, brow,
+    agss, agrs, xss, xrs, fss, frs, qss, qrs, oss, ors, outs,
+):
+    me = Place(G)
+    T = x_ref.shape[0]
+    rm, rw, rn = rows
+    own = {"g": me.g, "b": me.b, "a": me.a}
+    w0[me.g, me.b, me.a] = wid_ref[0].astype(BF)
+    w1[me.g, me.b, me.a] = wid_ref[1].astype(BF)
+    mx[me.g, me.b, me.a] = mix_ref[...].astype(BF)
+    n0[me.g, me.b, me.a] = nar_ref[0].astype(BF)
+    n1[me.g, me.b, me.a] = nar_ref[1].astype(BF)
+    xb[me.g] = x_ref[...].astype(BF)
+    greet(me, close_peers(me))
+    ga = [Gather(me, W, agss.at[i], agrs.at[i]) for i, W in enumerate((w0, mx, n0, w1, n1))]
+    gw0, gmx, gn0, gw1, gn1 = ga
+    sent = []
+
+    def go(src, dst, ss, rs, dev):
+        cp = rcopy(src, dst, ss, rs, dev)
+        cp.start()
+        sent.append(cp)
+
+    def got(ref, ss, rs):
+        rcopy(ref, ref, ss, rs, me.sib()).wait_recv()
+
+    def line_send(ref_at, ss, rs):
+        for k in range(1, G):
+            go(ref_at(me.g), ref_at(me.g), ss.at[k], rs.at[k], me.at(me.line(k), me.b, me.a))
+
+    def line_got(ref_at, ss, rs):
+        for k in range(1, G):
+            got(ref_at((me.g + G - k) % G), ss.at[k], rs.at[k])
+
+    def plane_send(ref_at, ss, rs):
+        for k in range(1, 4):
+            q = me.plane(k)
+            go(ref_at(me.p), ref_at(me.p), ss.at[k], rs.at[k], me.at(me.g, q // 2, q % 2))
+
+    def plane_got(ref_at, ss, rs):
+        for k in range(1, 4):
+            got(ref_at((me.p + 4 - k) % 4), ss.at[k], rs.at[k])
+
+    gw0.z()
+    line_send(lambda i: xb.at[i], xss, xrs)
+    gmx.z()
+    damp, mix, dec, inf, outf = decays_of(avg_ref)
+    zero = jnp.zeros((NH, D), F32)
+    fin[me.p] = ma_pass(x_ref, zero, dec, inf, outf, None)
+    plane_send(lambda i: fin.at[i], fss.at[0], frs.at[0])
+    gn0.z()
+    gw0.first()
+    plane_got(lambda i: fin.at[i], fss.at[0], frs.at[0])
+    whole = power(dec, T)
+    tot = fin[0]
+    for q in range(1, 4):
+        tot = whole * tot + fin[q]
+    ftot[me.g] = tot
+    line_send(lambda i: ftot.at[i], fss.at[1], frs.at[1])
+    gmx.first()
+    gw0.second()
+    gw1.z()
+    line_got(lambda i: ftot.at[i], fss.at[1], frs.at[1])
+    ent = zero
+    whole4 = power(whole, 4)
+    for i in range(G - 1):
+        ent = jnp.where(i < me.g, whole4 * ent + ftot[i], ent)
+    for q in range(3):
+        ent = jnp.where(q < me.p, whole * ent + fin[q], ent)
+    gn1.z()
+    ma_pass(x_ref, ent, dec, inf, outf, pre_o, ent_o)
+    pre = pre_o[...] + vec(vec_ref, OFF_OM, D) * x_ref[...]
+    pre_o[...] = pre
+    gn0.first()
+    gw0.third()
+    gmx.second()
+    gw0.done()
+    line_got(lambda i: xb.at[i], xss, xrs)
+    step = max(1, G // 2)
+    wide = step * 4 * rw
+    for i in range(G // step):
+        wblk = w0[i * step : (i + 1) * step].reshape(wide, D)
+        for gg in range(G):
+            vp = dot(xb[gg], wblk, NT) + vec(vec_ref, OFF_V + i * wide, wide)
+            vp_o[gg * T : (gg + 1) * T, i * wide : (i + 1) * wide] = silu_grad(vp).astype(BF)
+            v_o[gg * T : (gg + 1) * T, i * wide : (i + 1) * wide] = silu(vp).astype(BF)
+    gw1.first()
+    gn0.second()
+    gmx.third()
+    gmx.done()
+    cols = MX // (4 * G)
+    for i in range(4 * G):
+        mxc[i * cols : (i + 1) * cols] = mx[i // 4, (i // 2) % 2, i % 2, :cols]
+    prime = silu(pre_o[...]).astype(BF)
+    for i in range(5):
+        w = MX // 5
+        mixed_o[:, i * w : (i + 1) * w] = (
+            dot(prime, mxc[i * w : (i + 1) * w], NT) + vec(vec_ref, OFF_MX + i * w, w)
+        )
+    shared = silu(mixed_o[:, D : D + ZD])
+    scaling = ZD ** (-0.5)
+    qb[me.p] = (
+        (shared * vec(vec_ref, OFF_QG, ZD) + vec(vec_ref, OFF_QS, ZD)) * scaling
+    ).astype(BF)
+    kb[me.g] = (
+        shared * vec(vec_ref, OFF_QG + ZD, ZD) + vec(vec_ref, OFF_QS + ZD, ZD)
+    ).astype(BF)
+    plane_send(lambda i: qb.at[i], qss.at[0], qrs.at[0])
+    line_send(lambda i: kb.at[i], qss.at[1], qrs.at[1])
+    gn1.first()
+    gw1.second()
+    gn0.third()
+    plane_got(lambda i: qb.at[i], qss.at[0], qrs.at[0])
+    line_got(lambda i: kb.at[i], qss.at[1], qrs.at[1])
+    first_row = me.p - 4 * me.g - 4 + 4 * G
+    table = jnp.broadcast_to(vec(vec_ref, OFF_TB, NB), (128, NB)).T
+    for r in range(4 * G + 1):
+        hit = bias_ref[pl.ds(first_row + r, 1), :] == lax.broadcasted_iota(jnp.int32, (NB, 128), 0)
+        brow[r : r + 1] = jnp.sum(jnp.where(hit, table, 0.0), axis=0, keepdims=True)
+    kall = kb[...].reshape(G * T, ZD)
+    for kk in range(1, 4):
+        i = (me.p + kk) % 4
+        attend_block(G, T, me, i, qb, kall, v_o, brow, s_o, ob, lout, None)
+        go(ob.at[i], oin.at[me.p], oss.at[kk], ors.at[kk], me.at(me.g, i // 2, i % 2))
+        go(lout.at[i], lin.at[me.p], oss.at[4 + kk], ors.at[4 + kk], me.at(me.g, i // 2, i % 2))
+    gn1.second()
+    gw1.third()
+    attend_block(G, T, me, me.p, qb, kall, v_o, brow, s_o, ob, lout, att_o)
+    lin[me.p] = lout[me.p]
+    gn0.done()
+    gn1.third()
+    for k in range(1, 4):
+        got(oin.at[(me.p + 4 - k) % 4], oss.at[k], ors.at[k])
+        got(lin.at[(me.p + 4 - k) % 4], oss.at[4 + k], ors.at[4 + k])
+    ls = [as_col(lin[j]) for j in range(4)]
+    peak = functools.reduce(jnp.maximum, ls)
+    lse = peak + jnp.log(functools.reduce(jnp.add, [jnp.exp(l - peak) for l in ls]))
+    mine = as_col(lout[me.p])
+    att_o[...] = att_o[...] * jnp.exp(mine - lse)
+    for k in range(1, 4):
+        j = (me.p + k) % 4
+        wj = jnp.exp(as_col(lin[j]) - lse)
+        att_o[...] += oin[j].astype(F32) * wj
+    lse_o[...] = as_rows(lse)
+    xb_o[...] = xb[...]
+    q_o[...] = qb[...]
+    k_o[...] = kb[...]
+    gw1.done()
+    gn1.done()
+    for ga_ in ga:
+        ga_.drain()
+    for cp in sent:
+        cp.wait_send()
+    pairs = [(w0, w0_o), (mxc, mx_o), (n0, n0_o), (w1, w1_o), (n1, n1_o)]
+    cps = [pltpu.make_async_copy(s, d, outs.at[i]) for i, (s, d) in enumerate(pairs)]
+    for cp in cps:
+        cp.start()
+    for cp in cps:
+        cp.wait()
+
+
+def attend_block(G, T, me, i, q_o, kall, v_o, brow, s_o, ob, lout, att_o):
+    s = dot(q_o[i], kall, NT)
+    tops = []
+    for kk in range(G):
+        m = 4 * kk - i + 3
+        tops.append(toeplitz_block(brow, m))
+    s = s + jnp.concatenate(tops, axis=1)
+    s_o[i] = s
+    top = jnp.max(s, axis=1, keepdims=True)
+    e = jnp.exp(s - top)
+    tot = jnp.sum(e, axis=1, keepdims=True)
+    o = dot(e.astype(BF), v_o[...]) / tot
+    if att_o is None:
+        ob[i] = o.astype(BF)
+    else:
+        att_o[...] = o
+    lout[i] = as_rows(top + jnp.log(tot))
+
+
+def forward_call(G, x, wid, mix, nar, avg, vec, bias):
+    T = x.shape[0]
+    rm, rw, rn = mix.shape[0], wid.shape[1], nar.shape[1]
+    A = jax.ShapeDtypeStruct
+    slots = gather_slots(G)
+    out_shape = (
+        A((G, 2, 2, rw, D), BF), A((MX, D), BF), A((G, 2, 2, rn, VD), BF), A((G, 2, 2, rw, D), BF), A((G, 2, 2, rn, FF), BF),
+        A((T, MX), F32), A((T, D), F32), A((T // 8, NH, D), F32), A((T, VD), F32), A((8, 128), F32),
+        A((4, T, G * T), F32), A((4, T, ZD), BF), A((G, T, ZD), BF), A((G * T, VD), BF), A((G * T, VD), BF), A((G, T, D), BF),
+    )
+    vm = pl.BlockSpec(memory_space=pltpu.VMEM)
+    anys = pl.BlockSpec(memory_space=pl.ANY)
+    S = pltpu.SemaphoreType.DMA
+    return pl.pallas_call(
+        functools.partial(fwd_kernel, G, (rm, rw, rn)),
+        out_shape=out_shape,
+        in_specs=[vm] * 7,
+        out_specs=[anys] * 5 + [vm] * 11,
+        scratch_shapes=[
+            pltpu.VMEM((G, 2, 2, rw, D), BF), pltpu.VMEM((G, 2, 2, rm, D), BF), pltpu.VMEM((G, 2, 2, rn, VD), BF),
+            pltpu.VMEM((G, 2, 2, rw, D), BF), pltpu.VMEM((G, 2, 2, rn, FF), BF), pltpu.VMEM((MX, D), BF),
+            pltpu.VMEM((4, NH, D), F32), pltpu.VMEM((G, NH, D), F32),
+            pltpu.VMEM((4, T, VD), BF), pltpu.VMEM((4, T, VD), BF), pltpu.VMEM((4, 8, 128), F32), pltpu.VMEM((4, 8, 128), F32),
+            pltpu.VMEM((G, T, D), BF), pltpu.VMEM((4, T, ZD), BF), pltpu.VMEM((G, T, ZD), BF), pltpu.VMEM((4 * G + 8, 128), F32),
+            S((5, slots)), S((5, slots)), S((G,)), S((G,)), S((2, max(4, G))), S((2, max(4, G))), S((2, max(4, G))), S((2, max(4, G))), S((8,)), S((8,)),
+            S((5,)),
+        ],
+        compiler_params=pltpu.CompilerParams(collective_id=1, has_side_effects=True, vmem_limit_bytes=60 * 2**20),
+    )(x, wid, mix, nar, avg, vec, bias)
+
+
+def padded(v, axis):
+    extra = -v.shape[axis] % 16
+    if extra == 0:
+        return v
+    pads = [(0, 0)] * v.ndim
+    pads[axis] = (0, extra)
+    return jnp.pad(v, pads)
+
+
+class Link:
+    def __init__(self, me, ssem, rsem):
+        self.me, self.ssem, self.rsem = me, ssem, rsem
+        self.used = 0
+        self.started = []
+
+    def slot(self):
+        self.used += 1
+        return self.used - 1
+
+    def go(self, src, dst, slot, dev):
+        cp = rcopy(src, dst, self.ssem.at[slot], self.rsem.at[slot], dev)
+        cp.start()
+        self.started.append(cp)
+
+    def got(self, ref, slot):
+        rcopy(ref, ref, self.ssem.at[slot], self.rsem.at[slot], self.me.sib()).wait_recv()
+
+    def drain(self):
+        for cp in self.started:
+            cp.wait_send()
+
+    def swap(self, src, dst):
+        s = self.slot()
+        self.go(src, dst, s, self.me.sib())
+        return lambda: self.got(dst, s)
+
+    def plane(self, src, dst):
+        me = self.me
+        slots = [self.slot() for _ in range(3)]
+        for k in range(1, 4):
+            q = (me.p + k) % 4
+            self.go(src(q), dst(me.p), slots[k - 1], me.at(me.g, q // 2, q % 2))
+
+        def wait():
+            for k in range(1, 4):
+                self.got(dst((me.p + 4 - k) % 4), slots[k - 1])
+
+        return wait
+
+    def line(self, src, dst):
+        me, G = self.me, self.me.lines
+        slots = [self.slot() for _ in range(G - 1)]
+        for k in range(1, G):
+            h = (me.g + k) % G
+            self.go(src(h), dst(me.g), slots[k - 1], me.at(h, me.b, me.a))
+
+        def wait():
+            for k in range(1, G):
+                self.got(dst((me.g + G - k) % G), slots[k - 1])
+
+        return wait
+
+    def pairs(self, src, dst, count):
+        me = self.me
+        slots = [self.slot() for _ in range(count - 1)]
+        for k in range(1, count):
+            d = (me.dp // 2 + k) % count
+            self.go(src, dst(me.dp // 2), slots[k - 1], (2 * d + me.c, me.blk))
+
+        def wait():
+            for k in range(1, count):
+                self.got(dst((me.dp // 2 + count - k) % count), slots[k - 1])
+
+        return wait
+
+
+class Reduce:
+    def __init__(self, me, link, H, R, RL):
+        self.me, self.link, self.H, self.R, self.RL = me, link, H, R, RL
+        self.slots = [link.slot() for _ in range(3)]
+
+    def bundle(self, b, a):
+        return self.H.at[:, b, a]
+
+    def first(self):
+        me = self.me
+        b, a = me.pick(me.nb, me.b), me.pick(me.a, me.na)
+        dev = me.at(me.g, b, a)
+        self.link.go(self.bundle(me.nb, me.na), self.R.at[0], self.slots[0], dev)
+        self.link.go(self.bundle(b, a), self.R.at[1], self.slots[1], dev)
+
+    def second(self):
+        me, H = self.me, self.H
+        self.link.got(self.R.at[0], self.slots[0])
+        b, a = me.pick(me.b, me.nb), me.pick(me.na, me.a)
+        for g in range(me.lines):
+            H[g, b, a] = (H[g, b, a].astype(F32) + self.R[0, g].astype(F32)).astype(BF)
+        self.link.go(self.bundle(b, a), self.R.at[2], self.slots[2], me.at(me.g, b, a))
+
+    def third(self):
+        me, H, R = self.me, self.H, self.R
+        self.link.got(R.at[1], self.slots[1])
+        self.link.got(R.at[2], self.slots[2])
+        for g in range(me.lines):
+            H[g, me.b, me.a] = (
+                H[g, me.b, me.a].astype(F32) + R[1, g].astype(F32) + R[2, g].astype(F32)
+            ).astype(BF)
+        self.wait = self.link.line(lambda h: H.at[h, me.b, me.a], lambda h: self.RL.at[h])
+
+    def fourth(self):
+        me = self.me
+        self.wait()
+        self.RL[me.g] = self.H[me.g, me.b, me.a]
+        total = self.RL[0].astype(F32)
+        for g in range(1, me.lines):
+            total = total + self.RL[g].astype(F32)
+        return total
+
+
+def into_blocks(H, value, first, rows):
+    n = 4 * H.shape[0]
+    count = value.shape[0]
+    value = value.astype(BF)
+    if H.shape[3] == rows and first == 0 and count == n * rows:
+        H[...] = value.reshape(H.shape)
+        return
+    for i in range(n):
+        lo, hi = max(first, i * rows), min(first + count, (i + 1) * rows)
+        if lo < hi:
+            H[i // 4, (i // 2) % 2, i % 2, lo - i * rows : hi - i * rows] = value[lo - first : hi - first]
+
+
+def norm(v):
+    centered = v - jnp.mean(v, axis=-1, keepdims=True)
+    inverse = lax.rsqrt(jnp.mean(centered * centered, axis=-1, keepdims=True) + EPS_NORM)
+    return centered * inverse, inverse
+
+
+def norm_back(incoming, normed, inverse, gain):
+    scaled = incoming * gain
+    return inverse * (
+        scaled
+        - jnp.mean(scaled, axis=-1, keepdims=True)
+        - normed * jnp.mean(scaled * normed, axis=-1, keepdims=True)
+    )
+
+
+def down(v):
+    return jnp.sum(v.astype(F32), axis=0, keepdims=True)
+
+
+def put(ref, off, row):
+    width, at = row.shape[1], 0
+    while at < width:
+        r, lane = (off + at) // D, (off + at) % D
+        take = min(width - at, D - lane)
+        ref[r : r + 1, lane : lane + take] = row[:, at : at + take]
+        at += take
+
+
+def bwd_kernel(
+    G, count, sizes,
+    x_ref, cot_ref, w0_h, mx_h, n0_h, w1_h, n1_h, mixed_ref, pre_ref, keep_ref, att_ref, lse_ref,
+    s_ref, q_ref, k_ref, v_ref, vp_h, xb_ref, avg_ref, vec_ref, index_ref,
+    block_o, tok_o, gm_o, gw_o, gn_o, sum_o, ma_o,
+    GD, EX, GU, LL, GH, GT, GV, XB, GM, PB, full, W0, WM, HM, WN0, W1, WN1, R0, RM, RN0, R1, RN1, L0, LM, LN0, L1, LN1,
+    F0, FM, FN0, F1, FN1, GA, ST, P16, GS, QP, KS, KP, DX, DP, BP, fin, ftot, pairbuf,
+    AV, AS, AW, AT, AP, AL, prof, PA, P0, PM, PN0, P1, PN1, ssem, rsem, lsem,
+):
+    me = Place(G)
+    T = x_ref.shape[0]
+    loads = {}
+    for i, (name, src, dst) in enumerate(
+        (("n0", n0_h, WN0), ("w1", w1_h, W1), ("n1", n1_h, WN1), ("sgv", vp_h, GV.at[0]), ("w0", w0_h, W0), ("mx", mx_h, WM))
+    ):
+        loads[name] = pltpu.make_async_copy(src, dst, lsem.at[i])
+        loads[name].start()
+    link = Link(me, ssem, rsem)
+    others = close_peers(me)
+    for k in range(1, count):
+        others.append((2 * ((me.dp // 2 + k) % count) + me.c, me.blk))
+    greet(me, others)
+    o = 1 - me.c
+
+    def cols(c, half):
+        return pl.ds(pl.multiple_of(c * half, 128), half)
+
+    def share_half(ref, own, dst):
+        half = dst.shape[-1]
+        idx = (slice(None),) * (len(own.shape) - 1)
+        dst[0] = own[idx + (cols(me.c, half),)]
+        return link.swap(own.at[idx + (cols(o, half),)], dst.at[1])
+
+    AV[...] = jnp.zeros_like(AV)
+    H0, HN0, H1, HN1 = (W.at[:, :, :, :, 0 : W.shape[-1] // 2] for W in (W0, WN0, W1, WN1))
+
+    def flat(W):
+        return W[...].reshape(4 * G * W.shape[3], W.shape[4])
+
+    for i in range(4 * G):
+        extra = HM.shape[3] - MX // (4 * G)
+        if extra:
+            HM[i // 4, (i // 2) % 2, i % 2, MX // (4 * G) :] = jnp.zeros((extra, HM.shape[4]), BF)
+    got_xb = share_half(None, xb_ref, XB)
+    full[1, :, :D] = silu(pre_ref[...]).astype(BF)
+    PB[0] = full[1, :, cols(me.c, D // 2)]
+    got_pb = link.swap(full.at[1, :, cols(o, D // 2)], PB.at[1])
+
+    x = x_ref[...]
+    mixed = lambda off, w: mixed_ref[:, off : off + w]
+    reset = silu(mixed(D + ZD, VD))
+    full[0] = (reset * att_ref[...]).astype(BF)
+    GT[0] = full[0, :, cols(me.c, VD // 2)]
+    got_gt = link.swap(full.at[0, :, cols(o, VD // 2)], GT.at[1])
+    loads["n0"].wait()
+    hidden_pre = mixed(D + ZD + VD, D) + dot(full[0], flat(WN0), NT) + vec(vec_ref, OFF_H, D)
+    upd = sigmoid(mixed(0, D))
+    act = silu(hidden_pre)
+    one = x + upd * (act - x)
+    gain_one = vec(vec_ref, OFF_G1, D)
+    gain_two = vec(vec_ref, OFF_G2, D)
+    n_one, r_one = norm(one)
+    layer = n_one * gain_one + vec(vec_ref, OFF_S1, D)
+    full[2, :, :D] = layer.astype(BF)
+    LL[0] = full[2, :, cols(me.c, D // 2)]
+    got_ll = link.swap(full.at[2, :, cols(o, D // 2)], LL.at[1])
+    loads["w1"].wait()
+    expand_pre = dot(full[2, :, :D], flat(W1), NT) + vec(vec_ref, OFF_UP, FF)
+    full[3] = silu(expand_pre).astype(BF)
+    EX[0] = full[3, :, cols(me.c, FF // 2)]
+    got_ex = link.swap(full.at[3, :, cols(o, FF // 2)], EX.at[1])
+    loads["n1"].wait()
+    two = layer + dot(full[3], flat(WN1), NT) + vec(vec_ref, OFF_DOWN, D)
+    n_two, r_two = norm(two)
+    block_o[...] = n_two * gain_two + vec(vec_ref, OFF_S2, D)
+    cot = cot_ref[...]
+    back_two = norm_back(cot, n_two, r_two, gain_two)
+    put(AV, OFF_G2, down(cot * n_two))
+    put(AV, OFF_S2, down(cot))
+    GD[0] = back_two.astype(BF)
+    got_gd = link.swap(GD.at[0], GD.at[1])
+    put(AV, OFF_DOWN, down(GD[0]))
+    GU[0] = (dot(GD[0], flat(WN1)) * silu_grad(expand_pre)).astype(BF)
+    got_gu = link.swap(GU.at[0], GU.at[1])
+    put(AV, OFF_UP, down(GU[0]))
+    into_one = back_two + dot(GU[0], flat(W1))
+    put(AV, OFF_G1, down(into_one * n_one))
+    put(AV, OFF_S1, down(into_one))
+    back_one = norm_back(into_one, n_one, r_one, gain_one)
+    GH[0] = (back_one * upd * silu_grad(hidden_pre)).astype(BF)
+    got_gh = link.swap(GH.at[0], GH.at[1])
+    put(AV, OFF_H, down(GH[0]))
+    back_gated = dot(GH[0], flat(WN0))
+    GA[me.p] = (back_gated * reset).astype(BF)
+    inner = jnp.sum(GA[me.p].astype(F32) * att_ref[...], axis=1, keepdims=True)
+    ST[me.p, 0] = lse_ref[...]
+    ST[me.p, 1] = as_rows(inner)
+    got_ga = link.plane(lambda q: GA.at[me.p], lambda q: GA.at[q])
+    got_st = link.plane(lambda q: ST.at[me.p], lambda q: ST.at[q])
+    GM[0, :, 0:D] = (back_one * (act - x) * upd * (1.0 - upd)).astype(BF)
+    GM[0, :, D + ZD : D + ZD + VD] = (
+        back_gated * att_ref[...] * silu_grad(mixed(D + ZD, VD))
+    ).astype(BF)
+    GM[0, :, D + ZD + VD :] = GH[0]
+    tok_o[...] = back_one * (1.0 - upd)
+    red = [
+        Reduce(me, link, H, R, L)
+        for H, R, L in ((HN1, RN1, LN1), (H1, R1, L1), (HN0, RN0, LN0), (H0, R0, L0), (HM, RM, LM))
+    ]
+    rn1, r1, rn0, r0, rmx = red
+
+    def both(ref):
+        return ref[...].reshape(2 * T, ref.shape[-1])
+
+    def grads(H, out, into):
+        rhs = both(into)
+        for j in range(0, out.shape[-1], 384):
+            lhs = out[:, :, j : j + 384].reshape(2 * T, 384)
+            into_blocks(H, dot(lhs, rhs, TN), j, out.shape[-1] // (4 * G))
+
+    got_gd()
+    got_ex()
+    grads(HN1, GD, EX)
+    rn1.first()
+    got_gu()
+    got_ll()
+    grads(H1, GU, LL)
+    r1.first()
+    got_gh()
+    got_gt()
+    grads(HN0, GH, GT)
+    rn1.second()
+    rn0.first()
+    got_ga()
+    got_st()
+    kall = k_ref[...].reshape(G * T, ZD)
+    for kk in (1, 2, 3, 0):
+        i = (me.p + kk) % 4
+        probs = jnp.exp(s_ref[i] - as_col(ST[i, 0]))
+        back = dot(GA[i], v_ref[...], NT)
+        gs = (probs * (back - as_col(ST[i, 1]))).astype(BF)
+        P16[i] = probs.astype(BF)
+        GS[i] = gs
+        QP[i] = dot(gs, kall)
+    got_q = link.plane(lambda q: QP.at[q], lambda q: KS.at[q])
+    r1.second()
+    rn1.third()
+    gsall = GS[...].reshape(4 * T, G * T)
+    KP[...] = dot(gsall, q_ref[...].reshape(4 * T, ZD), TN).reshape(G, T, ZD)
+    got_k = link.line(lambda h: KP.at[h], lambda h: DP.at[h])
+    pall = P16[...].reshape(4 * T, G * T)
+    gall = GA[...].reshape(4 * T, VD)
+    loads["sgv"].wait()
+    wide = 512
+    for j in range(VD // wide):
+        sl = slice(j * wide, (j + 1) * wide)
+        dv = dot(pall, gall[:, sl], TN)
+        gv = (dv * GV[0, :, sl].astype(F32)).astype(BF)
+        GV[0, :, sl] = gv
+        put(AV, OFF_V + j * wide, down(gv))
+    got_gv = link.swap(GV.at[0], GV.at[1])
+    rn0.second()
+    loads["w0"].wait()
+    for g in range(G):
+        DX[g] = dot(GV[0, g * T : (g + 1) * T], flat(W0)).astype(BF)
+    got_dx = link.line(lambda h: DX.at[h], lambda h: BP.at[h])
+    r1.third()
+    got_gv()
+    got_xb()
+    xball = XB[...].reshape(2 * G * T, D // 2)
+    wide = VD // 4
+    for j in range(4):
+        gvall = GV[:, :, j * wide : (j + 1) * wide].reshape(2 * G * T, wide)
+        into_blocks(H0, dot(gvall, xball, TN), j * wide, VD // (4 * G))
+    r0.first()
+    rn0.third()
+    got_q()
+    KS[me.p] = QP[me.p]
+    DP[me.g] = KP[me.g]
+    scaling = ZD ** (-0.5)
+    back_q = (KS[0] + KS[1] + KS[2] + KS[3]) * scaling
+    got_k()
+    back_k = DP[0]
+    for g in range(1, G):
+        back_k = back_k + DP[g]
+    sp = mixed(D, ZD)
+    shared = silu(sp)
+    put(AV, OFF_QG, down(back_q * shared))
+    put(AV, OFF_QG + ZD, down(back_k * shared))
+    put(AV, OFF_QS, down(back_q))
+    put(AV, OFF_QS + ZD, down(back_k))
+    back_shared = back_q * vec(vec_ref, OFF_QG, ZD) + back_k * vec(vec_ref, OFF_QG + ZD, ZD)
+    GM[0, :, D : D + ZD] = (back_shared * silu_grad(sp)).astype(BF)
+    got_gm = link.swap(GM.at[0], GM.at[1])
+    put(AV, OFF_MX, down(GM[0]))
+    loads["mx"].wait()
+    back_pre = dot(GM[0], WM[...]) * silu_grad(pre_ref[...])
+    tok_o[...] += vec(vec_ref, OFF_OM, D) * back_pre
+    put(AV, OFF_OM, down(back_pre * x))
+    pre_buf = pairbuf
+    pre_buf[...] = back_pre
+    got_gm()
+    got_pb()
+    gmall = both(GM)
+    pball = both(PB)
+    step = MX // 5
+    for j in range(5):
+        into_blocks(
+            HM, dot(gmall[:, j * step : (j + 1) * step], pball, TN), j * step, MX // (4 * G)
+        )
+    rmx.first()
+    r0.second()
+    damp, mix, dec, inf, outf = decays_of(avg_ref)
+    zero = jnp.zeros((NH, D), F32)
+    fin[me.p] = ma_back_first(pre_buf, dec, outf, zero)
+    got_fin = link.plane(lambda q: fin.at[me.p], lambda q: fin.at[q])
+    diagonals(G, T, GS, prof)
+    got_fin()
+    whole = power(dec, T)
+    tot = fin[3]
+    for q in (2, 1, 0):
+        tot = whole * tot + fin[q]
+    ftot[me.g] = tot
+    got_tot = link.line(lambda h: ftot.at[me.g], lambda h: ftot.at[h])
+    rmx.second()
+    r0.third()
+    got_tot()
+    whole4 = power(whole, 4)
+    leave = zero
+    for i in range(G - 1, 0, -1):
+        leave = jnp.where(i > me.g, whole4 * leave + ftot[i], leave)
+    for q in (3, 2, 1):
+        leave = jnp.where(q > me.p, whole * leave + fin[q], leave)
+    ma_back(x_ref, pre_buf, keep_ref, leave, dec, inf, outf, tok_o, AV)
+    table_rows(G, me, prof, index_ref, AV)
+    rmx.third()
+    got_av = link.swap(AV, AS)
+    got_dx()
+    BP[me.g] = DX[me.g]
+    for g in range(G):
+        tok_o[...] += BP[g].astype(F32)
+    finish = []
+
+    def pair_sum(value, buf):
+        buf[me.dp // 2] = value
+        link.pairs(buf.at[me.dp // 2], lambda d: buf.at[d], count)()
+        value = buf[0]
+        for d in range(1, count):
+            value = value + buf[d]
+        return value
+
+    def close(r, F, buf):
+        total = r.fourth()
+        half = total.shape[-1]
+        if count > 1:
+            total = pair_sum(total, buf)
+        F[:, cols(me.c, half)] = total
+        part = F.at[:, cols(me.c, half)]
+        s = link.slot()
+        link.go(part, part, s, me.sib())
+        finish.append(lambda: link.got(F.at[:, cols(o, half)], s))
+
+    close(rn1, FN1, PN1)
+    close(r1, F1, P1)
+    close(rn0, FN0, PN0)
+    got_av()
+    AW[...] = AV[...] + AS[...]
+    hr = AV.shape[0] // 2
+    qr = hr // 4
+
+    def part(ref, q):
+        return ref.at[pl.ds(pl.multiple_of(me.c * hr + q * qr, 8), qr), :]
+
+    got_ap = link.plane(lambda q: part(AW, q), lambda q: AP.at[q])
+    close(r0, F0, P0)
+    got_ap()
+    AP[me.p] = AW[pl.ds(pl.multiple_of(me.c * hr + me.p * qr, 8), qr), :]
+    AL[me.g] = AP[0] + AP[1] + AP[2] + AP[3]
+    got_al = link.line(lambda h: AL.at[me.g], lambda h: AL.at[h])
+    close(rmx, FM, PM)
+    got_al()
+    tot = AL[0]
+    for g in range(1, G):
+        tot = tot + AL[g]
+    if count > 1:
+        tot = pair_sum(tot, PA)
+    AT[pl.ds(pl.multiple_of(me.c * hr + me.p * qr, 8), qr), :] = tot
+    got_as = link.plane(lambda q: part(AT, me.p), lambda q: part(AT, q))
+    got_as()
+    mine = AT.at[pl.ds(pl.multiple_of(me.c * hr, 8), hr), :]
+    theirs = AT.at[pl.ds(pl.multiple_of(o * hr, 8), hr), :]
+    s = link.slot()
+    link.go(mine, mine, s, me.sib())
+    link.got(theirs, s)
+    for f in finish:
+        f()
+    gm_o[...] = FM[...]
+    gw_o[0] = F0[...]
+    gw_o[1] = F1[...]
+    gn_o[0] = FN0[...]
+    gn_o[1] = FN1[...]
+    sum_o[...] = AT[0:16]
+    ma_o[...] = AT[16:64].reshape(3, NH, D)
+    link.drain()
+
+
+def ma_back_first(bp_ref, dec, outf, h):
+    n8 = bp_ref.shape[0] // 8
+
+    def step(i, h):
+        bs = bp_ref[pl.ds((n8 - 1 - i) * 8, 8), :]
+        for r in range(7, -1, -1):
+            h = dec * (outf * bs[r : r + 1] + h)
+        return h
+
+    return lax.fori_loop(0, n8, step, h)
+
+
+def ma_back(x_ref, bp_ref, keep_ref, leave, dec, inf, outf, tok_o, AV):
+    n8 = x_ref.shape[0] // 8
+    wide = 256
+    for j in range(D // wide):
+        sl = slice(j * wide, (j + 1) * wide)
+        d, f, u = dec[:, sl], inf[:, sl], outf[:, sl]
+
+        def step(i, carry):
+            h, dd, di, du = carry
+            at = n8 - 1 - i
+            xs = x_ref[pl.ds(at * 8, 8), sl]
+            bs = bp_ref[pl.ds(at * 8, 8), sl]
+            states = [keep_ref[at, :, sl]]
+            for r in range(8):
+                states.append(d * states[-1] + f * xs[r : r + 1])
+            rows = [None] * 8
+            for r in range(7, -1, -1):
+                adj = u * bs[r : r + 1] + h
+                dd = dd + adj * states[r]
+                di = di + adj * xs[r : r + 1]
+                du = du + bs[r : r + 1] * states[r + 1]
+                rows[r] = jnp.sum(f * adj, axis=0, keepdims=True)
+                h = d * adj
+            tok_o[pl.ds(at * 8, 8), sl] += jnp.concatenate(rows, axis=0)
+            return h, dd, di, du
+
+        zero = jnp.zeros((NH, wide), F32)
+        _, dd, di, du = lax.fori_loop(0, n8, step, (leave[:, sl], zero, zero, zero))
+        AV[16 : 16 + NH, sl] = dd
+        AV[16 + NH : 16 + 2 * NH, sl] = di
+        AV[16 + 2 * NH : 16 + 3 * NH, sl] = du
+
+
+def diagonals(G, T, GS, prof):
+    flip = (
+        lax.broadcasted_iota(jnp.int32, (T, T), 0) + lax.broadcasted_iota(jnp.int32, (T, T), 1) == T - 1
+    ).astype(F32).astype(BF)
+    for i in range(4):
+        turned = dot(flip, GS[i])
+        for kk in range(G):
+            m = 4 * kk - i + 3
+            block = jnp.concatenate([turned[:, kk * T : (kk + 1) * T], jnp.zeros((T, T), F32)], axis=1)
+            s = jnp.sum(pltpu.roll(block, 0, 1, stride=1, stride_axis=0), axis=0, keepdims=True)
+            prof[m : m + 1] += s[:, :T]
+            prof[m + 1 : m + 2] += s[:, T:]
+
+
+def table_rows(G, me, prof, index_ref, AV):
+    first_row = me.p - 4 * me.g - 4 + 4 * G
+    total = jnp.zeros((NB, 128), F32)
+    for r in range(4 * G + 1):
+        hit = index_ref[pl.ds(first_row + r, 1), :] == lax.broadcasted_iota(jnp.int32, (NB, 128), 0)
+        total = total + jnp.where(hit, prof[r : r + 1], 0.0)
+    col = jnp.sum(total, axis=1, keepdims=True)
+    put(AV, OFF_TB, as_rows(col)[0:1])
+
+
+def backward_call(G, count, sizes, x, cot, weights, saved, avg, vv, index):
+    T = x.shape[0]
+    rm, rw, rn = sizes
+    A = jax.ShapeDtypeStruct
+    V = pltpu.VMEM
+    half = D // 2
+    hv = VD // 2
+    vm = pl.BlockSpec(memory_space=pltpu.VMEM)
+    hbm = pl.BlockSpec(memory_space=pl.ANY)
+    S = pltpu.SemaphoreType.DMA
+    out_shape = (
+        A((T, D), F32), A((T, D), F32), A((rm, D), F32), A((2, rw, D), F32), A((2, rn, VD), F32),
+        A((16, D), F32), A((3, NH, D), F32),
+    )
+    scratch = [
+        V((2, T, D), BF), V((2, T, hv), BF), V((2, T, FF), BF), V((2, T, half), BF), V((2, T, D), BF), V((2, T, hv), BF),
+        V((2, G * T, VD), BF), V((2, G, T, half), BF), V((2, T, MX), BF), V((2, T, half), BF), V((4, T, VD), BF),
+        V((G, 2, 2, rw, D), BF), V((MX, D), BF), V((G, 2, 2, rm, half), BF), V((G, 2, 2, rn, VD), BF), V((G, 2, 2, rw, D), BF), V((G, 2, 2, rn, VD), BF),
+        V((3, G, rw, half), BF), V((3, G, rm, half), BF), V((3, G, rn, hv), BF), V((3, G, rw, half), BF), V((3, G, rn, hv), BF),
+        V((G, rw, half), BF), V((G, rm, half), BF), V((G, rn, hv), BF), V((G, rw, half), BF), V((G, rn, hv), BF),
+        V((rw, D), F32), V((rm, D), F32), V((rn, VD), F32), V((rw, D), F32), V((rn, VD), F32),
+        V((4, T, VD), BF), V((4, 2, 8, 128), F32), V((4, T, G * T), BF), V((4, T, G * T), BF),
+        V((4, T, ZD), F32), V((4, T, ZD), F32), V((G, T, ZD), F32), V((G, T, D), BF), V((G, T, ZD), F32), V((G, T, D), BF),
+        V((4, NH, D), F32), V((G, NH, D), F32), V((T, D), F32),
+        V((64, D), F32), V((64, D), F32), V((64, D), F32), V((64, D), F32), V((4, 8, D), F32), V((G, 8, D), F32), V((4 * G + 8, 128), F32),
+    ]
+    if count > 1:
+        scratch += [V((count, r, w), F32) for r, w in ((8, D), (rw, half), (rm, half), (rn, hv), (rw, half), (rn, hv))]
+    else:
+        scratch += [V((8, 128), F32)] * 6
+    slots = 80 + 6 * G + 6 * count
+    scratch += [S((slots,)), S((slots,)), S((6,))]
+    return pl.pallas_call(
+        functools.partial(bwd_kernel, G, count, sizes),
+        out_shape=out_shape,
+        in_specs=[vm] * 2 + [hbm] * 5 + [vm] * 9 + [hbm] + [vm] * 4,
+        out_specs=[vm] * 7,
+        scratch_shapes=scratch,
+        compiler_params=pltpu.CompilerParams(collective_id=2, has_side_effects=True, vmem_limit_bytes=58 * 2**20),
+    )(x, cot, *weights, *saved, avg, vv, index)
+
+
+def prologue(mixer_weight, widen_weight, narrow_weight, vectors, averager, bias_index):
+    n = lax.axis_size("blk")
+    mix = padded(mixer_weight.T, 0)
+    wid = padded(jnp.swapaxes(widen_weight, 1, 2), 1)
+    nar = padded(jnp.swapaxes(narrow_weight, 1, 2), 1)
+    avg = jnp.swapaxes(averager, 1, 2)
+    index = jnp.pad(bias_index, (0, 1)).reshape(2 * n, 128)
+    return mix, wid, nar, avg, vectors.reshape(NVEC // D, D), index
 
 
 def carried_in(part, axis, combine, identity, reverse):
@@ -51,11 +1072,6 @@
     return jnp.einsum(pattern, left_side, right_side, preferred_element_type=jnp.float32)
 
 
-def silu_grad(values):
-    logistic = jax.nn.sigmoid(values)
-    return logistic * (1.0 + values * (1.0 - logistic))
-
-
 def layer_norm(values, norm_gain, norm_shift):
     centered = values - jnp.mean(values, axis=-1, keepdims=True)
     inverse = lax.rsqrt(jnp.mean(centered * centered, axis=-1, keepdims=True) + EPS_NORM)
@@ -63,7 +1079,7 @@
     return (normed * norm_gain + norm_shift, normed, inverse)
 
 
-def norm_back(incoming, normed, inverse, norm_gain):
+def norm_back_sums(incoming, normed, inverse, norm_gain):
     scaled = incoming * norm_gain
     result = inverse * (
         scaled
@@ -117,7 +1133,7 @@
     return (weight - RATE * jnp.maximum(EPS_TWO, rms_weight) * update, moment_new)
 
 
-def on_device(
+def with_collectives(
     tokens,
     cotangent,
     mixer_weight,
@@ -229,7 +1245,7 @@
         jnp.dot(expand_low, narrow_low[1], preferred_element_type=jnp.float32) + bias_project
     )
     block_out, normed_two, inverse_two = layer_norm(layer_one + project_two, gain_two, shift_two)
-    grad_second, gain_two_grad, shift_two_grad = norm_back(
+    grad_second, gain_two_grad, shift_two_grad = norm_back_sums(
         cotangent[0], normed_two, inverse_two, gain_two
     )
     project_low = grad_second.astype(jnp.bfloat16)
@@ -239,7 +1255,7 @@
     ).astype(jnp.bfloat16)
     grad_up = product(layer_low, expand_grad_low, "td,tf->df")
     grad_layer = grad_second + product(expand_grad_low, widen_low[1], "tf,df->td")
-    grad_first, gain_one_grad, shift_one_grad = norm_back(
+    grad_first, gain_one_grad, shift_one_grad = norm_back_sums(
         grad_layer, normed_one, inverse_one, gain_one
     )
     grad_update = grad_first * (hidden_act - inputs)
@@ -433,48 +1449,272 @@
     )
 
 
+def matrices(G, gm_ref, gw_ref, gn_ref, wm_ref, ww_ref, wn_ref):
+    r0, r1, r2 = (t // (4 * G) for t in (MX, VD, D))
+    return [
+        (lambda: gm_ref[0:r0], lambda: wm_ref[0:r0], MX, D),
+        (lambda: gw_ref[0, 0:r1], lambda: ww_ref[0, 0:r1], VD, D),
+        (lambda: gw_ref[1, 0:r1], lambda: ww_ref[1, 0:r1], VD, D),
+        (lambda: gn_ref[0, 0:r2], lambda: wn_ref[0, 0:r2], D, VD),
+        (lambda: gn_ref[1, 0:r2], lambda: wn_ref[1, 0:r2], D, VD),
+    ]
+
+
+def raw_averager(avg, ma_ref):
+    damp = sigmoid(avg[0])
+    mix = sigmoid(avg[1])
+    d_dec, d_inf, d_out = ma_ref[0], ma_ref[1], ma_ref[2]
+    return [
+        (-mix * d_dec + avg[2] * d_inf) * damp * (1.0 - damp),
+        -damp * d_dec * mix * (1.0 - mix),
+        damp * d_inf,
+        d_out * NH ** (-0.5),
+    ]
+
+
+def stat_kernel(
+    G,
+    gm_ref, gw_ref, gn_ref, sum_ref, ma_ref, wm_ref, ww_ref, wn_ref, rm_ref, rw_ref, rn_ref, cm_ref, cw_ref, cn_ref, avg_ref,
+    rm_o, rw_o, rn_o, cm_o, cw_o, cn_o, scal_o,
+    rp, rl, up, ul, ssem, rsem,
+):
+    me = Place(G)
+    link = Link(me, ssem, rsem)
+    peers = []
+    for k in range(1, G):
+        peers.append(me.at(me.line(k), me.b, me.a))
+    for k in range(1, 4):
+        q = me.plane(k)
+        peers.append(me.at(me.g, q // 2, q % 2))
+    greet(me, peers)
+
+    def allsum(value, pb, lb):
+        pb[me.p] = value
+        link.plane(lambda q: pb.at[me.p], lambda q: pb.at[q])()
+        lb[me.g] = pb[0] + pb[1] + pb[2] + pb[3]
+        link.line(lambda h: lb.at[me.g], lambda h: lb.at[h])()
+        out = lb[0]
+        for g in range(1, G):
+            out = out + lb[g]
+        return out
+
+    rate = 1.0 - STEP ** (-0.8)
+    mats = matrices(G, gm_ref, gw_ref, gn_ref, wm_ref, ww_ref, wn_ref)
+    olds = [
+        (rm_ref[0:1], cm_ref[...].T), (rw_ref[0:1], cw_ref[0:1].T), (rw_ref[1:2], cw_ref[1:2].T),
+        (rn_ref[0:1], cn_ref[0:1].T), (rn_ref[1:2], cn_ref[1:2].T),
+    ]
+    lanes = lax.broadcasted_iota(jnp.int32, (1, D), 1)
+    rows, cs, extra = [], [], jnp.zeros((1, D), F32)
+    for i, (g, w, _, width) in enumerate(mats):
+        sq = g()
+        sq = sq * sq
+        s = jnp.sum(sq, axis=0, keepdims=True)
+        for j in range(width // D):
+            rows.append(s[:, j * D : (j + 1) * D])
+        cs.append(jnp.sum(sq, axis=1, keepdims=True))
+        wv = w()
+        extra = jnp.where(lanes == i, jnp.sum(wv * wv), extra)
+    rows.append(extra)
+    small = jnp.sum(sum_ref[...] * sum_ref[...])
+    for v in raw_averager([avg_ref[i] for i in range(4)], ma_ref):
+        small = small + jnp.sum(v * v)
+    tot = allsum(jnp.concatenate(rows, axis=0), rp, rl)
+    norm = jnp.sqrt(jnp.sum(tot[0:7]) + small)
+    factor = jnp.minimum(1.0, CLIP_NORM / norm)
+    at = 0
+    squares = jnp.zeros((1, 128), F32)
+    means = jnp.zeros((1, 128), F32)
+    lane = lanes[:, :128]
+    for i, (g, w, total, width) in enumerate(mats):
+        ro, co = olds[i]
+        row = jnp.concatenate([tot[at + j : at + j + 1] for j in range(width // D)], axis=1)
+        at += width // D
+        rnew = rate * ro + (1.0 - rate) * (factor * factor * row / total + EPS_ONE)
+        cnew = rate * co + (1.0 - rate) * (factor * factor * cs[i] / width + EPS_ONE)
+        mean = jnp.sum(rnew) / width
+        u = factor * g() * lax.rsqrt(rnew * cnew / mean)
+        squares = jnp.where(lane == i, jnp.sum(u * u), squares)
+        means = jnp.where(lane == i, mean, means)
+        ref, k = ((rm_o, 0), (rw_o, 0), (rw_o, 1), (rn_o, 0), (rn_o, 1))[i]
+        ref[k : k + 1] = rnew
+        ref, k = ((cm_o, 0), (cw_o, 0), (cw_o, 1), (cn_o, 0), (cn_o, 1))[i]
+        ref[k : k + 1] = cnew.T
+    sums = allsum(jnp.broadcast_to(squares, (8, 128)), up, ul)
+    scal_o[0:1] = sums[0:1]
+    scal_o[1:2] = tot[7:8, :128]
+    scal_o[2:3] = means
+    scal_o[3:4] = jnp.full((1, 128), norm, F32)
+    scal_o[4:5] = jnp.full((1, 128), factor, F32)
+    scal_o[5:8] = jnp.zeros((3, 128), F32)
+    link.drain()
+
+
+def step_kernel(
+    G,
+    gm_ref, gw_ref, gn_ref, sum_ref, ma_ref, wm_ref, ww_ref, wn_ref, rm_ref, rw_ref, rn_ref, cm_ref, cw_ref, cn_ref, scal_ref,
+    vec_ref, vmom_ref, avg_ref, amom_ref, block_ref, tok_ref,
+    gm_o, gw_o, gn_o, vg_o, ag_o, nm_o, nw_o, nn_o, nv_o, na_o, rm_o, cm_o, rw_o, cw_o, rn_o, cn_o, vmom_o, amom_o, clip_o,
+    block_o, tok_o,
+    s96, sems,
+):
+    cps = [pltpu.make_async_copy(block_ref, block_o, sems.at[0]), pltpu.make_async_copy(tok_ref, tok_o, sems.at[1])]
+    for cp in cps:
+        cp.start()
+    rate = 1.0 - STEP ** (-0.8)
+    lane = lax.broadcasted_iota(jnp.int32, (1, 128), 1)
+
+    def scalar(row, i):
+        return jnp.sum(jnp.where(lane == i, scal_ref[row : row + 1], 0.0))
+
+    factor = scalar(4, 0)
+    clip_o[...] = scal_ref[3:4, 0:1]
+    rm_o[...] = rm_ref[...]
+    rw_o[...] = rw_ref[...]
+    rn_o[...] = rn_ref[...]
+    cm_o[...] = cm_ref[...]
+    cw_o[...] = cw_ref[...]
+    cn_o[...] = cn_ref[...]
+    mats = matrices(G, gm_ref, gw_ref, gn_ref, wm_ref, ww_ref, wn_ref)
+    stats = [
+        (rm_ref[0:1], cm_ref[...].T, gm_o, nm_o, None), (rw_ref[0:1], cw_ref[0:1].T, gw_o, nw_o, 0),
+        (rw_ref[1:2], cw_ref[1:2].T, gw_o, nw_o, 1), (rn_ref[0:1], cn_ref[0:1].T, gn_o, nn_o, 0),
+        (rn_ref[1:2], cn_ref[1:2].T, gn_o, nn_o, 1),
+    ]
+    for i, (g, w, total, width) in enumerate(mats):
+        rnew, cnew, go, no, k = stats[i]
+        entries = total * width
+        rms_u = jnp.sqrt(scalar(0, i) / entries)
+        rms_w = jnp.sqrt(scalar(1, i) / entries)
+        scale = RATE * jnp.maximum(EPS_TWO, rms_w) / jnp.maximum(1.0, rms_u / CLIP_UPDATE)
+        gv = factor * g()
+        new = w() - scale * (gv * lax.rsqrt(rnew * cnew / scalar(2, i)))
+        if k is None:
+            go[...] = gv
+            no[...] = new
+        else:
+            go[k] = gv
+            no[k] = new
+    for r in range(16):
+        for j in range(D // 128):
+            s96[r * (D // 128) + j : r * (D // 128) + j + 1] = sum_ref[r : r + 1, j * 128 : (j + 1) * 128]
+    gv = factor * s96[...]
+    vg_o[...] = gv
+    mom = rate * vmom_ref[...] + (1.0 - rate) * (gv * gv + EPS_ONE)
+    vmom_o[...] = mom
+    u = gv * lax.rsqrt(mom)
+    rms_u = jnp.sqrt(jnp.sum(u * u) / NVEC)
+    wv = vec_ref[...]
+    rms_w = jnp.sqrt(jnp.sum(wv * wv) / NVEC)
+    nv_o[...] = wv - RATE * jnp.maximum(EPS_TWO, rms_w) * (u / jnp.maximum(1.0, rms_u / CLIP_UPDATE))
+    avg = [avg_ref[i] for i in range(4)]
+    raw = raw_averager(avg, ma_ref)
+    us, su, sw = [], 0.0, 0.0
+    for i in range(4):
+        gv = factor * raw[i]
+        ag_o[i] = gv
+        mom = rate * amom_ref[i] + (1.0 - rate) * (gv * gv + EPS_ONE)
+        amom_o[i] = mom
+        u = gv * lax.rsqrt(mom)
+        us.append(u)
+        su = su + jnp.sum(u * u)
+        sw = sw + jnp.sum(avg[i] * avg[i])
+    count = 4 * D * NH
+    scale = RATE * jnp.maximum(EPS_TWO, jnp.sqrt(sw / count)) / jnp.maximum(1.0, jnp.sqrt(su / count) / CLIP_UPDATE)
+    for i in range(4):
+        na_o[i] = avg[i] - scale * us[i]
+    for cp in cps:
+        cp.wait()
+
+
+def stat_call(G, grads, masters, rows, cols, avg):
+    A = jax.ShapeDtypeStruct
+    V = pltpu.VMEM
+    S = pltpu.SemaphoreType.DMA
+    vm = pl.BlockSpec(memory_space=pltpu.VMEM)
+    r0, r1, r2 = (t // (4 * G) for t in (MX, VD, D))
+    slots = 4 * (3 + G)
+    return pl.pallas_call(
+        functools.partial(stat_kernel, G),
+        out_shape=(
+            A((1, D), F32), A((2, D), F32), A((2, VD), F32), A((1, r0), F32), A((2, r1), F32), A((2, r2), F32), A((8, 128), F32),
+        ),
+        in_specs=[vm] * 15,
+        out_specs=[vm] * 7,
+        scratch_shapes=[
+            V((4, 8, D), F32), V((G, 8, D), F32), V((4, 8, 128), F32), V((G, 8, 128), F32), S((slots,)), S((slots,)),
+        ],
+        compiler_params=pltpu.CompilerParams(collective_id=3, has_side_effects=True, vmem_limit_bytes=56 * 2**20),
+    )(*grads, *masters, *rows, *cols, avg)
+
+
+def step_call(G, grads, masters, stats, vectors, vmom, avg, amom, block, tok):
+    A = jax.ShapeDtypeStruct
+    V = pltpu.VMEM
+    vm = pl.BlockSpec(memory_space=pltpu.VMEM)
+    hbm = pl.BlockSpec(memory_space=pl.ANY)
+    r0, r1, r2 = (t // (4 * G) for t in (MX, VD, D))
+    avgs, vecs = A((4, NH, D), F32), A((NVEC // 128, 128), F32)
+    out_shape = (
+        A((r0, D), F32), A((2, r1, D), F32), A((2, r2, VD), F32), vecs, avgs,
+        A((r0, D), F32), A((2, r1, D), F32), A((2, r2, VD), F32), vecs, avgs,
+        A((1, D), F32), A((1, r0), F32), A((2, D), F32), A((2, r1), F32), A((2, VD), F32), A((2, r2), F32),
+        vecs, avgs, A((1, 1), F32), A(block.shape, F32), A(tok.shape, F32),
+    )
+    return pl.pallas_call(
+        functools.partial(step_kernel, G),
+        out_shape=out_shape,
+        in_specs=[vm] * 19 + [hbm] * 2,
+        out_specs=[vm] * 19 + [hbm] * 2,
+        scratch_shapes=[V((NVEC // 128, 128), F32), pltpu.SemaphoreType.DMA((2,))],
+        compiler_params=pltpu.CompilerParams(vmem_limit_bytes=56 * 2**20),
+    )(*grads, *masters, *stats, vectors, vmom, avg, amom, block, tok)
+
+
+def on_device(
+    tokens, cotangent, mixer_weight, widen_weight, narrow_weight, vectors, averager, bias_index,
+    mixer_rows, mixer_cols, widen_rows, widen_cols, narrow_rows, narrow_cols, vector_moment, averager_moment,
+):
+    G = lax.axis_size("blk") // 4
+    count = lax.axis_size("dp") // 2
+    mix, wid, nar, avg, vv, index = prologue(
+        mixer_weight, widen_weight, narrow_weight, vectors, averager, bias_index
+    )
+    w0, mx, n0, w1, n1, *saved = forward_call(G, tokens[0], wid, mix, nar, avg, vv, index)
+    sizes = (mix.shape[0], wid.shape[1], nar.shape[1])
+    whole = (w0, mx, n0, w1, n1)
+    block, tok, *grads = backward_call(
+        G, count, sizes, tokens[0], cotangent[0], whole, saved, avg, vv, index
+    )
+    stats = stat_call(
+        G, grads, (mix, wid, nar), (mixer_rows[None], widen_rows, narrow_rows),
+        (mixer_cols[None], widen_cols, narrow_cols), avg,
+    )
+    out = step_call(
+        G, grads, (mix, wid, nar), stats, vectors.reshape(NVEC // 128, 128),
+        vector_moment.reshape(NVEC // 128, 128), avg, jnp.swapaxes(averager_moment, 1, 2), block, tok,
+    )
+    gm, gw, gn, vg, ag, nm, nw, nn, nv, na, rm, cm, rw, cw, rn, cn, vmom, amom, clip, block, tok = out
+    ag, na, amom, gw, gn, nw, nn = (jnp.swapaxes(v, 1, 2) for v in (ag, na, amom, gw, gn, nw, nn))
+    gm, nm = gm.T, nm.T
+    return (
+        block[None], tok[None], gm, gw, gn, vg.reshape(NVEC), ag, nm, nw, nn, nv.reshape(NVEC), na,
+        rm[0], cm[0], rw, cw, rn, cn, vmom.reshape(NVEC), amom, clip[0, 0],
+    )
+
+
 def solution(mesh):
     in_specs = (
-        P("dp", "blk", None),
-        P("dp", "blk", None),
-        P(None, "blk"),
-        P(None, None, "blk"),
-        P(None, None, "blk"),
-        P(),
-        P(),
-        P(),
-        P(),
-        P("blk"),
-        P(),
-        P(None, "blk"),
-        P(),
-        P(None, "blk"),
-        P(),
-        P(),
+        P("dp", "blk", None), P("dp", "blk", None), P(None, "blk"), P(None, None, "blk"), P(None, None, "blk"),
+        P(), P(), P(), P(), P("blk"), P(), P(None, "blk"), P(), P(None, "blk"), P(), P(),
     )
     out_specs = (
-        P("dp", "blk", None),
-        P("dp", "blk", None),
-        P(None, "blk"),
-        P(None, None, "blk"),
-        P(None, None, "blk"),
-        P(),
-        P(),
-        P(None, "blk"),
-        P(None, None, "blk"),
-        P(None, None, "blk"),
-        P(),
-        P(),
-        P(),
-        P("blk"),
-        P(),
-        P(None, "blk"),
-        P(),
-        P(None, "blk"),
-        P(),
-        P(),
-        P(),
-    )
+        P("dp", "blk", None), P("dp", "blk", None), P(None, "blk"), P(None, None, "blk"), P(None, None, "blk"),
+        P(), P(), P(None, "blk"), P(None, None, "blk"), P(None, None, "blk"), P(), P(), P(), P("blk"), P(),
+        P(None, "blk"), P(), P(None, "blk"), P(), P(), P(),
+    )
+    small = mesh.shape["dp"] % 2 == 0 and mesh.shape["blk"] in (8, 16)
+    body = on_device if small else with_collectives
     return jax.shard_map(
-        on_device, mesh=mesh, in_specs=in_specs, out_specs=out_specs, check_vma=False
-    )
+        body, mesh=mesh, in_specs=in_specs, out_specs=out_specs, check_vma=False
+    )

time: 1540 us -> 319 us (0.21)
  waiting for transfers between devices: 910 us -> 0 us
  blocking collectives: 379 us -> 0 us
  Pallas kernels: 0 us -> 312 us
  other arithmetic: 106 us -> 1.27 us
  matrix products: 57.7 us -> 0 us
  local copies, waits for them, and re-layouts: 54.2 us -> 5.3 us
  between operations: 25.6 us -> 0.71 us
    reduce_scatter x4 -> x0, waiting for transfers between devices: 431 us -> none  [the longest x1 143 us: on_device(): lax.psum_scatter(full_grads[1].astype(jnp.bfloat16), 'blk', scatter_dimen...]
    pallas_call x0 -> x4, Pallas kernels: none -> 312 us  [the longest x1 130 us: forward_call(): pl.pallas_call(functools.partial(fwd_kernel, G, (rm, rw, rn)), out_shape=...]
    psum x4 -> x0, blocking collectives: 190 us -> none  [the longest x1 71.8 us: on_device(): lax.psum(tuple((jnp.sum(square_part, axis=2) for square_part in squares))...]
    all_gather x4 -> x0, blocking collectives: 189 us -> none  [the longest x3 144 us: carried_in(): gathered = jax.tree.map(lambda a: lax.all_gather(a, axis), part)]
    unnamed x12 -> x0, waiting for transfers between devices: 185 us -> none
    all_gather x4 -> x0, waiting for transfers between devices: 183 us -> none  [the longest x1 81 us: on_device(): lax.all_gather(shards[1], 'blk', axis=2, tiled=True)]
    psum x2 -> x0, waiting for transfers between devices: 110 us -> none  [the longest x1 110 us: on_device(): lax.psum((vector_local, average_grad), ('dp', 'blk'))]
    dot_general x23 -> x0, matrix products: 57.7 us -> none  [the longest x15 35.5 us: product(): jnp.einsum(pattern, left_side, right_side, preferred_element_type=jnp.flo...]
  transfers between devices with their start and end apart: 11 -> 0, of which waited for: 9 -> 0; matrix products, arithmetic and copies ran while one was open for 10% -> 0% of each run, Pallas kernels for 0% -> 0%
where the time goes in v1:
time: 319 us
  Pallas kernels  312 us (98%)
  local copies, waits for them, and re-layouts  5.3 us (2%)
    pallas_call x1, Pallas kernels, forward_call(): pl.pallas_call(functools.partial(fwd_kernel, G, (rm, rw, rn)), out_shape=...  130 us
    pallas_call x1, Pallas kernels, backward_call(): pl.pallas_call(functools.partial(bwd_kernel, G, count, sizes), out_shape=...  128 us
    pallas_call x1, Pallas kernels, step_call(): pl.pallas_call(functools.partial(step_kernel, G), out_shape=out_shape, in...  29.3 us
    pallas_call x1, Pallas kernels, stat_call(): pl.pallas_call(functools.partial(stat_kernel, G), out_shape=(A((1, D), F3...  24.3 us

profile of v1, /device:TPU:0, one launch (start us, length us, event | category | flops | bytes accessed | tf_op | source)
XLA Modules:
  0.0 319.0 jit_solution(14515761973654298760)
XLA Ops:
  0.7 2.0 pad.8.mix_ref.wm_ref
  2.6 1.4 reshape.63.vec_ref
  4.0 1.3 pad_bitcast_fusion.bias_ref.index_ref
  5.4 129.9 %shard_map.319 = (bf16[4,2,2,96,768]{4,3,2,1,0:T(8,128)(2,1)}, bf16[3200,768]{1,0:T(8,128)(2,1)}, bf16[4,2,2,48,1536]{4,3,2,1,0:T(8,128)(2,1)}, bf16[4,2,2,96,76...) custom-call(f32[128,768]{1,0:T(8,128)} %bitcast.38, ...), custom_call_target="tpu_custom_call" | custom-call | tf_op jit(solution)/shard_map/pallas_call | solution.py:440
  135.3 0.0 copy-start
  135.3 128.2 %shard_map.320 = (f32[128,768]{1,0:T(8,128)}, f32[128,768]{1,0:T(8,128)}, f32[208,768]{1,0:T(8,128)}, f32[2,96,768]{2,1,0:T(8,128)}, f32[2,48,1536]{2,1,0:T(8,12...) custom-call(f32[128,768]{1,0:T(8,128)} %bitcast.39, f32[128,768]{1,0:T(8,128)} %bitcast.41, ...), custom_call_target="tpu_custom_call" | custom-call | tf_op jit(solution)/shard_map/pallas_call | solution.py:1025
  263.5 0.0 copy-done
  263.5 0.6 broadcast_in_dim.12.rm_ref
  264.1 24.3 %shard_map.321 = (f32[1,768]{1,0:T(1,128)}, f32[2,768]{1,0:T(2,128)}, f32[2,1536]{1,0:T(2,128)}, f32[1,200]{1,0:T(1,128)}, f32[2,96]{1,0:T(2,128)}, /*index=5*/f32[2,48]{1,0:T(2,128)}, f32[8,128]{1,0:T(8,128)}) custom-call(f32[208,768]{1,0:T(8,128)} %get-tuple-element.88.gm_ref, f32[2,96,768]{2,1,0:T(8,128)} %get-tuple-element.89.gw_ref, ...), custom_call_target="tpu_custom_call" | custom-call | tf_op jit(solution)/shard_map/pallas_call | solution.py:1637
  288.4 29.3 %shard_map.322 = (f32[200,768]{1,0:T(8,128)}, f32[2,96,768]{2,1,0:T(8,128)}, f32[2,48,1536]{2,1,0:T(8,128)}, f32[96,128]{1,0:T(8,128)}, f32[4,16,768]{2,1,0:T(8,...) custom-call(f32[208,768]{1,0:T(8,128)} %get-tuple-element.88.gm_ref,, ...), custom_call_target="tpu_custom_call" | custom-call | tf_op jit(solution)/shard_map/pallas_call | solution.py:1664
  317.8 1.3 reduce
Async XLA Ops:
  135.3 128.3 %copy-start = (f32[768]{0:T(1024)S(1)}, f32[768]{0:T(1024)}, u32[]{:S(2)}) copy-start(f32[768]{0:T(1024)} %param.24) | copy-start | bytes 9220

commit v2 on v0

--- a/solution.py
+++ b/solution.py
@@ -1,6 +1,9 @@
+import functools
 import jax
 import jax.numpy as jnp
 from jax import lax
+from jax.experimental import pallas as pl
+from jax.experimental.pallas import tpu as pltpu
 from jax.sharding import PartitionSpec as P
 
 D = 768
@@ -11,14 +14,1306 @@
 NB = 128
 STEP = 10
 MX = 3200
-
-
 EPS_NORM = 1e-05
 EPS_ONE = 1e-30
 EPS_TWO = 0.001
 CLIP_NORM = 1.0
 CLIP_UPDATE = 1.0
 RATE = 0.5
+
+OFF_MX = 0
+OFF_V = MX
+OFF_H = OFF_V + VD
+OFF_UP = OFF_H + D
+OFF_DOWN = OFF_UP + FF
+OFF_G1 = OFF_DOWN + D
+OFF_S1 = OFF_G1 + D
+OFF_G2 = OFF_S1 + D
+OFF_S2 = OFF_G2 + D
+OFF_OM = OFF_S2 + D
+OFF_QG = OFF_OM + D
+OFF_QS = OFF_QG + 2 * ZD
+OFF_TB = OFF_QS + 2 * ZD
+NVEC = OFF_TB + NB
+
+MESH = pl.DeviceIdType.MESH
+BF = jnp.bfloat16
+F32 = jnp.float32
+NN = (((1,), (0,)), ((), ()))
+NT = (((1,), (1,)), ((), ()))
+TN = (((0,), (0,)), ((), ()))
+
+
+def dot(a, b, dims=NN):
+    return lax.dot_general(a, b, dims, preferred_element_type=F32)
+
+
+def sigmoid(v):
+    return jax.nn.sigmoid(v)
+
+
+def silu(v):
+    return v * sigmoid(v)
+
+
+def silu_grad(v):
+    s = sigmoid(v)
+    return s * (1.0 + v * (1.0 - s))
+
+
+class Place:
+    def __init__(self, lines):
+        self.lines = lines
+        self.dp = lax.axis_index("dp")
+        blk = lax.axis_index("blk")
+        self.blk = blk
+        self.c = self.dp % 2
+        self.g = blk // 4
+        self.p = blk % 4
+        self.b = self.p // 2
+        self.a = self.p % 2
+        self.na = 1 - self.a
+        self.nb = 1 - self.b
+
+    def sib(self):
+        return (self.dp + 1 - 2 * self.c, self.blk)
+
+    def at(self, g, b, a):
+        return (self.dp, g * 4 + b * 2 + a)
+
+    def line(self, k):
+        return (self.g + k) % self.lines
+
+    def plane(self, k):
+        return (self.p + k) % 4
+
+    def pick(self, first, second):
+        return first + self.c * (second - first)
+
+
+def vec(ref, off, width):
+    rows = range(off // 128, (off + width) // 128)
+    return jnp.concatenate([ref[r : r + 1] for r in rows], axis=1)
+
+
+def greet(others):
+    bar = pltpu.get_barrier_semaphore()
+    for dev in others:
+        pl.semaphore_signal(bar, inc=1, device_id=dev, device_id_type=MESH)
+
+
+def greeted(others):
+    pl.semaphore_wait(pltpu.get_barrier_semaphore(), len(others))
+
+
+def close_peers(me):
+    out = [me.sib()]
+    for k in range(1, me.lines):
+        out.append(me.at(me.line(k), me.b, me.a))
+    for k in range(1, 4):
+        q = me.plane(k)
+        out.append(me.at(me.g, q // 2, q % 2))
+    return out
+
+
+def rcopy(src, dst, ssem, rsem, dev):
+    return pltpu.make_async_remote_copy(
+        src_ref=src, dst_ref=dst, send_sem=ssem, recv_sem=rsem, device_id=dev, device_id_type=MESH
+    )
+
+
+class Gather:
+    def __init__(self, me, W, ssem, rsem):
+        self.me, self.W, self.ssem, self.rsem = me, W, ssem, rsem
+        self.half = W.shape[-1] // 2
+        self.G = me.lines
+        self.started = []
+        self.maybe = []
+        self.chained = set()
+        self.by_plane = False
+
+    def one(self, g, b, a, c):
+        return self.W.at[g, b, a, :, pl.ds(pl.multiple_of(c * self.half, 128), self.half)]
+
+    def go(self, src, slot, dev):
+        cp = rcopy(src, src, self.ssem.at[slot], self.rsem.at[slot], dev)
+        cp.start()
+        self.started.append(cp)
+
+    def await_in(self, ref, slot):
+        rcopy(ref, ref, self.ssem.at[slot], self.rsem.at[slot], self.me.sib()).wait_recv()
+
+    def near(self, j):
+        me, G = self.me, self.G
+        if j == 0:
+            return me.g
+        up = j - 1 + (me.g <= j - 1).astype(jnp.int32)
+        down = G - j - (me.g >= G - j).astype(jnp.int32)
+        low = (me.g < G // 2).astype(jnp.int32)
+        return low * up + (1 - low) * down
+
+    def along(self, h, way):
+        me = self.me
+        to = me.g + way
+        up = jnp.asarray(way > 0, jnp.int32)
+        ok = jnp.logical_and(to >= 0, to < self.G)
+        src = self.one(h, me.b, me.a, me.c)
+        cp = rcopy(
+            src, src, self.ssem.at[8 * self.G + h + self.G * up], self.rsem.at[h], me.at(jnp.clip(to, 0, self.G - 1), me.b, me.a)
+        )
+        pl.when(ok)(cp.start)
+        self.maybe.append((ok, cp))
+
+    def z(self):
+        self.along(self.me.g, 1)
+        self.along(self.me.g, -1)
+
+    def chain(self, j):
+        if j > 0 and j not in self.chained:
+            h = self.near(j)
+            self.await_in(self.one(h, self.me.b, self.me.a, self.me.c), h)
+            self.along(h, 2 * (h < self.me.g).astype(jnp.int32) - 1)
+            self.chained.add(j)
+
+    def first(self, j):
+        me, G = self.me, self.G
+        h = self.near(j)
+        src = self.one(h, me.b, me.a, me.c)
+        self.chain(j)
+        self.go(src, G + h, me.at(me.g, me.b, me.na))
+        self.go(src, 2 * G + h, me.at(me.g, me.nb, me.a))
+        if j > 0:
+            self.go(src, 4 * G + h, me.sib())
+
+    def second(self, j):
+        me, G = self.me, self.G
+        h = self.near(j)
+        x = self.one(h, me.b, me.na, me.c)
+        y = self.one(h, me.nb, me.a, me.c)
+        self.await_in(x, G + h)
+        self.await_in(y, 2 * G + h)
+        fwd = self.one(h, me.pick(me.b, me.nb), me.pick(me.na, me.a), me.c)
+        self.go(fwd, 3 * G + h, me.at(me.g, me.pick(me.nb, me.b), me.pick(me.a, me.na)))
+        self.go(x, 5 * G + h, me.sib())
+        self.go(y, 6 * G + h, me.sib())
+
+    def third(self, j):
+        me, G = self.me, self.G
+        h = self.near(j)
+        d = self.one(h, me.nb, me.na, me.c)
+        self.await_in(d, 3 * G + h)
+        self.go(d, 7 * G + h, me.sib())
+
+    def done(self):
+        me, G = self.me, self.G
+        o = 1 - me.c
+        for j in range(G):
+            h = self.near(j)
+            if j > 0 and self.by_plane:
+                self.await_in(self.bundle(h, o), 4 * G + h)
+                continue
+            if j > 0:
+                self.await_in(self.one(h, me.b, me.a, o), 4 * G + h)
+            self.await_in(self.one(h, me.b, me.na, o), 5 * G + h)
+            self.await_in(self.one(h, me.nb, me.a, o), 6 * G + h)
+            self.await_in(self.one(h, me.nb, me.na, o), 7 * G + h)
+
+    def bundle(self, h, c):
+        return self.W.at[h, :, :, :, pl.ds(pl.multiple_of(c * self.half, 128), self.half)]
+
+    def bundle_along(self, h, way):
+        me = self.me
+        to = me.g + way
+        up = jnp.asarray(way > 0, jnp.int32)
+        ok = jnp.logical_and(to >= 0, to < self.G)
+        src = self.bundle(h, me.c)
+        cp = rcopy(
+            src, src, self.ssem.at[8 * self.G + h + self.G * up], self.rsem.at[h], me.at(jnp.clip(to, 0, self.G - 1), me.b, me.a)
+        )
+        pl.when(ok)(cp.start)
+        self.maybe.append((ok, cp))
+
+    def bundle_out(self):
+        self.by_plane = True
+        self.bundle_along(self.me.g, 1)
+        self.bundle_along(self.me.g, -1)
+
+    def bundle_in(self, j):
+        me, G = self.me, self.G
+        h = self.near(j)
+        src = self.bundle(h, me.c)
+        self.await_in(src, h)
+        self.bundle_along(h, 2 * (h < me.g).astype(jnp.int32) - 1)
+        self.go(src, 4 * G + h, me.sib())
+
+    def drain(self):
+        for cp in self.started:
+            cp.wait_send()
+        for ok, cp in self.maybe:
+            pl.when(ok)(cp.wait_send)
+        self.started, self.maybe = [], []
+
+
+def gather_slots(G):
+    return 10 * G
+
+
+def decays_of(avg_ref):
+    damp = sigmoid(avg_ref[0])
+    mix = sigmoid(avg_ref[1])
+    dec = 1.0 - damp * mix
+    return damp, mix, dec, damp * avg_ref[2], avg_ref[3] * NH ** (-0.5)
+
+
+def power(v, n):
+    while n > 1:
+        v = v * v
+        n = n // 2
+    return v
+
+
+def ma_pass(x_ref, h, dec, inf, outf, pre_ref, keep=None):
+    def step(i, h):
+        if keep is not None:
+            keep[i] = h
+        xs = x_ref[pl.ds(i * 8, 8), :]
+        rows = []
+        for r in range(8):
+            h = dec * h + inf * xs[r : r + 1]
+            if pre_ref is not None:
+                rows.append(jnp.sum(outf * h, axis=0, keepdims=True))
+        if pre_ref is not None:
+            pre_ref[pl.ds(i * 8, 8), :] = jnp.concatenate(rows, axis=0)
+        return h
+
+    return lax.fori_loop(0, x_ref.shape[0] // 8, step, h)
+
+
+def toeplitz_block(bias_ref, m):
+    w = jnp.concatenate([bias_ref[pl.ds(m, 1), :], bias_ref[pl.ds(m + 1, 1), :]], axis=1)
+    return pltpu.roll(jnp.broadcast_to(w, (128, 256)), 1, 1, stride=1, stride_axis=0)[:, 128:]
+
+
+def as_rows(col):
+    return jnp.broadcast_to(col, (128, 128)).T[0:8]
+
+
+def as_col(rows):
+    return jnp.broadcast_to(rows[0:1], (128, 128)).T[:, 0:1]
+
+
+def attend_block(G, T, me, i, q_o, kall, v_o, brow, s_o, ob, lout, att_o):
+    s = dot(q_o[i], kall, NT)
+    tops = []
+    for kk in range(G):
+        m = 4 * kk - i + 3
+        tops.append(toeplitz_block(brow, m))
+    s = s + jnp.concatenate(tops, axis=1)
+    s_o[i] = s
+    top = jnp.max(s, axis=1, keepdims=True)
+    e = jnp.exp(s - top)
+    tot = jnp.sum(e, axis=1, keepdims=True)
+    o = dot(e.astype(BF), v_o[...]) / tot
+    if att_o is None:
+        ob[i] = o.astype(BF)
+    else:
+        att_o[...] = o
+    lout[i] = as_rows(top + jnp.log(tot))
+
+
+class Link:
+    def __init__(self, me, ssem, rsem):
+        self.me, self.ssem, self.rsem = me, ssem, rsem
+        self.used = 0
+        self.started = []
+
+    def slot(self, count=1):
+        self.used += count
+        return self.used - count
+
+    def go(self, src, dst, slot, dev, sent=None):
+        cp = rcopy(src, dst, self.ssem.at[slot if sent is None else sent], self.rsem.at[slot], dev)
+        cp.start()
+        self.started.append(cp)
+
+    def got(self, ref, slot):
+        rcopy(ref, ref, self.ssem.at[slot], self.rsem.at[slot], self.me.sib()).wait_recv()
+
+    def drain(self):
+        for cp in self.started:
+            cp.wait_send()
+        self.started = []
+
+    def swap(self, src, dst):
+        s = self.slot()
+        self.go(src, dst, s, self.me.sib())
+        return lambda: self.got(dst, s)
+
+    def plane(self, src, dst):
+        me = self.me
+        slots = [self.slot() for _ in range(3)]
+        for k in range(1, 4):
+            q = (me.p + k) % 4
+            self.go(src(q), dst(me.p), slots[k - 1], me.at(me.g, q // 2, q % 2))
+
+        def wait():
+            for k in range(1, 4):
+                self.got(dst((me.p + 4 - k) % 4), slots[k - 1])
+
+        return wait
+
+    def line(self, src, dst):
+        me, G = self.me, self.me.lines
+        slots = [self.slot() for _ in range(G - 1)]
+        for k in range(1, G):
+            h = (me.g + k) % G
+            self.go(src(h), dst(me.g), slots[k - 1], me.at(h, me.b, me.a))
+
+        def wait():
+            for k in range(1, G):
+                self.got(dst((me.g + G - k) % G), slots[k - 1])
+
+        return wait
+
+    def pairs(self, src, dst, count):
+        me = self.me
+        slots = [self.slot() for _ in range(count - 1)]
+        for k in range(1, count):
+            d = (me.dp // 2 + k) % count
+            self.go(src, dst(me.dp // 2), slots[k - 1], (2 * d + me.c, me.blk))
+
+        def wait():
+            for k in range(1, count):
+                self.got(dst((me.dp // 2 + count - k) % count), slots[k - 1])
+
+        return wait
+
+
+class Reduce:
+    def __init__(self, me, link, near, H, R, RL):
+        self.me, self.link, self.near, self.H, self.R, self.RL = me, link, near, H, R, RL
+        self.base = link.slot(6 * me.lines)
+        self.by_plane = False
+        self.s = (me.pick(me.nb, me.b), me.pick(me.a, me.na))
+        self.m = (me.pick(me.b, me.nb), me.pick(me.na, me.a))
+
+    def at(self, h):
+        return 0 if self.by_plane else h
+
+    def send(self, h, place, kind, to):
+        self.link.go(
+            self.H.at[h, place[0], place[1]], self.R.at[kind, self.at(h)], self.base + kind * self.me.lines + h,
+            self.me.at(self.me.g, to[0], to[1]),
+        )
+
+    def got(self, h, kind):
+        self.link.got(self.R.at[kind, self.at(h)], self.base + kind * self.me.lines + h)
+
+    def add(self, h, place, kinds):
+        total = self.H[h, place[0], place[1]].astype(F32)
+        for kind in kinds:
+            total = total + self.R[kind, self.at(h)].astype(F32)
+        self.H[h, place[0], place[1]] = total.astype(BF)
+
+    def behind(self, j):
+        self.send(self.near(j), (self.me.nb, self.me.na), 0, self.s)
+
+    def theirs(self, j):
+        self.send(self.near(j), self.s, 1, self.s)
+
+    def passed(self, j):
+        h = self.near(j)
+        self.got(h, 0)
+        self.add(h, self.m, (0,))
+        self.send(h, self.m, 2, self.m)
+
+    def mine(self, j):
+        me, h = self.me, self.near(j)
+        self.got(h, 1)
+        self.got(h, 2)
+        self.add(h, (me.b, me.a), (1, 2))
+        if j > 0 and not self.by_plane:
+            self.link.go(
+                self.H.at[h, me.b, me.a], self.RL.at[me.g], self.base + 3 * me.lines + me.g, me.at(h, me.b, me.a),
+                self.base + 3 * me.lines + h,
+            )
+
+    def flow(self, j):
+        me, G = self.me, self.me.lines
+        h = self.near(j)
+        self.by_plane = True
+        base = self.base + 3 * G
+        if j == 0:
+            for slot, ok in ((h, me.g > 0), (G, me.g < G - 1)):
+                pl.when(ok)(functools.partial(self.flow_in, h, slot))
+            return
+        up = (h > me.g).astype(jnp.int32)
+        pl.when(jnp.where(up == 1, me.g > 0, me.g < G - 1))(functools.partial(self.flow_in, h, h))
+        slot = jnp.where(h == me.g - 1, G, h)
+        self.link.go(self.H.at[h], self.RL.at[slot], base + slot, me.at(me.g + 2 * up - 1, me.b, me.a), base + 2 * G + h)
+
+    def flow_in(self, h, slot):
+        self.link.got(self.RL.at[slot], self.base + 3 * self.me.lines + slot)
+        self.H[h] = (self.H[h].astype(F32) + self.RL[slot].astype(F32)).astype(BF)
+
+    def total(self):
+        me = self.me
+        if self.by_plane:
+            return self.H[me.g, me.b, me.a].astype(F32)
+        for k in range(1, me.lines):
+            h = (me.g + k) % me.lines
+            self.link.got(self.RL.at[h], self.base + 3 * me.lines + h)
+        self.RL[me.g] = self.H[me.g, me.b, me.a]
+        total = self.RL[0].astype(F32)
+        for g in range(1, me.lines):
+            total = total + self.RL[g].astype(F32)
+        return total
+
+
+def into_blocks(H, value, first, rows):
+    n = 4 * H.shape[0]
+    count = value.shape[0]
+    value = value.astype(BF)
+    if H.shape[3] == rows and first == 0 and count == n * rows:
+        H[...] = value.reshape(H.shape)
+        return
+    for i in range(n):
+        lo, hi = max(first, i * rows), min(first + count, (i + 1) * rows)
+        if lo < hi:
+            H[i // 4, (i // 2) % 2, i % 2, lo - i * rows : hi - i * rows] = value[lo - first : hi - first]
+
+
+def norm(v):
+    centered = v - jnp.mean(v, axis=-1, keepdims=True)
+    inverse = lax.rsqrt(jnp.mean(centered * centered, axis=-1, keepdims=True) + EPS_NORM)
+    return centered * inverse, inverse
+
+
+def norm_back(incoming, normed, inverse, gain):
+    scaled = incoming * gain
+    return inverse * (
+        scaled
+        - jnp.mean(scaled, axis=-1, keepdims=True)
+        - normed * jnp.mean(scaled * normed, axis=-1, keepdims=True)
+    )
+
+
+def down(v):
+    return jnp.sum(v.astype(F32), axis=0, keepdims=True)
+
+
+def put(ref, off, row):
+    width, at = row.shape[1], 0
+    while at < width:
+        r, lane = (off + at) // D, (off + at) % D
+        take = min(width - at, D - lane)
+        ref[r : r + 1, lane : lane + take] = row[:, at : at + take]
+        at += take
+
+
+def ma_back_first(bp_ref, dec, outf, h):
+    n8 = bp_ref.shape[0] // 8
+
+    def step(i, h):
+        bs = bp_ref[pl.ds((n8 - 1 - i) * 8, 8), :]
+        for r in range(7, -1, -1):
+            h = dec * (outf * bs[r : r + 1] + h)
+        return h
+
+    return lax.fori_loop(0, n8, step, h)
+
+
+def ma_back(x_ref, bp_ref, keep_ref, leave, dec, inf, outf, tok_o, AV):
+    n8 = x_ref.shape[0] // 8
+    wide = 256
+    for j in range(D // wide):
+        sl = slice(j * wide, (j + 1) * wide)
+        d, f, u = dec[:, sl], inf[:, sl], outf[:, sl]
+
+        def step(i, carry):
+            h, dd, di, du = carry
+            at = n8 - 1 - i
+            xs = x_ref[pl.ds(at * 8, 8), sl]
+            bs = bp_ref[pl.ds(at * 8, 8), sl]
+            states = [keep_ref[at, :, sl]]
+            for r in range(8):
+                states.append(d * states[-1] + f * xs[r : r + 1])
+            rows = [None] * 8
+            for r in range(7, -1, -1):
+                adj = u * bs[r : r + 1] + h
+                dd = dd + adj * states[r]
+                di = di + adj * xs[r : r + 1]
+                du = du + bs[r : r + 1] * states[r + 1]
+                rows[r] = jnp.sum(f * adj, axis=0, keepdims=True)
+                h = d * adj
+            tok_o[pl.ds(at * 8, 8), sl] += jnp.concatenate(rows, axis=0)
+            return h, dd, di, du
+
+        zero = jnp.zeros((NH, wide), F32)
+        _, dd, di, du = lax.fori_loop(0, n8, step, (leave[:, sl], zero, zero, zero))
+        AV[16 : 16 + NH, sl] = dd
+        AV[16 + NH : 16 + 2 * NH, sl] = di
+        AV[16 + 2 * NH : 16 + 3 * NH, sl] = du
+
+
+def diagonals(G, T, GS, prof):
+    flip = (
+        lax.broadcasted_iota(jnp.int32, (T, T), 0) + lax.broadcasted_iota(jnp.int32, (T, T), 1) == T - 1
+    ).astype(F32).astype(BF)
+    for i in range(4):
+        turned = dot(flip, GS[i])
+        for kk in range(G):
+            m = 4 * kk - i + 3
+            block = jnp.concatenate([turned[:, kk * T : (kk + 1) * T], jnp.zeros((T, T), F32)], axis=1)
+            s = jnp.sum(pltpu.roll(block, 0, 1, stride=1, stride_axis=0), axis=0, keepdims=True)
+            prof[m : m + 1] += s[:, :T]
+            prof[m + 1 : m + 2] += s[:, T:]
+
+
+def table_rows(G, me, prof, index_ref, AV):
+    first_row = me.p - 4 * me.g - 4 + 4 * G
+    total = jnp.zeros((NB, 128), F32)
+    for r in range(4 * G + 1):
+        hit = index_ref[pl.ds(first_row + r, 1), :] == lax.broadcasted_iota(jnp.int32, (NB, 128), 0)
+        total = total + jnp.where(hit, prof[r : r + 1], 0.0)
+    col = jnp.sum(total, axis=1, keepdims=True)
+    put(AV, OFF_TB, as_rows(col)[0:1])
+
+
+(
+    SEND_X, AVERAGE_PLANE, AVERAGE, VALUES_0, VALUES_1, MIXING, BIAS_ROWS, MERGE, HIDDEN, FEED, FEED_OUT,
+    BACK_UP, BACK_ONE, BACK_GATE, BACK_QUERIES, BACK_KEYS, SWAP_VALUES, VALUES_TO_TOKENS, GRADS_VALUES,
+    BACK_SHARED, BACK_PRE, GRADS_MIXER, ADJOINT_FIRST, ADJOINT_PLANE, ADJOINT, DIAGONALS, TABLE_ROWS,
+    SUMS_CORE, SUMS_PLANE, SUMS_LINE, SUMS_BACK, SUMS_ALL, ADD_VALUES, STATS, GRADS_DOWN, GRADS_UP,
+    GRADS_HIDDEN,
+) = range(37)
+(
+    FIRST, SECOND, THIRD, CHAIN, BUNDLE_IN, BEHIND, THEIRS, PASSED, MINE, FLOW, ALONG, BUNDLE_OUT, READY,
+    CLOSE, ATTEND, ATTEND_BACK, VALUES_BACK,
+) = range(100, 1800, 100)
+ORDER = (
+    ALONG + 0, FIRST + 40, FIRST + 10, ALONG + 1, CHAIN + 2, FIRST + 2, ALONG + 2, CHAIN + 1, SECOND + 40, CHAIN + 11,
+    FIRST + 30, CHAIN + 22, FIRST + 1, FIRST + 11, FIRST + 0, ALONG + 3, SECOND + 2, BIAS_ROWS, CHAIN + 12,
+    CHAIN + 31, FIRST + 12, THIRD + 40, AVERAGE_PLANE, FIRST + 31, FIRST + 20, SECOND + 10, CHAIN + 3, SECOND + 30,
+    CHAIN + 13, CHAIN + 21, CHAIN + 23, FIRST + 13, FIRST + 3, AVERAGE, CHAIN + 33, SECOND + 31, SECOND + 0,
+    CHAIN + 32, SECOND + 12, SEND_X, SECOND + 3, FIRST + 22, THIRD + 31, THIRD + 10, SECOND + 13, THIRD + 0,
+    FIRST + 21, SECOND + 11, THIRD + 12, SECOND + 21, THIRD + 3, SECOND + 20, THIRD + 13, THIRD + 11, SECOND + 1,
+    SECOND + 22, THIRD + 2, READY + 1, THIRD + 20, BUNDLE_OUT + 4, FIRST + 32, FIRST + 33, THIRD + 1, MIXING,
+    READY + 0, FIRST + 23, VALUES_0, SECOND + 32, VALUES_1, SECOND + 23, SECOND + 33, ATTEND + 2, ATTEND + 1,
+    BUNDLE_IN + 41, THIRD + 30, ATTEND + 0, BUNDLE_IN + 42, THIRD + 22, THIRD + 21, THIRD + 32, ATTEND + 3,
+    THIRD + 23, READY + 2, THIRD + 33, BUNDLE_IN + 43, READY + 3, READY + 4, MERGE, HIDDEN, FEED, FEED_OUT, BACK_UP,
+    BACK_ONE, BACK_GATE, GRADS_DOWN, FLOW + 43, GRADS_HIDDEN, BEHIND + 22, GRADS_UP, PASSED + 22, FLOW + 42,
+    ATTEND_BACK + 2, THEIRS + 20, BEHIND + 30, ATTEND_BACK + 3, BEHIND + 31, THEIRS + 22, FLOW + 41, THEIRS + 31,
+    ATTEND_BACK + 1, BEHIND + 23, BEHIND + 21, ATTEND_BACK + 0, BACK_KEYS, THEIRS + 23, VALUES_BACK + 0,
+    VALUES_BACK + 2, VALUES_BACK + 1, SWAP_VALUES, BEHIND + 33, PASSED + 30, BEHIND + 32, BACK_QUERIES,
+    VALUES_TO_TOKENS, PASSED + 23, THEIRS + 32, THEIRS + 30, PASSED + 21, GRADS_VALUES, PASSED + 33, BEHIND + 0,
+    THEIRS + 33, THEIRS + 1, BACK_SHARED, BEHIND + 1, BACK_PRE, ADJOINT_FIRST, PASSED + 0, DIAGONALS, PASSED + 31,
+    PASSED + 1, THEIRS + 21, THEIRS + 3, BEHIND + 2, PASSED + 32, GRADS_MIXER, BEHIND + 12, ADJOINT_PLANE,
+    THEIRS + 11, MINE + 1, MINE + 22, MINE + 31, MINE + 30, BEHIND + 3, MINE + 33, BEHIND + 13, THEIRS + 13,
+    PASSED + 12, MINE + 23, TABLE_ROWS, FLOW + 40, THEIRS + 12, BEHIND + 40, THEIRS + 0, MINE + 32, ADJOINT,
+    PASSED + 3, BEHIND + 20, ADD_VALUES, SUMS_CORE, PASSED + 13, THEIRS + 40, MINE + 3, SUMS_PLANE, PASSED + 20,
+    BEHIND + 11, MINE + 12, PASSED + 40, SUMS_LINE, MINE + 13, THEIRS + 2, BEHIND + 10, MINE + 21, MINE + 40,
+    PASSED + 11, MINE + 11, SUMS_BACK, PASSED + 2, CLOSE + 3, CLOSE + 4, MINE + 0, MINE + 20, THEIRS + 10,
+    PASSED + 10, SUMS_ALL, CLOSE + 2, MINE + 10, MINE + 2, CLOSE + 1, CLOSE + 0, STATS,
+)
+
+
+class Refs:
+    def __init__(self, names, refs):
+        self.__dict__.update(zip(names, refs))
+
+
+def main_kernel(G, count, in_names, out_names, scratch_names, *refs):
+    a, b = len(in_names), len(in_names) + len(out_names)
+    I, O, S = Refs(in_names, refs[:a]), Refs(out_names, refs[a:b]), Refs(scratch_names, refs[b:])
+    me = Place(G)
+    T = I.x.shape[0]
+    o = 1 - me.c
+    others = close_peers(me)
+    for k in range(1, count):
+        others.append((2 * ((me.dp // 2 + k) % count) + me.c, me.blk))
+    greet(others)
+    Ws = (S.w0, S.mx, S.n0, S.w1, S.n1)
+    for W, src in zip(Ws, (I.wid.at[0], I.mix, I.nar.at[0], I.wid.at[1], I.nar.at[1])):
+        r = src.shape[0]
+        W[me.g, me.b, me.a, 0:r] = src[...].astype(BF)
+        if r < W.shape[3]:
+            W[me.g, me.b, me.a, r:] = jnp.zeros((W.shape[3] - r, W.shape[4]), BF)
+    S.xb[me.g] = I.x[...].astype(BF)
+    damp, mix, dec, inf, outf = decays_of(I.avg)
+    zero = jnp.zeros((NH, D), F32)
+    whole = power(dec, T)
+    S.fin[me.p] = ma_pass(I.x, zero, dec, inf, outf, None)
+    S.AV[...] = jnp.zeros_like(S.AV)
+    S.prof[...] = jnp.zeros_like(S.prof)
+    greeted(others)
+    link = Link(me, S.ssem, S.rsem)
+    got = {}
+    val = {}
+    ga = [Gather(me, W, S.agss.at[i], S.agrs.at[i]) for i, W in enumerate(Ws)]
+    got["fin"] = link.plane(lambda q: S.fin.at[me.p], lambda q: S.fin.at[q])
+    mixed = lambda off, w: S.mixed[:, off : off + w]
+    vector = lambda off, w: vec(I.vec, off, w)
+    scaling = ZD ** (-0.5)
+
+    def cols(c, half):
+        return pl.ds(pl.multiple_of(c * half, 128), half)
+
+    def flat(W):
+        return W[...].reshape(4 * G * W.shape[3], W.shape[4])
+
+    def send_x():
+        got["x"] = link.line(lambda h: S.xb.at[me.g], lambda h: S.xb.at[h])
+
+    def average_plane():
+        got.pop("fin")()
+        tot = S.fin[0]
+        for q in range(1, 4):
+            tot = whole * tot + S.fin[q]
+        S.ftot[me.g] = tot
+        got["ftot"] = link.line(lambda h: S.ftot.at[me.g], lambda h: S.ftot.at[h])
+
+    def average_second():
+        got.pop("ftot")()
+        ent = zero
+        whole4 = power(whole, 4)
+        for i in range(G - 1):
+            ent = jnp.where(i < me.g, whole4 * ent + S.ftot[i], ent)
+        for q in range(3):
+            ent = jnp.where(q < me.p, whole * ent + S.fin[q], ent)
+        ma_pass(I.x, ent, dec, inf, outf, S.pre, S.keep)
+        S.pre[...] = S.pre[...] + vector(OFF_OM, D) * I.x[...]
+
+    def values(i):
+        if i == 0:
+            got.pop("x")()
+            got["xb"] = link.swap(S.xb.at[:, :, cols(o, D // 2)], S.XB)
+        step = max(1, G // 2)
+        wide = step * 4 * S.w0.shape[3]
+        wblk = S.w0[i * step : (i + 1) * step].reshape(wide, D)
+        sl = slice(i * wide, (i + 1) * wide)
+        for gg in range(G):
+            vp = dot(S.xb[gg], wblk, NT) + vector(OFF_V + i * wide, wide)
+            S.GV[0, gg * T : (gg + 1) * T, sl] = silu_grad(vp).astype(BF)
+            S.v[gg * T : (gg + 1) * T, sl] = silu(vp).astype(BF)
+
+    chunk = MX // 5
+
+    def mixer_rows(i):
+        r = MX // (4 * G)
+        at = 0
+        for k in range(4 * G):
+            lo, hi = max(i * chunk, k * r), min((i + 1) * chunk, (k + 1) * r)
+            if lo < hi:
+                S.mc[at : at + hi - lo] = S.mx[k // 4, (k // 2) % 2, k % 2, lo - k * r : hi - k * r]
+                at += hi - lo
+        return S.mc[...]
+
+    def mixing():
+        prime = silu(S.pre[...]).astype(BF)
+        for i in (1, 0, 2, 3, 4):
+            sl = slice(i * chunk, (i + 1) * chunk)
+            S.mixed[:, sl] = dot(prime, mixer_rows(i), NT) + vector(OFF_MX + i * chunk, chunk)
+            if i == 0:
+                shared = silu(mixed(D, ZD))
+                S.qb[me.p] = ((shared * vector(OFF_QG, ZD) + vector(OFF_QS, ZD)) * scaling).astype(BF)
+                S.kb[me.g] = (shared * vector(OFF_QG + ZD, ZD) + vector(OFF_QS + ZD, ZD)).astype(BF)
+                got["q"] = link.plane(lambda q: S.qb.at[me.p], lambda q: S.qb.at[q])
+                got["k"] = link.line(lambda h: S.kb.at[me.g], lambda h: S.kb.at[h])
+
+    def bias_rows():
+        first_row = me.p - 4 * me.g - 4 + 4 * G
+        table = jnp.broadcast_to(vector(OFF_TB, NB), (128, NB)).T
+        for r in range(4 * G + 1):
+            hit = I.index[pl.ds(first_row + r, 1), :] == lax.broadcasted_iota(jnp.int32, (NB, 128), 0)
+            S.brow[r : r + 1] = jnp.sum(jnp.where(hit, table, 0.0), axis=0, keepdims=True)
+
+    def attend(kk):
+        if kk == 2:
+            got.pop("q")()
+            got.pop("k")()
+            val["o"] = [link.slot(4), link.slot(4)]
+        i = (me.p + kk) % 4
+        kall = S.kb[...].reshape(G * T, ZD)
+        attend_block(G, T, me, i, S.qb, kall, S.v, S.brow, S.s, S.ob, S.lout, S.att if kk == 0 else None)
+        if kk:
+            to = me.at(me.g, i // 2, i % 2)
+            link.go(S.ob.at[i], S.oin.at[me.p], val["o"][0] + kk, to)
+            link.go(S.lout.at[i], S.lin.at[me.p], val["o"][1] + kk, to)
+        else:
+            S.lin[me.p] = S.lout[me.p]
+
+    def merge():
+        for k in range(1, 4):
+            link.got(S.oin.at[(me.p + 4 - k) % 4], val["o"][0] + k)
+            link.got(S.lin.at[(me.p + 4 - k) % 4], val["o"][1] + k)
+        ls = [as_col(S.lin[j]) for j in range(4)]
+        peak = functools.reduce(jnp.maximum, ls)
+        lse = peak + jnp.log(functools.reduce(jnp.add, [jnp.exp(l - peak) for l in ls]))
+        S.att[...] = S.att[...] * jnp.exp(as_col(S.lout[me.p]) - lse)
+        for k in range(1, 4):
+            j = (me.p + k) % 4
+            S.att[...] += S.oin[j].astype(F32) * jnp.exp(as_col(S.lin[j]) - lse)
+        S.ST[me.p, 0] = as_rows(lse)
+        link.drain()
+
+    full = S.ob
+
+    def share_half(k, width, dst):
+        half = width // 2
+        dst[0] = full[k, :, cols(me.c, half)]
+        return link.swap(full.at[k, :, cols(o, half)], dst.at[1])
+
+    def hidden():
+        x = I.x[...]
+        full[1, :, :D] = silu(S.pre[...]).astype(BF)
+        got["pb"] = share_half(1, D, S.PB)
+        full[0] = (silu(mixed(D + ZD, VD)) * S.att[...]).astype(BF)
+        got["gt"] = share_half(0, VD, S.GT)
+        hidden_pre = mixed(D + ZD + VD, D) + dot(full[0], flat(S.n0), NT) + vector(OFF_H, D)
+        upd = sigmoid(mixed(0, D))
+        act = silu(hidden_pre)
+        one = x + upd * (act - x)
+        n_one, r_one = norm(one)
+        layer = n_one * vector(OFF_G1, D) + vector(OFF_S1, D)
+        full[2, :, :D] = layer.astype(BF)
+        got["ll"] = share_half(2, D, S.LL)
+        val.update(x=x, hidden_pre=hidden_pre, upd=upd, act=act, n_one=n_one, r_one=r_one, layer=layer)
+
+    def feed():
+        val["expand_pre"] = dot(full[2, :, :D], flat(S.w1), NT) + vector(OFF_UP, FF)
+        full[3] = silu(val["expand_pre"]).astype(BF)
+        got["ex"] = share_half(3, FF, S.EX)
+
+    def feed_out():
+        two = val["layer"] + dot(full[3], flat(S.n1), NT) + vector(OFF_DOWN, D)
+        n_two, r_two = norm(two)
+        gain_two = vector(OFF_G2, D)
+        O.block[...] = n_two * gain_two + vector(OFF_S2, D)
+        cot = I.cot[...]
+        val["back_two"] = norm_back(cot, n_two, r_two, gain_two)
+        put(S.AV, OFF_G2, down(cot * n_two))
+        put(S.AV, OFF_S2, down(cot))
+        S.GD[0] = val["back_two"].astype(BF)
+        got["gd"] = link.swap(S.GD.at[0], S.GD.at[1])
+        put(S.AV, OFF_DOWN, down(S.GD[0]))
+
+    def back_up():
+        S.GU[0] = (dot(S.GD[0], flat(S.n1)) * silu_grad(val["expand_pre"])).astype(BF)
+        got["gu"] = link.swap(S.GU.at[0], S.GU.at[1])
+        put(S.AV, OFF_UP, down(S.GU[0]))
+
+    def back_first():
+        into_one = val["back_two"] + dot(S.GU[0], flat(S.w1))
+        put(S.AV, OFF_G1, down(into_one * val["n_one"]))
+        put(S.AV, OFF_S1, down(into_one))
+        back_one = norm_back(into_one, val["n_one"], val["r_one"], vector(OFF_G1, D))
+        S.GH[0] = (back_one * val["upd"] * silu_grad(val["hidden_pre"])).astype(BF)
+        got["gh"] = link.swap(S.GH.at[0], S.GH.at[1])
+        put(S.AV, OFF_H, down(S.GH[0]))
+        val["back_one"] = back_one
+
+    def back_gate():
+        upd, back_one = val["upd"], val["back_one"]
+        back_gated = dot(S.GH[0], flat(S.n0))
+        S.GA[me.p] = (back_gated * silu(mixed(D + ZD, VD))).astype(BF)
+        S.ST[me.p, 1] = as_rows(jnp.sum(S.GA[me.p].astype(F32) * S.att[...], axis=1, keepdims=True))
+        got["ga"] = link.plane(lambda q: S.GA.at[me.p], lambda q: S.GA.at[q])
+        got["st"] = link.plane(lambda q: S.ST.at[me.p], lambda q: S.ST.at[q])
+        S.GM[0, :, 0:D] = (back_one * (val["act"] - val["x"]) * upd * (1.0 - upd)).astype(BF)
+        S.GM[0, :, D + ZD : D + ZD + VD] = (back_gated * S.att[...] * silu_grad(mixed(D + ZD, VD))).astype(BF)
+        S.GM[0, :, D + ZD + VD :] = S.GH[0]
+        O.tok[...] = back_one * (1.0 - upd)
+
+    Hs = [W.at[:, :, :, :, 0 : W.shape[-1] // 2] for W in Ws]
+    near = ga[0].near
+    red = [Reduce(me, link, near, H, R, L) for H, R, L in zip(Hs, (S.R0, S.RM, S.RN0, S.R1, S.RN1), (S.L0, S.LM, S.LN0, S.L1, S.LN1))]
+
+    def both(ref):
+        return ref[...].reshape(2 * T, ref.shape[-1])
+
+    def grads(i, out, into, names):
+        for name in names:
+            got.pop(name)()
+        ga[i].drain()
+        rhs = both(into)
+        for j in range(0, out.shape[-1], 384):
+            lhs = out[:, :, j : j + 384].reshape(2 * T, 384)
+            into_blocks(Hs[i], dot(lhs, rhs, TN), j, out.shape[-1] // (4 * G))
+
+    def attend_back(kk):
+        if kk == 2:
+            got.pop("ga")()
+            got.pop("st")()
+        i = (me.p + kk) % 4
+        probs = jnp.exp(S.s[i] - as_col(S.ST[i, 0]))
+        back = dot(S.GA[i], S.v[...], NT)
+        gs = (probs * (back - as_col(S.ST[i, 1]))).astype(BF)
+        S.P16[i] = probs.astype(BF)
+        S.GS[i] = gs
+        S.QP[i] = dot(gs, S.kb[...].reshape(G * T, ZD))
+
+    def back_queries():
+        got["dq"] = link.plane(lambda q: S.QP.at[q], lambda q: S.KS.at[q])
+
+    def back_keys():
+        S.KP[...] = dot(S.GS[...].reshape(4 * T, G * T), S.qb[...].reshape(4 * T, ZD), TN).reshape(G, T, ZD)
+        got["dk"] = link.line(lambda h: S.KP.at[h], lambda h: S.DP.at[h])
+
+    def back_values(j):
+        wide = VD // 3
+        sl = slice(j * wide, (j + 1) * wide)
+        dv = dot(S.P16[...].reshape(4 * T, G * T), S.GA[:, :, sl].reshape(4 * T, wide), TN)
+        gv = (dv * S.GV[0, :, sl].astype(F32)).astype(BF)
+        S.GV[0, :, sl] = gv
+        put(S.AV, OFF_V + j * wide, down(gv))
+
+    def swap_values():
+        got["gv"] = link.swap(S.GV.at[0], S.GV.at[1])
+
+    def values_to_tokens():
+        for g in range(G):
+            S.DX[g] = dot(S.GV[0, g * T : (g + 1) * T], flat(S.w0)).astype(BF)
+        got["dx"] = link.line(lambda h: S.DX.at[h], lambda h: S.BP.at[h])
+
+    def grads_values():
+        got.pop("gv")()
+        got.pop("xb")()
+        ga[0].drain()
+        own = S.xb[:, :, cols(me.c, D // 2)].reshape(G * T, D // 2)
+        their = S.XB[...].reshape(G * T, D // 2)
+        wide = VD // 4
+        for j in range(4):
+            sl = slice(j * wide, (j + 1) * wide)
+            total = dot(S.GV[0, :, sl], own, TN) + dot(S.GV[1, :, sl], their, TN)
+            into_blocks(Hs[0], total, j * wide, VD // (4 * G))
+
+    def back_shared():
+        got.pop("dq")()
+        S.KS[me.p] = S.QP[me.p]
+        back_q = (S.KS[0] + S.KS[1] + S.KS[2] + S.KS[3]) * scaling
+        got.pop("dk")()
+        S.DP[me.g] = S.KP[me.g]
+        back_k = S.DP[0]
+        for g in range(1, G):
+            back_k = back_k + S.DP[g]
+        sp = mixed(D, ZD)
+        shared = silu(sp)
+        put(S.AV, OFF_QG, down(back_q * shared))
+        put(S.AV, OFF_QG + ZD, down(back_k * shared))
+        put(S.AV, OFF_QS, down(back_q))
+        put(S.AV, OFF_QS + ZD, down(back_k))
+        back = back_q * vector(OFF_QG, ZD) + back_k * vector(OFF_QG + ZD, ZD)
+        S.GM[0, :, D : D + ZD] = (back * silu_grad(sp)).astype(BF)
+        got["gm"] = link.swap(S.GM.at[0], S.GM.at[1])
+        put(S.AV, OFF_MX, down(S.GM[0]))
+
+    def back_pre():
+        back = jnp.zeros((T, D), F32)
+        for i in range(5):
+            back = back + dot(S.GM[0, :, i * chunk : (i + 1) * chunk], mixer_rows(i))
+        back = back * silu_grad(S.pre[...])
+        O.tok[...] += vector(OFF_OM, D) * back
+        put(S.AV, OFF_OM, down(back * I.x[...]))
+        S.bp[...] = back
+
+    def grads_mixer():
+        got.pop("gm")()
+        got.pop("pb")()
+        ga[1].drain()
+        rhs = both(S.PB)
+        for j in range(5):
+            sl = slice(j * chunk, (j + 1) * chunk)
+            into_blocks(Hs[1], dot(S.GM[:, :, sl].reshape(2 * T, chunk), rhs, TN), j * chunk, MX // (4 * G))
+
+    def average_back():
+        S.fin2[me.p] = ma_back_first(S.bp, dec, outf, zero)
+        got["fin2"] = link.plane(lambda q: S.fin2.at[me.p], lambda q: S.fin2.at[q])
+
+    def average_back_plane():
+        got.pop("fin2")()
+        tot = S.fin2[3]
+        for q in (2, 1, 0):
+            tot = whole * tot + S.fin2[q]
+        S.ftot2[me.g] = tot
+        got["ftot2"] = link.line(lambda h: S.ftot2.at[me.g], lambda h: S.ftot2.at[h])
+
+    def average_back_second():
+        got.pop("ftot2")()
+        whole4 = power(whole, 4)
+        leave = zero
+        for i in range(G - 1, 0, -1):
+            leave = jnp.where(i > me.g, whole4 * leave + S.ftot2[i], leave)
+        for q in (3, 2, 1):
+            leave = jnp.where(q > me.p, whole * leave + S.fin2[q], leave)
+        ma_back(I.x, S.bp, S.keep, leave, dec, inf, outf, O.tok, S.AV)
+
+    def pair_sum(value, buf):
+        buf[me.dp // 2] = value
+        link.pairs(buf.at[me.dp // 2], lambda d: buf.at[d], count)()
+        value = buf[0]
+        for d in range(1, count):
+            value = value + buf[d]
+        return value
+
+    Fs = (S.F0, S.FM, S.FN0, S.F1, S.FN1)
+    Ps = (S.P0, S.PM, S.PN0, S.P1, S.PN1)
+    finish = []
+
+    def close(i):
+        F = Fs[i]
+        total = red[i].total()
+        half = total.shape[-1]
+        if count > 1:
+            total = pair_sum(total, Ps[i])
+        F[:, cols(me.c, half)] = total
+        part = F.at[:, cols(me.c, half)]
+        s = link.slot()
+        link.go(part, part, s, me.sib())
+        finish.append(lambda: link.got(F.at[:, cols(o, half)], s))
+
+    hr = S.AV.shape[0] // 2
+    qr = hr // 4
+
+    def rows_of(core, q, n):
+        return pl.ds(pl.multiple_of(core * hr + q * qr, 8), n)
+
+    def sums_core():
+        got["av"] = link.swap(S.AV, S.AS)
+
+    def sums_plane():
+        got.pop("av")()
+        S.AW[...] = S.AV[...] + S.AS[...]
+        got["ap"] = link.plane(lambda q: S.AW.at[rows_of(me.c, q, qr), :], lambda q: S.AP.at[q])
+
+    def sums_line():
+        got.pop("ap")()
+        S.AP[me.p] = S.AW[rows_of(me.c, me.p, qr), :]
+        S.AL[me.g] = S.AP[0] + S.AP[1] + S.AP[2] + S.AP[3]
+        got["al"] = link.line(lambda h: S.AL.at[me.g], lambda h: S.AL.at[h])
+
+    def sums_back():
+        got.pop("al")()
+        tot = S.AL[0]
+        for g in range(1, G):
+            tot = tot + S.AL[g]
+        if count > 1:
+            tot = pair_sum(tot, S.PA)
+        S.AT[rows_of(me.c, me.p, qr), :] = tot
+        got["at"] = link.plane(lambda q: S.AT.at[rows_of(me.c, me.p, qr), :], lambda q: S.AT.at[rows_of(me.c, q, qr), :])
+
+    def sums_all():
+        got.pop("at")()
+        s = link.slot()
+        mine = S.AT.at[rows_of(me.c, 0, hr), :]
+        link.go(mine, mine, s, me.sib())
+        finish.append(lambda: link.got(S.AT.at[rows_of(o, 0, hr), :], s))
+
+    def add_values():
+        got.pop("dx")()
+        S.BP[me.g] = S.DX[me.g]
+        for g in range(G):
+            O.tok[...] += S.BP[g].astype(F32)
+
+    def allsum(value, pb, lb):
+        pb[me.p] = value
+        link.plane(lambda q: pb.at[me.p], lambda q: pb.at[q])()
+        lb[me.g] = pb[0] + pb[1] + pb[2] + pb[3]
+        link.line(lambda h: lb.at[me.g], lambda h: lb.at[h])()
+        out = lb[0]
+        for g in range(1, G):
+            out = out + lb[g]
+        return out
+
+    def stats():
+        for f in finish:
+            f()
+        O.sums[...] = S.AT[0:16]
+        O.ma[...] = S.AT[16:64].reshape(3, NH, D)
+        for F, dst, i in zip(Fs, (O.gw.at[0], O.gm, O.gn.at[0], O.gw.at[1], O.gn.at[1]), range(5)):
+            pltpu.make_async_copy(F, dst, S.outs.at[i]).start()
+        adafactor_stats(G, I, O, S, allsum)
+        for F, dst, i in zip(Fs, (O.gw.at[0], O.gm, O.gn.at[0], O.gw.at[1], O.gn.at[1]), range(5)):
+            pltpu.make_async_copy(F, dst, S.outs.at[i]).wait()
+
+    one = {
+        SEND_X: send_x, AVERAGE_PLANE: average_plane, AVERAGE: average_second, VALUES_0: lambda: values(0),
+        VALUES_1: lambda: values(1), MIXING: mixing, BIAS_ROWS: bias_rows, MERGE: merge, HIDDEN: hidden, FEED: feed,
+        FEED_OUT: feed_out, BACK_UP: back_up, BACK_ONE: back_first, BACK_GATE: back_gate, BACK_QUERIES: back_queries,
+        BACK_KEYS: back_keys, SWAP_VALUES: swap_values, VALUES_TO_TOKENS: values_to_tokens, GRADS_VALUES: grads_values,
+        BACK_SHARED: back_shared, BACK_PRE: back_pre, GRADS_MIXER: grads_mixer, ADJOINT_FIRST: average_back,
+        ADJOINT_PLANE: average_back_plane, ADJOINT: average_back_second,
+        DIAGONALS: lambda: diagonals(G, T, S.GS, S.prof), TABLE_ROWS: lambda: table_rows(G, me, S.prof, I.index, S.AV),
+        SUMS_CORE: sums_core, SUMS_PLANE: sums_plane, SUMS_LINE: sums_line, SUMS_BACK: sums_back, SUMS_ALL: sums_all,
+        ADD_VALUES: add_values, STATS: stats,
+        GRADS_DOWN: lambda: grads(4, S.GD, S.EX, ("gd", "ex")), GRADS_UP: lambda: grads(3, S.GU, S.LL, ("gu", "ll")),
+        GRADS_HIDDEN: lambda: grads(2, S.GH, S.GT, ("gh", "gt")),
+    }
+    part = {
+        CHAIN: lambda i, j: ga[i].chain(j), FIRST: lambda i, j: ga[i].first(j), SECOND: lambda i, j: ga[i].second(j),
+        THIRD: lambda i, j: ga[i].third(j), BEHIND: lambda i, j: red[i].behind(j), THEIRS: lambda i, j: red[i].theirs(j),
+        PASSED: lambda i, j: red[i].passed(j), MINE: lambda i, j: red[i].mine(j), BUNDLE_IN: lambda i, j: ga[i].bundle_in(j),
+        FLOW: lambda i, j: red[i].flow(j),
+    }
+    single = {
+        ATTEND: attend, ATTEND_BACK: attend_back, ALONG: lambda i: ga[i].z(), BUNDLE_OUT: lambda i: ga[i].bundle_out(),
+        READY: lambda i: ga[i].done(), CLOSE: close, VALUES_BACK: back_values,
+    }
+    for step in ORDER:
+        kind, rest = step - step % 100, step % 100
+        if kind == 0:
+            one[step]()
+        elif kind in single:
+            single[kind](rest)
+        else:
+            part[kind](rest // 10, rest % 10)
+    for gather in ga:
+        gather.drain()
+    link.drain()
+
+
+def adafactor_stats(G, I, O, S, allsum):
+    rate = 1.0 - STEP ** (-0.8)
+    mats = [
+        (S.FM, I.rm[0:1], I.cm[...].T, MX, D, O.rm, O.cm, 0),
+        (S.F0, I.rw[0:1], I.cw[0:1].T, VD, D, O.rw, O.cw, 0),
+        (S.F1, I.rw[1:2], I.cw[1:2].T, VD, D, O.rw, O.cw, 1),
+        (S.FN0, I.rn[0:1], I.cn[0:1].T, D, VD, O.rn, O.cn, 0),
+        (S.FN1, I.rn[1:2], I.cn[1:2].T, D, VD, O.rn, O.cn, 1),
+    ]
+    masters = (I.mix, I.wid.at[0], I.wid.at[1], I.nar.at[0], I.nar.at[1])
+    lanes = lax.broadcasted_iota(jnp.int32, (1, D), 1)
+    rows, cs, extra = [], [], jnp.zeros((1, D), F32)
+    for i, (F, _, _, total, width, _, _, _) in enumerate(mats):
+        sq = F[0 : total // (4 * G)]
+        sq = sq * sq
+        s = jnp.sum(sq, axis=0, keepdims=True)
+        for j in range(width // D):
+            rows.append(s[:, j * D : (j + 1) * D])
+        cs.append(jnp.sum(sq, axis=1, keepdims=True))
+        wv = masters[i][...]
+        extra = jnp.where(lanes == i, jnp.sum(wv * wv), extra)
+    rows.append(extra)
+    small = jnp.sum(O.sums[...] * O.sums[...])
+    for v in raw_averager([I.avg[i] for i in range(4)], O.ma):
+        small = small + jnp.sum(v * v)
+    tot = allsum(jnp.concatenate(rows, axis=0), S.rp, S.rl)
+    length = jnp.sqrt(jnp.sum(tot[0:7]) + small)
+    factor = jnp.minimum(1.0, CLIP_NORM / length)
+    at = 0
+    squares = jnp.zeros((1, 128), F32)
+    means = jnp.zeros((1, 128), F32)
+    lane = lanes[:, :128]
+    for i, (F, ro, co, total, width, rows_o, cols_o, k) in enumerate(mats):
+        row = jnp.concatenate([tot[at + j : at + j + 1] for j in range(width // D)], axis=1)
+        at += width // D
+        rnew = rate * ro + (1.0 - rate) * (factor * factor * row / total + EPS_ONE)
+        cnew = rate * co + (1.0 - rate) * (factor * factor * cs[i] / width + EPS_ONE)
+        mean = jnp.sum(rnew) / width
+        u = factor * F[0 : total // (4 * G)] * lax.rsqrt(rnew * cnew / mean)
+        squares = jnp.where(lane == i, jnp.sum(u * u), squares)
+        means = jnp.where(lane == i, mean, means)
+        rows_o[k : k + 1] = rnew
+        cols_o[k : k + 1] = cnew.T
+    sums = allsum(jnp.broadcast_to(squares, (8, 128)), S.up, S.ul)
+    O.scal[0:1] = sums[0:1]
+    O.scal[1:2] = tot[7:8, :128]
+    O.scal[2:3] = means
+    O.scal[3:4] = jnp.full((1, 128), length, F32)
+    O.scal[4:5] = jnp.full((1, 128), factor, F32)
+    O.scal[5:8] = jnp.zeros((3, 128), F32)
+
+
+def main_call(G, count, x, cot, mix, wid, nar, avg, vv, index, rows, cols):
+    T = x.shape[0]
+    r0, r1, r2 = (t // (4 * G) for t in (MX, VD, D))
+    rm, rw, rn = (r + -r % 16 for r in (r0, r1, r2))
+    A = jax.ShapeDtypeStruct
+    V = pltpu.VMEM
+    half, hv = D // 2, VD // 2
+    vm = pl.BlockSpec(memory_space=pltpu.VMEM)
+    hbm = pl.BlockSpec(memory_space=pl.ANY)
+    S = pltpu.SemaphoreType.DMA
+    ins = dict(
+        x=x, cot=cot, mix=mix, wid=wid, nar=nar, avg=avg, vec=vv, index=index,
+        rm=rows[0], rw=rows[1], rn=rows[2], cm=cols[0], cw=cols[1], cn=cols[2],
+    )
+    outs = dict(
+        block=A((T, D), F32), tok=A((T, D), F32), gm=A((rm, D), F32), gw=A((2, rw, D), F32), gn=A((2, rn, VD), F32),
+        sums=A((16, D), F32), ma=A((3, NH, D), F32), rm=A((1, D), F32), rw=A((2, D), F32), rn=A((2, VD), F32),
+        cm=A((1, r0), F32), cw=A((2, r1), F32), cn=A((2, r2), F32), scal=A((8, 128), F32),
+    )
+    out_specs = [hbm if name in ("gm", "gw", "gn") else vm for name in outs]
+    wide, narrow, mixer = (rw, half), (rn, hv), (rm, half)
+    five = (wide, mixer, narrow, wide, narrow)
+    scratch = dict(
+        w0=V((G, 2, 2, rw, D), BF), mx=V((G, 2, 2, rm, D), BF), n0=V((G, 2, 2, rn, VD), BF),
+        w1=V((G, 2, 2, rw, D), BF), n1=V((G, 2, 2, rn, FF), BF), mc=V((MX // 5, D), BF),
+        fin=V((4, NH, D), F32), ftot=V((G, NH, D), F32), fin2=V((4, NH, D), F32), ftot2=V((G, NH, D), F32),
+        ob=V((4, T, VD), BF), oin=V((4, T, VD), BF), lout=V((4, 8, 128), F32), lin=V((4, 8, 128), F32),
+        xb=V((G, T, D), BF), qb=V((4, T, ZD), BF), kb=V((G, T, ZD), BF), brow=V((4 * G + 8, 128), F32),
+        mixed=V((T, MX), F32), pre=V((T, D), F32), keep=V((T // 8, NH, D), F32), att=V((T, VD), F32),
+        s=V((4, T, G * T), F32), v=V((G * T, VD), BF), GV=V((2, G * T, VD), BF), XB=V((G, T, half), BF),
+        GD=V((2, T, D), BF), EX=V((2, T, hv), BF), GU=V((2, T, FF), BF), LL=V((2, T, half), BF),
+        GH=V((2, T, D), BF), GT=V((2, T, hv), BF), GM=V((2, T, MX), BF), PB=V((2, T, half), BF),
+        GA=V((4, T, VD), BF), ST=V((4, 2, 8, 128), F32), P16=V((4, T, G * T), BF), GS=V((4, T, G * T), BF),
+        QP=V((4, T, ZD), F32), KS=V((4, T, ZD), F32), KP=V((G, T, ZD), F32), DP=V((G, T, ZD), F32),
+        DX=V((G, T, D), BF), BP=V((G, T, D), BF), bp=V((T, D), F32),
+        AV=V((64, D), F32), AS=V((64, D), F32), AW=V((64, D), F32), AT=V((64, D), F32),
+        AP=V((4, 8, D), F32), AL=V((G, 8, D), F32), prof=V((4 * G + 8, 128), F32),
+        rp=V((4, 8, D), F32), rl=V((G, 8, D), F32), up=V((4, 8, 128), F32), ul=V((G, 8, 128), F32),
+    )
+    for i, (r, w) in enumerate(five):
+        name = ("0", "M", "N0", "1", "N1")[i]
+        plane = FLOW + 10 * i in ORDER
+        scratch["R" + name] = V((3, 1 if plane else G, r, w), BF)
+        scratch["L" + name] = V((G + 1, 2, 2, r, w) if plane else (G, r, w), BF)
+    for name, (r, w) in zip(("F0", "FM", "FN0", "F1", "FN1"), five):
+        scratch[name] = V((r, 2 * w), F32)
+    for name, (r, w) in zip(("PA", "P0", "PM", "PN0", "P1", "PN1"), ((8, D),) + five):
+        scratch[name] = V((count, r, w) if count > 1 else (8, 128), F32)
+    slots = 80 + 50 * G + 6 * count
+    scratch.update(
+        agss=S((5, gather_slots(G))), agrs=S((5, gather_slots(G))), ssem=S((slots,)), rsem=S((slots,)), outs=S((5,))
+    )
+    result = pl.pallas_call(
+        functools.partial(main_kernel, G, count, tuple(ins), tuple(outs), tuple(scratch)),
+        out_shape=tuple(outs.values()),
+        in_specs=[vm] * len(ins),
+        out_specs=out_specs,
+        scratch_shapes=list(scratch.values()),
+        compiler_params=pltpu.CompilerParams(collective_id=1, has_side_effects=True, vmem_limit_bytes=59 * 2**20),
+    )(*ins.values())
+    return dict(zip(outs, result))
+
+
+def matrices(G, gm_ref, gw_ref, gn_ref, wm_ref, ww_ref, wn_ref):
+    r0, r1, r2 = (t // (4 * G) for t in (MX, VD, D))
+    return [
+        (lambda: gm_ref[0:r0], lambda: wm_ref[0:r0], MX, D),
+        (lambda: gw_ref[0, 0:r1], lambda: ww_ref[0, 0:r1], VD, D),
+        (lambda: gw_ref[1, 0:r1], lambda: ww_ref[1, 0:r1], VD, D),
+        (lambda: gn_ref[0, 0:r2], lambda: wn_ref[0, 0:r2], D, VD),
+        (lambda: gn_ref[1, 0:r2], lambda: wn_ref[1, 0:r2], D, VD),
+    ]
+
+
+def raw_averager(avg, ma_ref):
+    damp = sigmoid(avg[0])
+    mix = sigmoid(avg[1])
+    d_dec, d_inf, d_out = ma_ref[0], ma_ref[1], ma_ref[2]
+    return [
+        (-mix * d_dec + avg[2] * d_inf) * damp * (1.0 - damp),
+        -damp * d_dec * mix * (1.0 - mix),
+        damp * d_inf,
+        d_out * NH ** (-0.5),
+    ]
+
+
+def step_kernel(
+    G,
+    gm_ref, gw_ref, gn_ref, sum_ref, ma_ref, wm_ref, ww_ref, wn_ref, rm_ref, rw_ref, rn_ref, cm_ref, cw_ref, cn_ref, scal_ref,
+    vec_ref, vmom_ref, avg_ref, amom_ref, block_ref, tok_ref,
+    gm_o, gw_o, gn_o, vg_o, ag_o, nm_o, nw_o, nn_o, nv_o, na_o, rm_o, cm_o, rw_o, cw_o, rn_o, cn_o, vmom_o, amom_o, clip_o,
+    block_o, tok_o,
+    s96,
+):
+    block_o[...] = block_ref[...]
+    tok_o[...] = tok_ref[...]
+    rate = 1.0 - STEP ** (-0.8)
+    lane = lax.broadcasted_iota(jnp.int32, (1, 128), 1)
+
+    def scalar(row, i):
+        return jnp.sum(jnp.where(lane == i, scal_ref[row : row + 1], 0.0))
+
+    factor = scalar(4, 0)
+    clip_o[...] = scal_ref[3:4, 0:1]
+    rm_o[...] = rm_ref[...]
+    rw_o[...] = rw_ref[...]
+    rn_o[...] = rn_ref[...]
+    cm_o[...] = cm_ref[...]
+    cw_o[...] = cw_ref[...]
+    cn_o[...] = cn_ref[...]
+    mats = matrices(G, gm_ref, gw_ref, gn_ref, wm_ref, ww_ref, wn_ref)
+    stats = [
+        (rm_ref[0:1], cm_ref[...].T, gm_o, nm_o, None), (rw_ref[0:1], cw_ref[0:1].T, gw_o, nw_o, 0),
+        (rw_ref[1:2], cw_ref[1:2].T, gw_o, nw_o, 1), (rn_ref[0:1], cn_ref[0:1].T, gn_o, nn_o, 0),
+        (rn_ref[1:2], cn_ref[1:2].T, gn_o, nn_o, 1),
+    ]
+    for i, (g, w, total, width) in enumerate(mats):
+        rnew, cnew, go, no, k = stats[i]
+        entries = total * width
+        rms_u = jnp.sqrt(scalar(0, i) / entries)
+        rms_w = jnp.sqrt(scalar(1, i) / entries)
+        scale = RATE * jnp.maximum(EPS_TWO, rms_w) / jnp.maximum(1.0, rms_u / CLIP_UPDATE)
+        gv = factor * g()
+        new = w() - scale * (gv * lax.rsqrt(rnew * cnew / scalar(2, i)))
+        if k is None:
+            go[...] = gv
+            no[...] = new
+        else:
+            go[k] = gv
+            no[k] = new
+    for r in range(16):
+        for j in range(D // 128):
+            s96[r * (D // 128) + j : r * (D // 128) + j + 1] = sum_ref[r : r + 1, j * 128 : (j + 1) * 128]
+    gv = factor * s96[...]
+    vg_o[...] = gv
+    mom = rate * vmom_ref[...] + (1.0 - rate) * (gv * gv + EPS_ONE)
+    vmom_o[...] = mom
+    u = gv * lax.rsqrt(mom)
+    rms_u = jnp.sqrt(jnp.sum(u * u) / NVEC)
+    wv = vec_ref[...]
+    rms_w = jnp.sqrt(jnp.sum(wv * wv) / NVEC)
+    nv_o[...] = wv - RATE * jnp.maximum(EPS_TWO, rms_w) * (u / jnp.maximum(1.0, rms_u / CLIP_UPDATE))
+    avg = [avg_ref[i] for i in range(4)]
+    raw = raw_averager(avg, ma_ref)
+    us, su, sw = [], 0.0, 0.0
+    for i in range(4):
+        gv = factor * raw[i]
+        ag_o[i] = gv
+        mom = rate * amom_ref[i] + (1.0 - rate) * (gv * gv + EPS_ONE)
+        amom_o[i] = mom
+        u = gv * lax.rsqrt(mom)
+        us.append(u)
+        su = su + jnp.sum(u * u)
+        sw = sw + jnp.sum(avg[i] * avg[i])
+    count = 4 * D * NH
+    scale = RATE * jnp.maximum(EPS_TWO, jnp.sqrt(sw / count)) / jnp.maximum(1.0, jnp.sqrt(su / count) / CLIP_UPDATE)
+    for i in range(4):
+        na_o[i] = avg[i] - scale * us[i]
+
+
+def step_call(G, grads, masters, stats, vectors, vmom, avg, amom, block, tok):
+    A = jax.ShapeDtypeStruct
+    V = pltpu.VMEM
+    vm = pl.BlockSpec(memory_space=pltpu.VMEM)
+    r0, r1, r2 = (t // (4 * G) for t in (MX, VD, D))
+    avgs, vecs = A((4, NH, D), F32), A((NVEC // 128, 128), F32)
+    out_shape = (
+        A((r0, D), F32), A((2, r1, D), F32), A((2, r2, VD), F32), vecs, avgs,
+        A((r0, D), F32), A((2, r1, D), F32), A((2, r2, VD), F32), vecs, avgs,
+        A((1, D), F32), A((1, r0), F32), A((2, D), F32), A((2, r1), F32), A((2, VD), F32), A((2, r2), F32),
+        vecs, avgs, A((1, 1), F32), A(block.shape, F32), A(tok.shape, F32),
+    )
+    return pl.pallas_call(
+        functools.partial(step_kernel, G),
+        out_shape=out_shape,
+        in_specs=[vm] * 21,
+        out_specs=[vm] * 21,
+        scratch_shapes=[V((NVEC // 128, 128), F32)],
+        compiler_params=pltpu.CompilerParams(vmem_limit_bytes=56 * 2**20),
+    )(*grads, *masters, *stats, vectors, vmom, avg, amom, block, tok)
+
+
+def prologue(mixer_weight, widen_weight, narrow_weight, vectors, averager, bias_index):
+    n = lax.axis_size("blk")
+    mix = mixer_weight.T
+    wid = jnp.swapaxes(widen_weight, 1, 2)
+    nar = jnp.swapaxes(narrow_weight, 1, 2)
+    avg = jnp.swapaxes(averager, 1, 2)
+    index = jnp.pad(bias_index, (0, 1)).reshape(2 * n, 128)
+    return mix, wid, nar, avg, vectors.reshape(NVEC // 128, 128), index
 
 
 def carried_in(part, axis, combine, identity, reverse):
@@ -51,11 +1346,6 @@
     return jnp.einsum(pattern, left_side, right_side, preferred_element_type=jnp.float32)
 
 
-def silu_grad(values):
-    logistic = jax.nn.sigmoid(values)
-    return logistic * (1.0 + values * (1.0 - logistic))
-
-
 def layer_norm(values, norm_gain, norm_shift):
     centered = values - jnp.mean(values, axis=-1, keepdims=True)
     inverse = lax.rsqrt(jnp.mean(centered * centered, axis=-1, keepdims=True) + EPS_NORM)
@@ -63,7 +1353,7 @@
     return (normed * norm_gain + norm_shift, normed, inverse)
 
 
-def norm_back(incoming, normed, inverse, norm_gain):
+def norm_back_sums(incoming, normed, inverse, norm_gain):
     scaled = incoming * norm_gain
     result = inverse * (
         scaled
@@ -117,7 +1407,7 @@
     return (weight - RATE * jnp.maximum(EPS_TWO, rms_weight) * update, moment_new)
 
 
-def on_device(
+def with_collectives(
     tokens,
     cotangent,
     mixer_weight,
@@ -229,7 +1519,7 @@
         jnp.dot(expand_low, narrow_low[1], preferred_element_type=jnp.float32) + bias_project
     )
     block_out, normed_two, inverse_two = layer_norm(layer_one + project_two, gain_two, shift_two)
-    grad_second, gain_two_grad, shift_two_grad = norm_back(
+    grad_second, gain_two_grad, shift_two_grad = norm_back_sums(
         cotangent[0], normed_two, inverse_two, gain_two
     )
     project_low = grad_second.astype(jnp.bfloat16)
@@ -239,7 +1529,7 @@
     ).astype(jnp.bfloat16)
     grad_up = product(layer_low, expand_grad_low, "td,tf->df")
     grad_layer = grad_second + product(expand_grad_low, widen_low[1], "tf,df->td")
-    grad_first, gain_one_grad, shift_one_grad = norm_back(
+    grad_first, gain_one_grad, shift_one_grad = norm_back_sums(
         grad_layer, normed_one, inverse_one, gain_one
     )
     grad_update = grad_first * (hidden_act - inputs)
@@ -433,48 +1723,45 @@
     )
 
 
+def on_device(
+    tokens, cotangent, mixer_weight, widen_weight, narrow_weight, vectors, averager, bias_index,
+    mixer_rows, mixer_cols, widen_rows, widen_cols, narrow_rows, narrow_cols, vector_moment, averager_moment,
+):
+    G = lax.axis_size("blk") // 4
+    count = lax.axis_size("dp") // 2
+    mix, wid, nar, avg, vv, index = prologue(
+        mixer_weight, widen_weight, narrow_weight, vectors, averager, bias_index
+    )
+    r = main_call(
+        G, count, tokens[0], cotangent[0], mix, wid, nar, avg, vv, index, (mixer_rows[None], widen_rows, narrow_rows),
+        (mixer_cols[None], widen_cols, narrow_cols),
+    )
+    out = step_call(
+        G, (r["gm"], r["gw"], r["gn"], r["sums"], r["ma"]), (mix, wid, nar),
+        (r["rm"], r["rw"], r["rn"], r["cm"], r["cw"], r["cn"], r["scal"]), vectors.reshape(NVEC // 128, 128),
+        vector_moment.reshape(NVEC // 128, 128), avg, jnp.swapaxes(averager_moment, 1, 2), r["block"], r["tok"],
+    )
+    gm, gw, gn, vg, ag, nm, nw, nn, nv, na, rm, cm, rw, cw, rn, cn, vmom, amom, clip, block, tok = out
+    ag, na, amom, gw, gn, nw, nn = (jnp.swapaxes(v, 1, 2) for v in (ag, na, amom, gw, gn, nw, nn))
+    gm, nm = gm.T, nm.T
+    return (
+        block[None], tok[None], gm, gw, gn, vg.reshape(NVEC), ag, nm, nw, nn, nv.reshape(NVEC), na,
+        rm[0], cm[0], rw, cw, rn, cn, vmom.reshape(NVEC), amom, clip[0, 0],
+    )
+
+
 def solution(mesh):
     in_specs = (
-        P("dp", "blk", None),
-        P("dp", "blk", None),
-        P(None, "blk"),
-        P(None, None, "blk"),
-        P(None, None, "blk"),
-        P(),
-        P(),
-        P(),
-        P(),
-        P("blk"),
-        P(),
-        P(None, "blk"),
-        P(),
-        P(None, "blk"),
-        P(),
-        P(),
+        P("dp", "blk", None), P("dp", "blk", None), P(None, "blk"), P(None, None, "blk"), P(None, None, "blk"),
+        P(), P(), P(), P(), P("blk"), P(), P(None, "blk"), P(), P(None, "blk"), P(), P(),
     )
     out_specs = (
-        P("dp", "blk", None),
-        P("dp", "blk", None),
-        P(None, "blk"),
-        P(None, None, "blk"),
-        P(None, None, "blk"),
-        P(),
-        P(),
-        P(None, "blk"),
-        P(None, None, "blk"),
-        P(None, None, "blk"),
-        P(),
-        P(),
-        P(),
-        P("blk"),
-        P(),
-        P(None, "blk"),
-        P(),
-        P(None, "blk"),
-        P(),
-        P(),
-        P(),
-    )
+        P("dp", "blk", None), P("dp", "blk", None), P(None, "blk"), P(None, None, "blk"), P(None, None, "blk"),
+        P(), P(), P(None, "blk"), P(None, None, "blk"), P(None, None, "blk"), P(), P(), P(), P("blk"), P(),
+        P(None, "blk"), P(), P(None, "blk"), P(), P(), P(),
+    )
+    small = mesh.shape["dp"] % 2 == 0 and mesh.shape["blk"] in (8, 16)
+    body = on_device if small else with_collectives
     return jax.shard_map(
-        on_device, mesh=mesh, in_specs=in_specs, out_specs=out_specs, check_vma=False
-    )
+        body, mesh=mesh, in_specs=in_specs, out_specs=out_specs, check_vma=False
+    )

time: 1540 us -> 227 us (0.15)
  waiting for transfers between devices: 910 us -> 0 us
  blocking collectives: 379 us -> 0 us
  Pallas kernels: 0 us -> 223 us
  other arithmetic: 106 us -> 0.6 us
  matrix products: 57.7 us -> 0 us
  local copies, waits for them, and re-layouts: 54.2 us -> 2.56 us
  between operations: 25.6 us -> 0.69 us
    reduce_scatter x4 -> x0, waiting for transfers between devices: 431 us -> none  [the longest x1 143 us: on_device(): lax.psum_scatter(full_grads[1].astype(jnp.bfloat16), 'blk', scatter_dimen...]
    pallas_call x0 -> x2, Pallas kernels: none -> 223 us  [the longest x1 217 us: main_call(): pl.pallas_call(functools.partial(main_kernel, G, count, tuple(ins), tuple...]
    psum x4 -> x0, blocking collectives: 190 us -> none  [the longest x1 71.8 us: on_device(): lax.psum(tuple((jnp.sum(square_part, axis=2) for square_part in squares))...]
    all_gather x4 -> x0, blocking collectives: 189 us -> none  [the longest x3 144 us: carried_in(): gathered = jax.tree.map(lambda a: lax.all_gather(a, axis), part)]
    unnamed x12 -> x0, waiting for transfers between devices: 185 us -> none
    all_gather x4 -> x0, waiting for transfers between devices: 183 us -> none  [the longest x1 81 us: on_device(): lax.all_gather(shards[1], 'blk', axis=2, tiled=True)]
    psum x2 -> x0, waiting for transfers between devices: 110 us -> none  [the longest x1 110 us: on_device(): lax.psum((vector_local, average_grad), ('dp', 'blk'))]
    dot_general x23 -> x0, matrix products: 57.7 us -> none  [the longest x15 35.5 us: product(): jnp.einsum(pattern, left_side, right_side, preferred_element_type=jnp.flo...]
  transfers between devices with their start and end apart: 11 -> 0, of which waited for: 9 -> 0; matrix products, arithmetic and copies ran while one was open for 10% -> 0% of each run, Pallas kernels for 0% -> 0%
where the time goes in v2:
time: 227 us
  Pallas kernels  223 us (98%)
  local copies, waits for them, and re-layouts  2.56 us (1%)
    pallas_call x1, Pallas kernels, main_call(): pl.pallas_call(functools.partial(main_kernel, G, count, tuple(ins), tuple...  217 us
    pallas_call x1, Pallas kernels, step_call(): pl.pallas_call(functools.partial(step_kernel, G), out_shape=out_shape, in...  5.76 us

profile of v2, /device:TPU:0, one launch (start us, length us, event | category | flops | bytes accessed | tf_op | source)
XLA Modules:
  0.0 226.8 jit_solution(6065053801720364402)
XLA Ops:
  0.7 0.0 copy-start
  0.7 1.3 broadcast_in_dim.12.refs_8_
  1.9 0.0 copy-done
  1.9 0.6 pad_bitcast_fusion.refs_7_
  2.6 217.1 %shard_map.319 = (f32[128,768]{1,0:T(8,128)}, f32[128,768]{1,0:T(8,128)}, f32[208,768]{1,0:T(8,128)}, f32[2,96,768]{2,1,0:T(8,128)}, f32[2,48,1536]{2,1,0:T(8,12...) custom-call(f32[128,768]{1,0:T(8,128)} %bitcast.36, ...), custom_call_target="tpu_custom_call" | custom-call | tf_op jit(solution)/shard_map/pallas_call | solution.py:1179
  219.7 5.8 %shard_map.320 = (f32[200,768]{1,0:T(8,128)}, f32[2,96,768]{2,1,0:T(8,128)}, f32[2,48,1536]{2,1,0:T(8,128)}, f32[96,128]{1,0:T(8,128)}, f32[4,16,768]{2,1,0:T(8,...) custom-call(f32[208,768]{1,0:T(8,128)} %get-tuple-element.56.gm_ref,, ...), custom_call_target="tpu_custom_call" | custom-call | tf_op jit(solution)/shard_map/pallas_call | solution.py:1299
  225.5 0.0 copy-start.1
  225.5 0.7 copy-done.1
  226.2 0.6 reduce
Async XLA Ops:
  0.7 1.3 copy-start
  225.5 0.7 copy-start.1

commit v3 on v2

--- a/solution.py
+++ b/solution.py
@@ -592,29 +592,29 @@
     CLOSE, ATTEND, ATTEND_BACK, VALUES_BACK,
 ) = range(100, 1800, 100)
 ORDER = (
-    ALONG + 0, FIRST + 40, FIRST + 10, ALONG + 1, CHAIN + 2, FIRST + 2, ALONG + 2, CHAIN + 1, SECOND + 40, CHAIN + 11,
-    FIRST + 30, CHAIN + 22, FIRST + 1, FIRST + 11, FIRST + 0, ALONG + 3, SECOND + 2, BIAS_ROWS, CHAIN + 12,
-    CHAIN + 31, FIRST + 12, THIRD + 40, AVERAGE_PLANE, FIRST + 31, FIRST + 20, SECOND + 10, CHAIN + 3, SECOND + 30,
-    CHAIN + 13, CHAIN + 21, CHAIN + 23, FIRST + 13, FIRST + 3, AVERAGE, CHAIN + 33, SECOND + 31, SECOND + 0,
-    CHAIN + 32, SECOND + 12, SEND_X, SECOND + 3, FIRST + 22, THIRD + 31, THIRD + 10, SECOND + 13, THIRD + 0,
-    FIRST + 21, SECOND + 11, THIRD + 12, SECOND + 21, THIRD + 3, SECOND + 20, THIRD + 13, THIRD + 11, SECOND + 1,
-    SECOND + 22, THIRD + 2, READY + 1, THIRD + 20, BUNDLE_OUT + 4, FIRST + 32, FIRST + 33, THIRD + 1, MIXING,
-    READY + 0, FIRST + 23, VALUES_0, SECOND + 32, VALUES_1, SECOND + 23, SECOND + 33, ATTEND + 2, ATTEND + 1,
-    BUNDLE_IN + 41, THIRD + 30, ATTEND + 0, BUNDLE_IN + 42, THIRD + 22, THIRD + 21, THIRD + 32, ATTEND + 3,
-    THIRD + 23, READY + 2, THIRD + 33, BUNDLE_IN + 43, READY + 3, READY + 4, MERGE, HIDDEN, FEED, FEED_OUT, BACK_UP,
-    BACK_ONE, BACK_GATE, GRADS_DOWN, FLOW + 43, GRADS_HIDDEN, BEHIND + 22, GRADS_UP, PASSED + 22, FLOW + 42,
-    ATTEND_BACK + 2, THEIRS + 20, BEHIND + 30, ATTEND_BACK + 3, BEHIND + 31, THEIRS + 22, FLOW + 41, THEIRS + 31,
-    ATTEND_BACK + 1, BEHIND + 23, BEHIND + 21, ATTEND_BACK + 0, BACK_KEYS, THEIRS + 23, VALUES_BACK + 0,
-    VALUES_BACK + 2, VALUES_BACK + 1, SWAP_VALUES, BEHIND + 33, PASSED + 30, BEHIND + 32, BACK_QUERIES,
-    VALUES_TO_TOKENS, PASSED + 23, THEIRS + 32, THEIRS + 30, PASSED + 21, GRADS_VALUES, PASSED + 33, BEHIND + 0,
-    THEIRS + 33, THEIRS + 1, BACK_SHARED, BEHIND + 1, BACK_PRE, ADJOINT_FIRST, PASSED + 0, DIAGONALS, PASSED + 31,
-    PASSED + 1, THEIRS + 21, THEIRS + 3, BEHIND + 2, PASSED + 32, GRADS_MIXER, BEHIND + 12, ADJOINT_PLANE,
-    THEIRS + 11, MINE + 1, MINE + 22, MINE + 31, MINE + 30, BEHIND + 3, MINE + 33, BEHIND + 13, THEIRS + 13,
-    PASSED + 12, MINE + 23, TABLE_ROWS, FLOW + 40, THEIRS + 12, BEHIND + 40, THEIRS + 0, MINE + 32, ADJOINT,
-    PASSED + 3, BEHIND + 20, ADD_VALUES, SUMS_CORE, PASSED + 13, THEIRS + 40, MINE + 3, SUMS_PLANE, PASSED + 20,
-    BEHIND + 11, MINE + 12, PASSED + 40, SUMS_LINE, MINE + 13, THEIRS + 2, BEHIND + 10, MINE + 21, MINE + 40,
-    PASSED + 11, MINE + 11, SUMS_BACK, PASSED + 2, CLOSE + 3, CLOSE + 4, MINE + 0, MINE + 20, THEIRS + 10,
-    PASSED + 10, SUMS_ALL, CLOSE + 2, MINE + 10, MINE + 2, CLOSE + 1, CLOSE + 0, STATS,
+    ALONG + 3, ALONG + 2, ALONG + 0, FIRST + 0, FIRST + 30, FIRST + 10, CHAIN + 31, CHAIN + 32, ALONG + 1,
+    AVERAGE_PLANE, CHAIN + 1, FIRST + 31, FIRST + 40, SECOND + 0, SECOND + 10, FIRST + 1, CHAIN + 11, SECOND + 40,
+    FIRST + 11, CHAIN + 12, FIRST + 20, SECOND + 31, SECOND + 1, FIRST + 12, CHAIN + 3, FIRST + 32, CHAIN + 21,
+    CHAIN + 33, FIRST + 3, CHAIN + 2, FIRST + 2, FIRST + 33, BIAS_ROWS, CHAIN + 13, SECOND + 11, AVERAGE, CHAIN + 23,
+    SEND_X, FIRST + 13, SECOND + 2, SECOND + 12, THIRD + 40, THIRD + 1, SECOND + 3, THIRD + 10, FIRST + 23,
+    SECOND + 30, SECOND + 33, SECOND + 13, THIRD + 11, SECOND + 32, CHAIN + 22, THIRD + 30, THIRD + 12, THIRD + 2,
+    FIRST + 21, BUNDLE_OUT + 4, SECOND + 20, THIRD + 33, THIRD + 0, THIRD + 31, SECOND + 23, FIRST + 22, THIRD + 13,
+    THIRD + 3, READY + 1, MIXING, READY + 0, VALUES_0, SECOND + 22, VALUES_1, BUNDLE_IN + 41, SECOND + 21, THIRD + 20,
+    ATTEND + 2, ATTEND + 1, THIRD + 32, BUNDLE_IN + 42, THIRD + 21, ATTEND + 3, THIRD + 22, THIRD + 23, READY + 3,
+    ATTEND + 0, BUNDLE_IN + 43, READY + 2, MERGE, HIDDEN, FEED, READY + 4, FEED_OUT, BACK_UP, BACK_ONE, BACK_GATE,
+    GRADS_DOWN, FLOW + 43, GRADS_HIDDEN, GRADS_UP, FLOW + 42, FLOW + 41, ATTEND_BACK + 2, THEIRS + 21, BEHIND + 22,
+    ATTEND_BACK + 0, ATTEND_BACK + 1, THEIRS + 32, BEHIND + 21, ATTEND_BACK + 3, VALUES_BACK + 1, BACK_KEYS,
+    VALUES_BACK + 2, THEIRS + 31, PASSED + 22, VALUES_BACK + 0, SWAP_VALUES, THEIRS + 30, BACK_QUERIES, BEHIND + 23,
+    THEIRS + 22, THEIRS + 23, FLOW + 40, BEHIND + 20, BEHIND + 33, BEHIND + 32, DIAGONALS, VALUES_TO_TOKENS,
+    BEHIND + 30, THEIRS + 40, PASSED + 23, BEHIND + 31, GRADS_VALUES, BEHIND + 2, PASSED + 33, THEIRS + 33,
+    BACK_SHARED, PASSED + 21, PASSED + 32, THEIRS + 3, BACK_PRE, ADJOINT_FIRST, BEHIND + 3, BEHIND + 40, GRADS_MIXER,
+    ADJOINT_PLANE, THEIRS + 2, PASSED + 3, THEIRS + 12, PASSED + 2, PASSED + 31, MINE + 22, MINE + 32, PASSED + 40,
+    PASSED + 20, MINE + 21, PASSED + 30, BEHIND + 1, THEIRS + 11, MINE + 31, MINE + 40, MINE + 23, BEHIND + 12,
+    MINE + 3, PASSED + 1, TABLE_ROWS, THEIRS + 1, MINE + 33, ADJOINT, BEHIND + 13, BEHIND + 11, ADD_VALUES, SUMS_CORE,
+    THEIRS + 20, PASSED + 12, PASSED + 11, SUMS_PLANE, BEHIND + 10, BEHIND + 0, MINE + 12, MINE + 30, PASSED + 13,
+    CLOSE + 4, MINE + 1, SUMS_LINE, THEIRS + 13, MINE + 2, MINE + 11, PASSED + 0, SUMS_BACK, MINE + 13, THEIRS + 10,
+    PASSED + 10, CLOSE + 3, MINE + 20, SUMS_ALL, CLOSE + 2, THEIRS + 0, MINE + 10, MINE + 0, CLOSE + 0, CLOSE + 1,
+    STATS,
 )
 
 
@@ -1075,7 +1075,7 @@
 def adafactor_stats(G, I, O, S, allsum):
     rate = 1.0 - STEP ** (-0.8)
     mats = [
-        (S.FM, I.rm[0:1], I.cm[...].T, MX, D, O.rm, O.cm, 0),
+        (S.FM, vec(I.rm, 0, D), I.cm[...].T, MX, D, O.rm, O.cm, 0),
         (S.F0, I.rw[0:1], I.cw[0:1].T, VD, D, O.rw, O.cw, 0),
         (S.F1, I.rw[1:2], I.cw[1:2].T, VD, D, O.rw, O.cw, 1),
         (S.FN0, I.rn[0:1], I.cn[0:1].T, D, VD, O.rn, O.cn, 0),
@@ -1228,7 +1228,8 @@
 
     factor = scalar(4, 0)
     clip_o[...] = scal_ref[3:4, 0:1]
-    rm_o[...] = rm_ref[...]
+    for r in range(D // 128):
+        rm_o[r : r + 1] = rm_ref[:, r * 128 : (r + 1) * 128]
     rw_o[...] = rw_ref[...]
     rn_o[...] = rn_ref[...]
     cm_o[...] = cm_ref[...]
@@ -1293,7 +1294,7 @@
     out_shape = (
         A((r0, D), F32), A((2, r1, D), F32), A((2, r2, VD), F32), vecs, avgs,
         A((r0, D), F32), A((2, r1, D), F32), A((2, r2, VD), F32), vecs, avgs,
-        A((1, D), F32), A((1, r0), F32), A((2, D), F32), A((2, r1), F32), A((2, VD), F32), A((2, r2), F32),
+        A((D // 128, 128), F32), A((1, r0), F32), A((2, D), F32), A((2, r1), F32), A((2, VD), F32), A((2, r2), F32),
         vecs, avgs, A((1, 1), F32), A(block.shape, F32), A(tok.shape, F32),
     )
     return pl.pallas_call(
@@ -1733,7 +1734,7 @@
         mixer_weight, widen_weight, narrow_weight, vectors, averager, bias_index
     )
     r = main_call(
-        G, count, tokens[0], cotangent[0], mix, wid, nar, avg, vv, index, (mixer_rows[None], widen_rows, narrow_rows),
+        G, count, tokens[0], cotangent[0], mix, wid, nar, avg, vv, index, (mixer_rows.reshape(D // 128, 128), widen_rows, narrow_rows),
         (mixer_cols[None], widen_cols, narrow_cols),
     )
     out = step_call(
@@ -1746,7 +1747,7 @@
     gm, nm = gm.T, nm.T
     return (
         block[None], tok[None], gm, gw, gn, vg.reshape(NVEC), ag, nm, nw, nn, nv.reshape(NVEC), na,
-        rm[0], cm[0], rw, cw, rn, cn, vmom.reshape(NVEC), amom, clip[0, 0],
+        rm.reshape(D), cm[0], rw, cw, rn, cn, vmom.reshape(NVEC), amom, clip.reshape(()),
     )
 
 

time: 227 us -> 214 us (0.943)
  Pallas kernels: 223 us -> 212 us
    pallas_call x1, Pallas kernels: 217 us -> 206 us  [main_call(): pl.pallas_call(functools.partial(main_kernel, G, count, tuple(ins), tuple...]
where the time goes in v3:
time: 214 us
  Pallas kernels  212 us (99%)
    pallas_call x1, Pallas kernels, main_call(): pl.pallas_call(functools.partial(main_kernel, G, count, tuple(ins), tuple...  206 us
    pallas_call x1, Pallas kernels, step_call(): pl.pallas_call(functools.partial(step_kernel, G), out_shape=out_shape, in...  5.76 us

profile of v3, /device:TPU:0, one launch (start us, length us, event | category | flops | bytes accessed | tf_op | source)
XLA Modules:
  0.0 213.7 jit_solution(17466163371599615924)
XLA Ops:
  0.7 0.0 copy-start
  0.7 0.7 copy-done
  1.4 0.6 pad_bitcast_fusion.refs_7_
  2.0 205.8 %shard_map.319 = (f32[128,768]{1,0:T(8,128)}, f32[128,768]{1,0:T(8,128)}, f32[208,768]{1,0:T(8,128)}, f32[2,96,768]{2,1,0:T(8,128)}, f32[2,48,1536]{2,1,0:T(8,12...) custom-call(f32[128,768]{1,0:T(8,128)} %bitcast.38, ...), custom_call_target="tpu_custom_call" | custom-call | tf_op jit(solution)/shard_map/pallas_call | solution.py:1179
  207.8 5.8 %shard_map.320 = (f32[200,768]{1,0:T(8,128)}, f32[2,96,768]{2,1,0:T(8,128)}, f32[2,48,1536]{2,1,0:T(8,128)}, f32[96,128]{1,0:T(8,128)}, f32[4,16,768]{2,1,0:T(8,...) custom-call(f32[208,768]{1,0:T(8,128)} %get-tuple-element.56.gm_ref,, ...), custom_call_target="tpu_custom_call" | custom-call | tf_op jit(solution)/shard_map/pallas_call | solution.py:1300
Async XLA Ops:
  0.7 0.7 copy-start
